TPU v7x, 256 devices: a whole 4x4x8 slice. The times are simulated.
256 devices in a mesh: dp: 16 (over x, y), expert: 16 (over z, core).
Axes of the slice: x: 4, y: 4, z: 8, core: 2. Of those that a mesh axis runs over, the one named last changes fastest.
Arguments:
- tokens: bfloat16 [32768, 1440], P(('dp', 'expert')), parts along dimension 0, may hold values from -6 to 6
- route_ids: int32 [32768, 4], P(('dp', 'expert')), parts along dimension 0, may hold values from 0 to 15, as said below
- route_level: int32 [32768, 4], P(('dp', 'expert')), parts along dimension 0, may hold values from 0 to 15
- gate_up_codes: int32 [16, 1440, 720], P('expert'), may hold values from 0 to 65535
- gate_up_scale: int32 [16, 45, 2880], P('expert'), may hold values from 119 to 122
- gate_up_bias: bfloat16 [16, 2880], P('expert'), may hold values from -3 to 3
- down_codes: int32 [16, 1440, 360], P('expert'), may hold values from 0 to 65535
- down_scale: int32 [16, 45, 1440], P('expert'), may hold values from 117 to 120
- down_bias: bfloat16 [16, 1440], P('expert'), may hold values from -3 to 3
- attn_gain: bfloat16 [1440], replicated, may hold values from 0.5 to 1.5
- query_weight: bfloat16 [1440, 2048], replicated, may hold values from -14 to 14
- key_matrix: bfloat16 [1440, 256], replicated, may hold values from -1 to 1
- value_matrix: bfloat16 [1440, 256], replicated, may hold values from -0.15625 to 0.15625
- sinks: float32 [32], replicated, may hold values from 4 to 12
Outputs:
- block_out: bfloat16 [32768, 1440], P(('dp', 'expert')), parts along dimension 0
- attended: bfloat16 [32768, 2048], P(('dp', 'expert')), parts along dimension 0
There are 16 independent parts, one for each index of `dp`. A program takes and returns all parts, laid end to end along the dimension named above; an argument that names none is the same for every part. Nothing has to cross between parts.
Inputs may be any that keep to these rules, and one draw needn't show every extreme that they name: `route_ids`: each row names 4 different experts. Among the 128 rows of one device no expert is named more than 64 times, and one expert is named exactly 64 times on each.
All inputs are finite; a program needn't handle non-finite values.
Results may differ from a plain program's by a relative error of at most 0.015.
The roundings to bfloat16 on the way count: a program that leaves them out, or rounds other values in their place, can miss the bound.
Values may be sent and summed in bfloat16 or wider, within the bound.
No kernel may reach another device: no remote copies, remote signals or barrier semaphores. Data moves between devices by JAX's collectives and lax.ppermute only.
A program may use at most 128 MiB of HBM per device.

v0:
```python
import functools

import jax
import jax.numpy as jnp
from jax import lax
from jax.experimental import pallas as pl
from jax.experimental.pallas import tpu as pltpu
from jax.sharding import PartitionSpec as P

HEAD_SIZE = 64
WINDOW_LENGTH = 128
MOST = 64
WIDE = 1536
CHUNKS = 3
RETURN_SCALE = 8.0
VMEM_LIMIT = 56 * 1024 * 1024
F32 = jnp.float32
BF16 = jnp.bfloat16


def twice_fp4(words, field_index):
    low = jnp.bitwise_and(jnp.right_shift(words, 4 * field_index), 7).astype(F32)
    return jnp.maximum(jnp.maximum(low, 2.0 * low - 4.0), 4.0 * low - 16.0)


def signed_scale(words, field_index, scale):
    return jnp.where(jnp.bitwise_and(words, 8 << (4 * field_index)) != 0, -scale, scale)


def decode_up_kernel(codes_ref, scale_ref, out_ref):
    for block in range(9):
        words = codes_ref[32 * block : 32 * block + 32, :]
        for place, field_index in enumerate((0, 2, 1, 3)):
            scale = scale_ref[0, 0, 4 * block + place : 4 * block + place + 1, :]
            value = twice_fp4(words, field_index) * signed_scale(words, field_index, scale)
            out_ref[0, 32 * block : 32 * block + 32, 256 * place : 256 * place + 256] = (
                value.astype(BF16)
            )


def decode_up(codes, scale):
    rows, words = codes.shape
    return pl.pallas_call(
        decode_up_kernel,
        grid=(CHUNKS, 5),
        in_specs=[
            pl.BlockSpec((288, 256), lambda b, r: (r, b)),
            pl.BlockSpec((1, 1, 36, 256), lambda b, r: (r, b, 0, 0)),
        ],
        out_specs=pl.BlockSpec((1, 288, 1024), lambda b, r: (b, r, 0)),
        out_shape=jax.ShapeDtypeStruct((CHUNKS, rows, 1024), BF16),
        compiler_params=pltpu.CompilerParams(vmem_limit_bytes=VMEM_LIMIT),
        cost_estimate=pl.CostEstimate(flops=60_000_000, bytes_accessed=14_000_000, transcendentals=0),
        name="decode_up",
    )(codes, scale)


def decode_down_kernel(left_ref, middle_ref, right_ref, scale_ref, out_ref):
    source = lax.broadcasted_iota(jnp.int32, (512, 512), 0)
    target = lax.broadcasted_iota(jnp.int32, (512, 512), 1)
    wanted = 4 * jnp.bitwise_and(source, 127) + jnp.right_shift(source, 7)
    spread = jnp.where(target == wanted, 1.0, 0.0).astype(BF16)
    for parity in range(2):
        for part, codes_ref in enumerate((left_ref, middle_ref, right_ref)):
            piece = codes_ref[pl.ds(parity, 256, 2), :]
            fields = []
            for field_index in range(4):
                size = twice_fp4(piece, field_index)
                value = jnp.where(
                    jnp.bitwise_and(piece, 8 << (4 * field_index)) != 0, -size, size
                )
                fields.append(value.astype(BF16))
            natural = jnp.dot(
                jnp.concatenate(fields, axis=1), spread, preferred_element_type=F32
            )
            for block in range(16):
                scale = scale_ref[block : block + 1, 512 * part : 512 * part + 512]
                row = 256 * parity + 16 * block
                out_ref[0, row : row + 16, 512 * part : 512 * part + 512] = (
                    natural[16 * block : 16 * block + 16] * scale
                ).astype(BF16)


def decode_down(codes, scale):
    return pl.pallas_call(
        decode_down_kernel,
        grid=(CHUNKS,),
        in_specs=[
            pl.BlockSpec((512, 128), lambda b: (b, 0)),
            pl.BlockSpec((512, 128), lambda b: (b, 1)),
            pl.BlockSpec((512, 128), lambda b: (b, 2)),
            pl.BlockSpec((16, WIDE), lambda b: (b, 0)),
        ],
        out_specs=pl.BlockSpec((1, 512, WIDE), lambda b: (b, 0, 0)),
        out_shape=jax.ShapeDtypeStruct((CHUNKS, 512, WIDE), BF16),
        compiler_params=pltpu.CompilerParams(vmem_limit_bytes=VMEM_LIMIT),
        cost_estimate=pl.CostEstimate(flops=60_000_000, bytes_accessed=7_000_000, transcendentals=0),
        name="decode_down",
    )(codes, codes, codes, scale)


def pack_kernel(tokens_ref, ids_ref, level_ref, out_ref):
    out_ref[:, :1440] = tokens_ref[...]
    out_ref[:, 1440:1444] = ids_ref[...].astype(F32).astype(BF16)
    out_ref[:, 1444:1448] = level_ref[...].astype(F32).astype(BF16)
    out_ref[:, 1448:] = jnp.zeros((128, WIDE - 1448), BF16)


def pack(tokens, route_ids, route_level):
    return pl.pallas_call(
        pack_kernel,
        out_shape=jax.ShapeDtypeStruct((128, WIDE), BF16),
        compiler_params=pltpu.CompilerParams(vmem_limit_bytes=VMEM_LIMIT),
        name="pack",
    )(tokens, route_ids, route_level)


def earlier_rows():
    row = lax.broadcasted_iota(jnp.int32, (128, 128), 0)
    column = lax.broadcasted_iota(jnp.int32, (128, 128), 1)
    return jnp.where(column < row, 1.0, 0.0).astype(BF16)


def expert_kernel(shard_count, place_ref, *refs):
    shards = refs[:shard_count]
    (
        first_ref,
        second_ref,
        first_bias_ref,
        second_bias_ref,
        near_ref,
        other_ref,
        rows_ref,
        total_ref,
    ) = refs[shard_count:]
    chunk = pl.program_id(0)
    half = shard_count // 2 * MOST

    @pl.when(chunk == 0)
    def _():
        before = earlier_rows()
        lane = lax.broadcasted_iota(jnp.int32, (128, 128), 1)
        slot = jnp.bitwise_and(lane, MOST - 1).astype(F32)
        lower = lane < MOST
        expert = place_ref[shard_count].astype(F32)
        for j in range(0, shard_count, 2):
            picks = []
            for i in range(2):
                meta = shards[j + i][:, 1408:1536].astype(F32)
                named = jnp.zeros((128, 1), F32)
                for choice in range(4):
                    named = named + jnp.where(
                        meta[:, 32 + choice : 33 + choice] == expert, 1.0, 0.0
                    )
                spread = jnp.broadcast_to(named, (128, 128))
                rank = jnp.dot(before, spread.astype(BF16), preferred_element_type=F32)
                pick = jnp.where((rank == slot) & (spread > 0.0), 1.0, 0.0)
                pick = jnp.where(lower if i == 0 else jnp.logical_not(lower), pick, 0.0)
                picks.append(pick.astype(BF16))
            rows = lax.dot_general(
                jnp.concatenate(picks, axis=0),
                jnp.concatenate([shards[j][...], shards[j + 1][...]], axis=0),
                (((0,), (0,)), ((), ())),
                preferred_element_type=F32,
            )
            rows_ref[MOST * j : MOST * j + 2 * MOST, :] = rows.astype(BF16)

    pre = jnp.dot(rows_ref[:, :1440], first_ref[0], preferred_element_type=F32)
    pre = pre + first_bias_ref[chunk]
    gate = jnp.minimum(pre[:, :512], 7.0)
    up = jnp.clip(pre[:, 512:], -7.0, 7.0)
    activated = ((up + 1.0) * gate * (0.5 + 0.5 * jnp.tanh(0.851 * gate))).astype(BF16)
    product = jnp.dot(activated, second_ref[0], preferred_element_type=F32)

    @pl.when(chunk == 0)
    def _():
        total_ref[...] = product + second_bias_ref[...]

    @pl.when(chunk == 1)
    def _():
        total_ref[...] += product

    @pl.when(chunk == CHUNKS - 1)
    def _():
        done = (total_ref[...] + product).astype(BF16)
        near_ref[...] = done[:half]
        other_ref[...] = done[half:]


def run_experts(shards, expert, gathered, first, second, first_bias, second_bias):
    count = len(shards)
    rows = count * MOST
    place = jnp.stack(shards + [expert]).astype(jnp.int32)

    def shard_spec(j):
        return pl.BlockSpec((128, WIDE), lambda b, place: (place[j], 0))

    half = jax.ShapeDtypeStruct((rows // 2, WIDE), BF16)
    half_spec = pl.BlockSpec((rows // 2, WIDE), lambda b, place: (0, 0))
    return pl.pallas_call(
        functools.partial(expert_kernel, count),
        grid_spec=pltpu.PrefetchScalarGridSpec(
            num_scalar_prefetch=1,
            grid=(CHUNKS,),
            in_specs=[shard_spec(j) for j in range(count)]
            + [
                pl.BlockSpec((1, 1440, 1024), lambda b, place: (b, 0, 0)),
                pl.BlockSpec((1, 512, WIDE), lambda b, place: (b, 0, 0)),
                pl.BlockSpec((CHUNKS, 1, 1024), lambda b, place: (0, 0, 0)),
                pl.BlockSpec((1, WIDE), lambda b, place: (0, 0)),
            ],
            out_specs=[half_spec, half_spec],
            scratch_shapes=[pltpu.VMEM((rows, WIDE), BF16), pltpu.VMEM((rows, WIDE), F32)],
        ),
        out_shape=[half, half],
        compiler_params=pltpu.CompilerParams(vmem_limit_bytes=VMEM_LIMIT),
        cost_estimate=pl.CostEstimate(
            flops=2 * rows * 1440 * 4320, bytes_accessed=15_000_000, transcendentals=0
        ),
        name="experts",
    )(place, *([gathered] * count), first, second, first_bias, second_bias)


def combine_kernel(shard_count, place_ref, *refs):
    metas = refs[:shard_count]
    near_ref, other_ref, out_ref = refs[shard_count:]
    before = earlier_rows()
    lane = lax.broadcasted_iota(jnp.int32, (128, 128), 1)
    slot = jnp.bitwise_and(lane, MOST - 1).astype(F32)
    expert = jnp.where(lane < MOST, place_ref[shard_count], place_ref[shard_count + 1]).astype(F32)
    for j in range(shard_count):
        meta = metas[j][...].astype(F32)
        raised = jnp.exp(meta / 4.0)
        named = jnp.zeros((128, 128), F32)
        chosen = jnp.zeros((128, 128), F32)
        whole = jnp.zeros((128, 1), F32)
        for choice in range(4):
            same = meta[:, 32 + choice : 33 + choice] == expert
            level = raised[:, 36 + choice : 37 + choice]
            named = jnp.where(same, 1.0, named)
            chosen = jnp.where(same, level, chosen)
            whole = whole + level
        rank = jnp.dot(before, named.astype(BF16), preferred_element_type=F32)
        weight = jnp.where((rank == slot) & (named > 0.0), chosen / whole * RETURN_SCALE, 0.0)
        high = weight.astype(BF16)
        low = (weight - high.astype(F32)).astype(BF16)
        near = near_ref[MOST * j : MOST * j + MOST, :]
        other = other_ref[MOST * j : MOST * j + MOST, :]
        out_ref[j] = jnp.dot(
            jnp.concatenate([high, low], axis=1),
            jnp.concatenate([near, other, near, other], axis=0),
            preferred_element_type=F32,
        )


def combine(shards, experts, gathered, near, other):
    count = len(shards)
    place = jnp.stack(shards + experts).astype(jnp.int32)

    def meta_spec(j):
        return pl.BlockSpec((128, 128), lambda i, place: (place[j], 11))

    rows_spec = pl.BlockSpec((count * MOST, WIDE), lambda i, place: (0, 0))
    return pl.pallas_call(
        functools.partial(combine_kernel, count),
        grid_spec=pltpu.PrefetchScalarGridSpec(
            num_scalar_prefetch=1,
            grid=(1,),
            in_specs=[meta_spec(j) for j in range(count)] + [rows_spec, rows_spec],
            out_specs=pl.BlockSpec((count, 128, WIDE), lambda i, place: (0, 0, 0)),
        ),
        out_shape=jax.ShapeDtypeStruct((count, 128, WIDE), F32),
        compiler_params=pltpu.CompilerParams(vmem_limit_bytes=VMEM_LIMIT),
        cost_estimate=pl.CostEstimate(
            flops=2 * count * 128 * 256 * WIDE, bytes_accessed=1_500_000 * count, transcendentals=0
        ),
        name="combine",
    )(place, *([gathered] * count), near, other)


def turned(block, cosine, sine_part):
    width = block.shape[1]
    lane = lax.broadcasted_iota(jnp.int32, block.shape, 1)
    first = jnp.bitwise_and(lane, 63) < 32
    swapped = jnp.where(first, pltpu.roll(block, width - 32, 1), pltpu.roll(block, 32, 1))
    copies = width // 128
    cosine = jnp.concatenate([cosine] * copies, axis=1)
    sine_part = jnp.concatenate([sine_part] * copies, axis=1)
    return block * cosine + swapped * sine_part


def mix_kernel(
    tokens_ref, mixture_ref, gain_ref, key_ref, value_ref, cos_ref, sin_ref, out_ref, normed_ref, kv_ref
):
    block_out = (tokens_ref[...].astype(F32) + mixture_ref[...]).astype(BF16)
    out_ref[...] = block_out
    widened = block_out.astype(F32)
    squares = jnp.sum(widened * widened, axis=1, keepdims=True) / 1440.0
    normed = (widened * lax.rsqrt(squares + 1e-05) * gain_ref[...].astype(F32)).astype(BF16)
    normed_ref[...] = normed
    keys = jnp.dot(normed, key_ref[...], preferred_element_type=F32)
    kv_ref[:, :256] = turned(keys, cos_ref[...], sin_ref[...]).astype(BF16)
    kv_ref[:, 256:] = jnp.dot(normed, value_ref[...], preferred_element_type=F32).astype(BF16)


def mix(tokens, mixture, gain, key_matrix, value_matrix, cosine, sine_part):
    return pl.pallas_call(
        mix_kernel,
        out_shape=[
            jax.ShapeDtypeStruct((128, 1440), BF16),
            jax.ShapeDtypeStruct((128, 1440), BF16),
            jax.ShapeDtypeStruct((128, 512), BF16),
        ],
        compiler_params=pltpu.CompilerParams(vmem_limit_bytes=VMEM_LIMIT),
        cost_estimate=pl.CostEstimate(
            flops=2 * 128 * 1440 * 512, bytes_accessed=3_000_000, transcendentals=0
        ),
        name="mix",
    )(tokens, mixture, gain, key_matrix, value_matrix, cosine, sine_part)


def queries_kernel(normed_ref, weight_ref, cos_ref, sin_ref, out_ref):
    projected = jnp.dot(normed_ref[...], weight_ref[...], preferred_element_type=F32)
    rotated = turned(projected, cos_ref[...], sin_ref[...])
    scaled = (rotated.astype(BF16).astype(F32) * 0.125).astype(BF16)
    for pair in range(4):
        out_ref[0, 128 * pair : 128 * pair + 128, :] = scaled[:, 128 * pair : 128 * pair + 128]


def queries(normed, weight, cosine, sine_part):
    return pl.pallas_call(
        queries_kernel,
        grid=(4,),
        in_specs=[
            pl.BlockSpec((128, 1440), lambda g: (0, 0)),
            pl.BlockSpec((1440, 512), lambda g: (0, g)),
            pl.BlockSpec((128, 128), lambda g: (0, 0)),
            pl.BlockSpec((128, 128), lambda g: (0, 0)),
        ],
        out_specs=pl.BlockSpec((1, 512, 128), lambda g: (g, 0, 0)),
        out_shape=jax.ShapeDtypeStruct((4, 512, 128), BF16),
        compiler_params=pltpu.CompilerParams(vmem_limit_bytes=VMEM_LIMIT),
        cost_estimate=pl.CostEstimate(
            flops=2 * 128 * 1440 * 2048, bytes_accessed=7_000_000, transcendentals=0
        ),
        name="queries",
    )(normed, weight, cosine, sine_part)


def attend_kernel(index_ref, sinks_ref, queries_ref, own_ref, halo_ref, out_ref):
    lane = lax.broadcasted_iota(jnp.int32, (128, 128), 1)
    lower = lane < 64

    def doubled(block, odd):
        block = block.astype(F32)
        if odd:
            high = jnp.where(lower, 0.0, block)
            low = pltpu.roll(high, 64, 1)
        else:
            low = jnp.where(lower, block, 0.0)
            high = pltpu.roll(low, 64, 1)
        return jnp.concatenate([low, high], axis=0).astype(BF16)

    row = lax.broadcasted_iota(jnp.int32, (128, 256), 0)
    column = jnp.bitwise_and(lax.broadcasted_iota(jnp.int32, (128, 256), 1), 127)
    mine = column <= row
    allowed = mine | jnp.broadcast_to(index_ref[0] > 0, mine.shape)
    for group in range(4):
        start = 128 * (group // 2)
        odd = group % 2 == 1
        query = queries_ref[group]
        across = (((1,), (1,)), ((), ()))
        here = lax.dot_general(
            query, doubled(own_ref[:, start : start + 128], odd), across, preferred_element_type=F32
        )
        there = lax.dot_general(
            query, doubled(halo_ref[:, start : start + 128], odd), across, preferred_element_type=F32
        )
        here_probs = []
        there_probs = []
        for pair in range(4):
            rows = slice(128 * pair, 128 * pair + 128)
            scores = jnp.where(mine, here[rows], there[rows])
            scores = jnp.where(allowed, scores, -1e30)
            halves = []
            for side in range(2):
                part = scores[:, 128 * side : 128 * side + 128]
                sink = sinks_ref[8 * group + 2 * pair + side]
                top = jnp.maximum(jnp.max(part, axis=1, keepdims=True), sink)
                weights = jnp.exp(part - top)
                whole = jnp.exp(sink - top) + jnp.sum(weights, axis=1, keepdims=True)
                halves.append(weights * (1.0 / whole))
            probs = jnp.where(allowed, jnp.concatenate(halves, axis=1), 0.0)
            here_probs.append(jnp.where(mine, probs, 0.0).astype(BF16))
            there_probs.append(jnp.where(mine, 0.0, probs).astype(BF16))
        mixed = jnp.dot(
            jnp.concatenate(here_probs, axis=0),
            doubled(own_ref[:, 256 + start : 384 + start], odd),
            preferred_element_type=F32,
        ) + jnp.dot(
            jnp.concatenate(there_probs, axis=0),
            doubled(halo_ref[:, 256 + start : 384 + start], odd),
            preferred_element_type=F32,
        )
        for pair in range(4):
            place = 512 * group + 128 * pair
            out_ref[:, place : place + 128] = mixed[128 * pair : 128 * pair + 128].astype(BF16)


def attend(index, sinks, query, own, halo):
    return pl.pallas_call(
        attend_kernel,
        in_specs=[
            pl.BlockSpec(memory_space=pltpu.SMEM),
            pl.BlockSpec(memory_space=pltpu.SMEM),
            pl.BlockSpec(memory_space=pltpu.VMEM),
            pl.BlockSpec(memory_space=pltpu.VMEM),
            pl.BlockSpec(memory_space=pltpu.VMEM),
        ],
        out_specs=pl.BlockSpec(memory_space=pltpu.VMEM),
        out_shape=jax.ShapeDtypeStruct((128, 2048), BF16),
        compiler_params=pltpu.CompilerParams(vmem_limit_bytes=VMEM_LIMIT),
        cost_estimate=pl.CostEstimate(
            flops=2 * 32 * 128 * 256 * 128, bytes_accessed=1_500_000, transcendentals=1_000_000
        ),
        name="attend",
    )(index, sinks, query, own, halo)


def by_field(rows):
    count = rows.shape[0]
    padded = jnp.pad(rows, ((0, 0), (0, 3072 - rows.shape[1]))).reshape(count, 6, 512)
    source = lax.broadcasted_iota(jnp.int32, (512, 512), 0)
    target = lax.broadcasted_iota(jnp.int32, (512, 512), 1)
    wanted = 128 * (source % 4) + source // 4
    spread = jnp.where(target == wanted, 1.0, 0.0).astype(BF16)
    sorted_rows = jnp.einsum("rbs,st->rbt", padded, spread, preferred_element_type=F32)
    sorted_rows = sorted_rows.reshape(count, CHUNKS, 2, 4, 128)
    places = [sorted_rows[:, :, :, field] for field in (0, 2, 1, 3)]
    return jnp.stack(places, axis=2).reshape(count, CHUNKS, 4, 256)


def body(
    tokens,
    route_ids,
    route_level,
    gate_up_codes,
    gate_up_scale,
    gate_up_bias,
    down_codes,
    down_scale,
    down_bias,
    attn_gain,
    query_weight,
    key_matrix,
    value_matrix,
    sinks,
):
    own_tokens, width = tokens.shape
    group_size = lax.axis_size("expert")
    chips = group_size // 2
    device_index = lax.axis_index("expert")
    chip = device_index // 2
    core = device_index % 2
    side = 2 * core - 1

    packed = pack(tokens, route_ids, route_level)
    gathered = lax.all_gather(packed, "expert", axis=0, tiled=True)

    up_scale = jnp.exp2((gate_up_scale[0] - 128).astype(F32)).astype(BF16)
    by_place = by_field(jnp.concatenate([up_scale, gate_up_bias], axis=0))
    up_scales = (
        by_place[:45].reshape(5, 9, CHUNKS, 4, 256).transpose(0, 2, 1, 3, 4)
    ).reshape(5, CHUNKS, 36, 256)
    first_bias = by_place[45].reshape(CHUNKS, 1, 1024)
    down_scales = jnp.pad(
        jnp.exp2((down_scale[0] - 128).astype(F32)), ((0, 3), (0, WIDE - width))
    )
    second_bias = jnp.pad(down_bias.astype(F32), ((0, 0), (0, WIDE - width)))
    second = decode_down(down_codes[0], down_scales)
    first = decode_up(gate_up_codes[0], up_scales)

    half_dim = HEAD_SIZE // 2
    frequency = jnp.power(
        jnp.float32(150000.0), -2.0 * jnp.arange(half_dim, dtype=F32) / (2 * half_dim)
    )
    token_positions = device_index * own_tokens + jnp.arange(own_tokens, dtype=jnp.int32)
    angles = token_positions.astype(F32)[:, None] * frequency[None, :]
    cosine = jnp.tile(jnp.cos(angles), (1, 4))
    sine_part = jnp.sin(angles)
    sine_part = jnp.concatenate([-sine_part, sine_part, -sine_part, sine_part], axis=1)

    def shard(toward, distance, column):
        return ((chip + toward * distance) % chips) * 2 + column

    far = chips // 2

    def order(toward, column, distances):
        chosen = []
        for distance in distances:
            chosen.append(shard(toward, distance, column))
            if 0 < distance < far:
                chosen.append(shard(toward, distance, 1 - column))
        return chosen

    partner = [(i, i ^ 1) for i in range(group_size)]
    experts = [device_index, device_index + 1 - 2 * core]

    def serve(distances):
        mine = order(side, core, distances)
        others = order(-side, 1 - core, distances)
        near, other = run_experts(
            mine + others, device_index, gathered, first, second, first_bias, second_bias
        )
        return combine(mine, experts, gathered, near, lax.ppermute(other, "expert", partner))

    early = serve([far, far - 1])
    late = serve(list(range(far - 2, -1, -1)))

    def onward(block, across):
        route = []
        for i in range(group_size):
            step = 2 if i % 2 else -2
            goal = (i + step) % group_size
            route.append((i, goal ^ 1 if across else goal))
        return lax.ppermute(block.astype(jnp.float16), "expert", route).astype(F32)

    moving = onward(early[0], False)
    moving = jnp.concatenate([early[1] + moving, early[2]], axis=0)
    for distance in range(far - 2, 0, -1):
        here = 2 * (far - 2 - distance)
        moving = onward(moving, False)
        moving = late[here : here + 2].reshape(2 * own_tokens, WIDE) + moving
    from_one = onward(moving[:own_tokens], False)
    from_other = onward(moving[own_tokens:], True)
    mixture = (late[2 * (far - 2)] + from_one + from_other)[:, :width] * (1.0 / RETURN_SCALE)

    block_out, normed, own_kv = mix(
        tokens, mixture, attn_gain[None], key_matrix, value_matrix, cosine, sine_part
    )
    ahead = [(i, i + 1) for i in range(group_size - 1)]
    halo_kv = lax.ppermute(own_kv, "expert", ahead)
    query = queries(normed, query_weight, cosine, sine_part)
    attended = attend(device_index.reshape(1), sinks, query, own_kv, halo_kv)
    return (block_out, attended)


def solution(mesh):
    in_specs = (
        P(("dp", "expert"), None),
        P(("dp", "expert"), None),
        P(("dp", "expert"), None),
        P("expert", None, None),
        P("expert", None, None),
        P("expert", None),
        P("expert", None, None),
        P("expert", None, None),
        P("expert", None),
        P(),
        P(),
        P(),
        P(),
        P(),
    )
    out_specs = (P(("dp", "expert"), None), P(("dp", "expert"), None))
    return jax.shard_map(body, mesh=mesh, in_specs=in_specs, out_specs=out_specs, check_vma=False)
```

profile of v0, /device:TPU:1, one launch (start us, length us, event | category | flops | bytes accessed | tf_op | source)
XLA Modules:
  0.0 173.8 jit_solution(1898847213380334132)
XLA Ops:
  7.2 0.0 all-gather.2.cloned.1.call-start
  7.2 1.5 copy.43.ids_ref
  8.7 1.4 copy.44.level_ref
  10.1 1.9 %copy.55.tokens_ref = bf16[128,1440]{1,0:T(8,128)(2,1)} copy(bf16[128,1440]{0,1:T(8,128)(2,1)} %param.14) | data formatting | bytes 737280 | tf_op args[0]
  12.0 1.9 %pack.1 = bf16[128,1536]{1,0:T(8,128)(2,1)} custom-call(bf16[128,1440]{1,0:T(8,128)(2,1)} %copy.55.tokens_ref, s32[128,4]{1,0:T(8,128)} %copy.43.ids_ref, s32[128,4]{1,0:T(8,128)} %copy.44.level_ref), custom_call_target="tpu_custom_call" | custom-call | tf_op jit(solution)/shard_map/pack/pallas_call | solution.py:110
  13.9 0.0 all-gather.2.cloned.1.call-update
  14.0 0.9 exponential_convert_fusion
  15.0 0.1 dot_general.5
  15.2 0.4 fusion.9
  15.8 0.4 copy.49
  16.1 0.1 copy.50
  16.3 0.6 copy.52
  16.9 1.0 reshape.124.scale_ref
  17.9 0.1 fusion.26
  18.0 0.7 pad.15.scale_ref
  18.7 0.6 stack.103.place_ref
  19.3 7.8 %decode_down.1.refs_11_.refs_7_ = bf16[3,512,1536]{2,1,0:T(8,128)(2,1)} custom-call(s32[1440,360]{1,0:T(8,128)} %bitcast.71, s32[1440,360]{1,0:T(8,128)} %bitcast.72, s32[1440,360]{1,0:T(8,128)} %bitcast.73, f32[48,1536]{1,0:T(8,128)} %pad.15.scale_ref), custom_call_target="tpu_custom_call" | custom-call | flops 60000000 | bytes 7000000 | tf_op jit(solution)/shard_map/decode_down/pallas_call | solution.py:85
  27.1 14.5 %decode_up.1.refs_10_.refs_6_ = bf16[3,1440,1024]{2,1,0:T(8,128)(2,1)} custom-call(s32[1440,720]{1,0:T(8,128)} %bitcast.74, f32[5,3,36,256]{3,2,1,0:T(8,128)} %reshape.124.scale_ref), custom_call_target="tpu_custom_call" | custom-call | flops 60000000 | bytes 14000000 | tf_op jit(solution)/shard_map/decode_up/pallas_call | solution.py:43
  41.6 0.6 pad_convert_fusion.refs_13_.refs_9_
  42.2 22.1 %all-gather.2.cloned.1.call-done.refs_0_.refs_1_.refs_2_.refs_3_.refs_4_.refs_5_.refs_6_.refs_7_.refs_8_.refs_9_ = bf16[2048,1536]{1,0:T(8,128)(2,1)} async-done(((bf16[128,1536]{1,0:T(8,128)(2,1)}), bf16[2048,1536]{1,0:T(8,128)(2,1)}) %all-gather.2.cloned.1.call-update) | async-done | bytes 6291472 | tf_op jit(solution)/shard_map/all_gather | solution.py:468
  64.3 13.2 %experts.3 = (bf16[192,1536]{1,0:T(8,128)(2,1)}, bf16[192,1536]{1,0:T(8,128)(2,1)}) custom-call(s32[7]{0:T(128)} %stack.103.place_ref, bf16[2048,1536]{1,0:T(8,128)(2,1)} %all-gather.2.cloned.1.call-done.refs_0_.refs_1_.refs_2_.refs_3_.refs_4_.refs_5_.refs_6_.refs_7_.refs_8_.refs_9_, ...), custom_call_target="tpu_custom_call" | custom-call | flops 4777574400 | bytes 15000000 | tf_op jit(solution)/shard_map/experts/pallas_call | solution.py:200
  77.6 0.3 collective-permute-start.1
  77.8 0.6 stack.99.place_ref
  78.4 0.6 stack.94.place_ref
  79.1 0.7 collective-permute-done.1.refs_4_
  79.8 0.8 copy-done.2
  80.6 4.5 %combine.3 = f32[3,128,1536]{2,1,0:T(8,128)} custom-call(s32[5]{0:T(128)} %stack.99.place_ref, bf16[2048,1536]{1,0:T(8,128)(2,1)} %all-gather.2.cloned.1.call-done.refs_0_.refs_1_.refs_2_.refs_3_.refs_4_.refs_5_.refs_6_.refs_7_.refs_8_.refs_9_, ...), custom_call_target="tpu_custom_call" | custom-call | flops 301989888 | bytes 4500000 | tf_op jit(solution)/shard_map/combine/pallas_call | solution.py:264
  85.1 1.8 %convert.19 = f16[3,128,1536]{2,1,0:T(8,128)(2,1)S(1)} convert(f32[3,128,1536]{2,1,0:T(8,128)} %combine.3) | non-fusion elementwise | flops 589824 | bytes 3538944 | tf_op jit(solution)/shard_map/convert.8
  86.9 0.1 slice_bitcast_fusion.3
  87.1 1.2 collective-permute-start.2
  88.2 18.6 %experts.2 = (bf16[320,1536]{1,0:T(8,128)(2,1)}, bf16[320,1536]{1,0:T(8,128)(2,1)}) custom-call(s32[11]{0:T(128)} %stack.94.place_ref, bf16[2048,1536]{1,0:T(8,128)(2,1)} %all-gather.2.cloned.1.call-done.refs_0_.refs_1_.refs_2_.refs_3_.refs_4_.refs_5_.refs_6_.refs_7_.refs_8_.refs_9_, ...), custom_call_target="tpu_custom_call" | custom-call | flops 7962624000 | bytes 15000000 | tf_op jit(solution)/shard_map/experts/pallas_call | solution.py:200
  106.8 1.2 collective-permute-start
  108.1 1.2 fusion.5
  109.3 0.2 pad_maximum_fusion
  109.5 0.1 collective-permute-start.3
  109.6 0.6 stack.88.place_ref
  110.2 0.3 collective-permute-done.refs_6_
  110.5 0.9 copy-done
  111.4 5.8 %combine.2 = f32[5,128,1536]{2,1,0:T(8,128)} custom-call(s32[7]{0:T(128)} %stack.88.place_ref, bf16[2048,1536]{1,0:T(8,128)(2,1)} %all-gather.2.cloned.1.call-done.refs_0_.refs_1_.refs_2_.refs_3_.refs_4_.refs_5_.refs_6_.refs_7_.refs_8_.refs_9_, ...), custom_call_target="tpu_custom_call" | custom-call | flops 503316480 | bytes 7500000 | tf_op jit(solution)/shard_map/combine/pallas_call | solution.py:264
  117.2 2.1 %fusion.37 = (f32[2,128,1536]{2,1,0:T(8,128)S(1)}, f32[2,128,1536]{2,1,0:T(8,128)S(1)}) fusion(f32[5,128,1536]{2,1,0:T(8,128)} %combine.2), kind=kLoop, calls=%fused_computation.67 | loop fusion | bytes 6291456 | tf_op jit(solution)/shard_map/slice | solution.py:533
  119.3 2.3 %collective-permute-done.3 = f16[256,1536]{1,0:T(8,128)(2,1)S(1)} collective-permute-done((f16[256,1536]{1,0:T(8,128)(2,1)S(1)}, f16[256,1536]{1,0:T(8,128)(2,1)S(1)}, u32[]{:S(2)}, u32[]{:S(2)}) %collective-permute-start.3) | collective-permute-done | bytes 786464 | tf_op jit(solution)/shard_map/ppermute | solution.py:526
  121.6 0.9 copy-done.1
  122.5 1.4 fusion
  123.9 0.1 collective-permute-start.4
  124.0 0.6 broadcast_in_dim.15.gain_ref
  124.7 0.3 fusion.27
  125.0 0.1 copy.54
  125.1 0.7 copy.56.cos_ref
  125.8 0.8 pad_maximum_fusion.2.sin_ref
  126.5 9.5 %collective-permute-done.4 = f16[256,1536]{1,0:T(8,128)(2,1)S(1)} collective-permute-done((f16[256,1536]{1,0:T(8,128)(2,1)S(1)}, f16[256,1536]{1,0:T(8,128)(2,1)S(1)}, u32[]{:S(2)}, u32[]{:S(2)}) %collective-permute-start.4) | collective-permute-done | bytes 786464 | tf_op jit(solution)/shard_map/ppermute | solution.py:526
  136.1 0.2 fusion.1
  136.3 0.1 fusion.38
  136.4 0.1 collective-permute-start.5
  136.5 1.6 collective-permute-start.6
  138.1 1.2 slice_bitcast_fusion.1
  139.3 5.1 %collective-permute-done.5 = f16[128,1536]{1,0:T(8,128)(2,1)S(1)} collective-permute-done((f16[128,1536]{1,0:T(8,128)(2,1)S(1)}, f16[128,1536]{1,0:T(8,128)(2,1)S(1)}, u32[]{:S(2)}, u32[]{:S(2)}) %collective-permute-start.5) | collective-permute-done | bytes 393248 | tf_op jit(solution)/shard_map/ppermute | solution.py:526
  144.3 3.7 %collective-permute-done.6 = f16[128,1536]{1,0:T(8,128)(2,1)S(1)} collective-permute-done((f16[128,1536]{1,0:T(8,128)(2,1)S(1)}, f16[128,1536]{1,0:T(8,128)(2,1)S(1)}, u32[]{:S(2)}, u32[]{:S(2)}) %collective-permute-start.6) | collective-permute-done | bytes 393248 | tf_op jit(solution)/shard_map/ppermute | solution.py:526
  148.0 1.0 fusion.3.mixture_ref
  149.1 3.1 %mix.1 = (bf16[128,1440]{1,0:T(8,128)(2,1)}, bf16[128,1440]{1,0:T(8,128)(2,1)}, bf16[128,512]{1,0:T(8,128)(2,1)}) custom-call(bf16[128,1440]{1,0:T(8,128)(2,1)} %copy.55.tokens_ref, f32[128,1440]{1,0:T(8,128)} %fusion.3.mixture_ref, bf16[1,1440]{1,0:T(2,128)(2,1)} %broadcast_in_dim.15.gain_ref, bf16[1440,256]{1,0:T(8,128)(2,1)} %key_ref.1, ...), custom_call_target="tpu_custom_call" | custom-call | flops 188743680 | bytes 3000000 | tf_op jit(solution)/shard_map/mix/pallas_call | solution.py:307
  152.2 2.1 %collective-permute-start.7 = (bf16[128,512]{1,0:T(8,128)(2,1)}, bf16[128,512]{1,0:T(8,128)(2,1)S(1)}, u32[]{:S(2)}, u32[]{:S(2)}) collective-permute-start(bf16[128,512]{1,0:T(8,128)(2,1)} %get-tuple-element.15.own_ref), channel_id=1, source_target_pairs={{0,1},{1,2},{2,3},{3,4},{4,5},{5,6},{6,7},{7,8},{8,9},{9,10},{10,1... | collective-permute-start | bytes 393224 | tf_op jit(solution)/shard_map/ppermute | solution.py:542
  154.3 1.9 %copy.58 = bf16[128,1440]{0,1:T(8,128)(2,1)} copy(bf16[128,1440]{1,0:T(8,128)(2,1)} %get-tuple-element.20) | data formatting | bytes 737280
  156.2 5.4 %queries.1.queries_ref = bf16[4,512,128]{2,1,0:T(8,128)(2,1)} custom-call(bf16[128,1440]{1,0:T(8,128)(2,1)} %get-tuple-element.14.normed_ref, bf16[1440,2048]{1,0:T(8,128)(2,1)} %weight_ref.1, f32[128,128]{1,0:T(8,128)} %copy.56.cos_ref, f32[128,128]{1,0:T(8,128)} %pad_maximum_fusion.2.sin_ref), custom_call_target="tpu_custom_call" | custom-call | flops 754974720 | bytes 7000000 | tf_op jit(solution)/shard_map/queries/pallas_call | solution.py:331
  161.6 0.6 copy-done.8
  162.2 4.7 %attend.1 = bf16[128,2048]{1,0:T(8,128)(2,1)} custom-call(s32[1]{0:T(128)} %bitcast.5.index_ref, f32[32]{0:T(128)} %sinks_ref.1, bf16[4,512,128]{2,1,0:T(8,128)(2,1)} %queries.1.queries_ref, bf16[128,512]{1,0:T(8,128)(2,1)} %get-tuple-element.15.own_ref, bf16[128,512]{1,0:T(8,128)(2,1)} %copy-done.8), custom_call_target="tpu_custom_call" | custom-call | flops 268435456 | bytes 1500000 | tf_op jit(solution)/shard_map/attend/pallas_call | solution.py:411
  (28 shorter events, 0.3 us)
Async XLA Ops:
  7.2 6.9 %copy-start.3 = (s32[1,45,2880]{2,0,1:T(1,128)S(1)}, s32[1,45,2880]{2,0,1:T(1,128)}, u32[]{:S(2)}) copy-start(s32[1,45,2880]{2,0,1:T(1,128)} %param.18) | copy-start | bytes 1555204
  7.2 57.2 %all-gather.2.cloned.1.call-start = ((), (), s32[]{:S(2)}) async-start(), calls=%async_computation | async-start | bytes 6684672 | tf_op jit(solution)/shard_map/all_gather | solution.py:468
  12.0 3.0 %copy-start.5 = (bf16[1,2880]{1,0:T(2,128)(2,1)S(1)}, bf16[1,2880]{1,0:T(2,128)(2,1)}, u32[]{:S(2)}) copy-start(bf16[1,2880]{1,0:T(2,128)(2,1)} %param.19) | copy-start | bytes 17284
  16.1 1.8 %copy-start.4 = (s32[1,45,1440]{2,0,1:T(1,128)S(1)}, s32[1,45,1440]{2,0,1:T(1,128)}, u32[]{:S(2)}) copy-start(s32[1,45,1440]{2,0,1:T(1,128)} %param.21) | copy-start | bytes 777604
  27.1 14.5 %copy-start.6 = (bf16[1,1440]{1,0:T(2,128)(2,1)S(1)}, bf16[1,1440]{1,0:T(2,128)(2,1)}, u32[]{:S(2)}) copy-start(bf16[1,1440]{1,0:T(2,128)(2,1)} %param.22) | copy-start | bytes 8644
  77.6 2.2 %collective-permute-start.1 = (bf16[192,1536]{1,0:T(8,128)(2,1)}, bf16[192,1536]{1,0:T(8,128)(2,1)S(1)}, u32[]{:S(2)}, u32[]{:S(2)}) collective-permute-start(bf16[192,1536]{1,0:T(8,128)(2,1)} %get-tuple-element.12), channel_id=1, source_target_pairs={{0,1},{1,0},{2,3},{3,2},{4,5},{5,4},{6,7},{7,6},{8,9},{9,8},{10,11... | collective-permute-start | bytes 1769480 | tf_op jit(solution)/shard_map/ppermute | solution.py:515
  79.8 0.8 copy-start.2
  87.1 21.0 %collective-permute-start.2 = (f16[128,1536]{1,0:T(8,128)(2,1)S(1)}, f16[128,1536]{1,0:T(8,128)(2,1)S(1)}, u32[]{:S(2)}, u32[]{:S(2)}) collective-permute-start(f16[128,1536]{1,0:T(8,128)(2,1)S(1)} %get-tuple-element.24), channel_id=1, source_target_pairs={{0,14},{1,3},{2,0},{3,5},{4,2},{5,7},{6,4},{7,9},{8,6},{9,11},{10,... | collective-permute-start | bytes 1179656 | tf_op jit(solution)/shard_map/ppermute | solution.py:526
  106.8 3.6 %collective-permute-start = (bf16[320,1536]{1,0:T(8,128)(2,1)}, bf16[320,1536]{1,0:T(8,128)(2,1)S(1)}, u32[]{:S(2)}, u32[]{:S(2)}) collective-permute-start(bf16[320,1536]{1,0:T(8,128)(2,1)} %get-tuple-element.10), channel_id=1, source_target_pairs={{0,1},{1,0},{2,3},{3,2},{4,5},{5,4},{6,7},{7,6},{8,9},{9,8},{10,11... | collective-permute-start | bytes 2949128 | tf_op jit(solution)/shard_map/ppermute | solution.py:515
  109.5 12.1 %collective-permute-start.3 = (f16[256,1536]{1,0:T(8,128)(2,1)S(1)}, f16[256,1536]{1,0:T(8,128)(2,1)S(1)}, u32[]{:S(2)}, u32[]{:S(2)}) collective-permute-start(f16[256,1536]{1,0:T(8,128)(2,1)S(1)} %pad_maximum_fusion), channel_id=1, source_target_pairs={{0,14},{1,3},{2,0},{3,5},{4,2},{5,7},{6,4},{7,9},{8,6},{9,11},{10,... | collective-permute-start | bytes 2359304 | tf_op jit(solution)/shard_map/ppermute | solution.py:526
  110.5 0.9 copy-start
  121.6 0.9 copy-start.1
  122.5 1.5 copy-start.7
  123.9 12.1 %collective-permute-start.4 = (f16[256,1536]{1,0:T(8,128)(2,1)S(1)}, f16[256,1536]{1,0:T(8,128)(2,1)S(1)}, u32[]{:S(2)}, u32[]{:S(2)}) collective-permute-start(f16[256,1536]{1,0:T(8,128)(2,1)S(1)} %fusion), channel_id=1, source_target_pairs={{0,14},{1,3},{2,0},{3,5},{4,2},{5,7},{6,4},{7,9},{8,6},{9,11},{10,... | collective-permute-start | bytes 2359304 | tf_op jit(solution)/shard_map/ppermute | solution.py:526
  136.4 7.9 %collective-permute-start.5 = (f16[128,1536]{1,0:T(8,128)(2,1)S(1)}, f16[128,1536]{1,0:T(8,128)(2,1)S(1)}, u32[]{:S(2)}, u32[]{:S(2)}) collective-permute-start(f16[128,1536]{1,0:T(8,128)(2,1)S(1)} %get-tuple-element.26), channel_id=1, source_target_pairs={{0,14},{1,3},{2,0},{3,5},{4,2},{5,7},{6,4},{7,9},{8,6},{9,11},{10,... | collective-permute-start | bytes 1179656 | tf_op jit(solution)/shard_map/ppermute | solution.py:526
  136.5 11.5 %collective-permute-start.6 = (f16[128,1536]{1,0:T(8,128)(2,1)S(1)}, f16[128,1536]{1,0:T(8,128)(2,1)S(1)}, u32[]{:S(2)}, u32[]{:S(2)}) collective-permute-start(f16[128,1536]{1,0:T(8,128)(2,1)S(1)} %get-tuple-element.27), channel_id=1, source_target_pairs={{0,15},{1,2},{2,1},{3,4},{4,3},{5,6},{6,5},{7,8},{8,7},{9,10},{10,... | collective-permute-start | bytes 1179656 | tf_op jit(solution)/shard_map/ppermute | solution.py:526
  152.2 9.4 %collective-permute-start.7 = (bf16[128,512]{1,0:T(8,128)(2,1)}, bf16[128,512]{1,0:T(8,128)(2,1)S(1)}, u32[]{:S(2)}, u32[]{:S(2)}) collective-permute-start(bf16[128,512]{1,0:T(8,128)(2,1)} %get-tuple-element.15.own_ref), channel_id=1, source_target_pairs={{0,1},{1,2},{2,3},{3,4},{4,5},{5,6},{6,7},{7,8},{8,9},{9,10},{10,1... | collective-permute-start | bytes 393224 | tf_op jit(solution)/shard_map/ppermute | solution.py:542
  161.6 0.6 copy-start.8
Sparse Core Ops, SparseCore 0:
  14.0 50.2 all-gather.1
where the time goes:
time: 175 us; the launch traced here: 174 us
  Pallas kernels  79.5 us (45%)
  waiting for transfers between devices  43.8 us (25%)
  local copies, waits for them, and re-layouts  20.5 us (12%)
  between operations  14.4 us (8%)
  other arithmetic  8.61 us (5%)
  starting transfers between devices  6.62 us (4%)
    pallas_call x2, Pallas kernels, run_experts(): pl.pallas_call(functools.partial(expert_kernel, count), grid_spec=pltpu.P...  31.9 us
    all_gather x1, waiting for transfers between devices, body(): gathered = lax.all_gather(packed, 'expert', axis=0, tiled=True)  22.1 us
    ppermute x5, waiting for transfers between devices, onward(): return lax.ppermute(block.astype(jnp.float16), 'expert', route).astype(F32)  20.6 us
    pallas_call x1, Pallas kernels, decode_up(): pl.pallas_call(decode_up_kernel, grid=(CHUNKS, 5), in_specs=[pl.BlockSpec...  14.5 us
    pallas_call x2, Pallas kernels, combine(): pl.pallas_call(functools.partial(combine_kernel, count), grid_spec=pltpu....  10.3 us
    unnamed x23, local copies, waits for them, and re-layouts  10.1 us
    pallas_call x1, Pallas kernels, decode_down(): pl.pallas_call(decode_down_kernel, grid=(CHUNKS,), in_specs=[pl.BlockSpec...  7.78 us
    pallas_call x1, Pallas kernels, queries(): pl.pallas_call(queries_kernel, grid=(4,), in_specs=[pl.BlockSpec((128, 14...  5.37 us
  transfers between devices with their start and end apart: 9, of which 7 were waited for; matrix products, arithmetic and copies ran while one was open for 10% of the time, Pallas kernels for 30%

commit v1 on v0

v1 whole, which is shorter than its diff:
```python
import functools

import jax
import jax.numpy as jnp
from jax import lax
from jax.experimental import pallas as pl
from jax.experimental.pallas import tpu as pltpu
from jax.sharding import PartitionSpec as P

HEAD_SIZE = 64
WINDOW_LENGTH = 128
MOST = 64
WIDE = 1536
CHUNKS = 3
RETURN_SCALE = 8.0
LARGE_LIMIT = 56 * 1024 * 1024
VMEM_LIMIT = 40 * 1024 * 1024
SMALL_LIMIT = 24 * 1024 * 1024
F32 = jnp.float32
BF16 = jnp.bfloat16


def twice_fp4(words, field_index):
    field = jnp.bitwise_and(jnp.right_shift(words, 4 * field_index), 15).astype(F32).astype(BF16)
    negative = field >= 8
    low = jnp.where(negative, field - 8, field)
    return negative, jnp.maximum(jnp.maximum(low, 2 * low - 4), 4 * low - 16)


def power_of_two(exponents, least, valid):
    step = exponents - least
    scale = jnp.where(step == 0, 1.0, jnp.where(step == 1, 2.0, jnp.where(step == 2, 4.0, 8.0)))
    return jnp.where(valid, scale * 2.0 ** (least - 128), 0.0)


def decode_up_kernel(codes_ref, exponent_ref, bias_ref, out_ref, bias_out_ref, scale_ref):
    source = lax.broadcasted_iota(jnp.int32, (512, 512), 0)
    target = lax.broadcasted_iota(jnp.int32, (512, 512), 1)
    wanted = 128 * jnp.bitwise_and(source, 3) + jnp.right_shift(source, 2)
    spread = jnp.where(target == wanted, 1.0, 0.0).astype(BF16)
    for half in range(2):
        lanes = slice(512 * half, 512 * half + 512)
        left = 2880 - 1024 * pl.program_id(0) - 512 * half
        column = lax.broadcasted_iota(jnp.int32, (45, 512), 1)
        scale = power_of_two(exponent_ref[:, lanes], 119, column < left)
        scale = jnp.dot(scale.astype(BF16), spread, preferred_element_type=F32)
        bias = jnp.where(column[:1] < left, bias_ref[:, lanes].astype(F32), 0.0)
        bias = jnp.broadcast_to(bias, (16, 512)).astype(BF16)
        bias = jnp.dot(bias, spread, preferred_element_type=F32)
        for place, field_index in enumerate((0, 2, 1, 3)):
            taken = slice(128 * field_index, 128 * field_index + 128)
            given = slice(256 * place + 128 * half, 256 * place + 128 * half + 128)
            scale_ref[:45, given] = scale[:, taken]
            bias_out_ref[0, :, given] = bias[:1, taken]
    for block in range(45):
        words = codes_ref[32 * block : 32 * block + 32, :]
        for place, field_index in enumerate((0, 2, 1, 3)):
            lanes = slice(256 * place, 256 * place + 256)
            scale = scale_ref[block : block + 1, lanes]
            negative, size = twice_fp4(words, field_index)
            scale = jnp.broadcast_to(scale.astype(BF16), size.shape)
            out_ref[0, 32 * block : 32 * block + 32, lanes] = size * jnp.where(
                negative, -scale, scale
            )


def decode_up(codes, exponents, bias):
    rows = codes.shape[0]
    return pl.pallas_call(
        decode_up_kernel,
        grid=(CHUNKS,),
        in_specs=[
            pl.BlockSpec((1440, 256), lambda b: (0, b)),
            pl.BlockSpec((45, 1024), lambda b: (0, b)),
            pl.BlockSpec((1, 1024), lambda b: (0, b)),
        ],
        out_specs=[
            pl.BlockSpec((1, 1440, 1024), lambda b: (b, 0, 0)),
            pl.BlockSpec((1, 1, 1024), lambda b: (b, 0, 0)),
        ],
        out_shape=[
            jax.ShapeDtypeStruct((CHUNKS, rows, 1024), BF16),
            jax.ShapeDtypeStruct((CHUNKS, 1, 1024), F32),
        ],
        scratch_shapes=[pltpu.VMEM((48, 1024), F32)],
        compiler_params=pltpu.CompilerParams(vmem_limit_bytes=LARGE_LIMIT),
        cost_estimate=pl.CostEstimate(flops=60_000_000, bytes_accessed=30_000_000, transcendentals=0),
        name="decode_up",
    )(codes, exponents, bias)


def decode_down_kernel(
    left_ref, middle_ref, right_ref, left_exp_ref, middle_exp_ref, right_exp_ref, out_ref
):
    row = lax.broadcasted_iota(jnp.int32, (16, 512), 0) + 16 * pl.program_id(0)
    column = lax.broadcasted_iota(jnp.int32, (16, 512), 1)
    scales = [
        power_of_two(exponent_ref[...], 117, (row < 45) & (column < 1440 - 512 * part))
        for part, exponent_ref in enumerate((left_exp_ref, middle_exp_ref, right_exp_ref))
    ]
    source = lax.broadcasted_iota(jnp.int32, (512, 512), 0)
    target = lax.broadcasted_iota(jnp.int32, (512, 512), 1)
    wanted = 4 * jnp.bitwise_and(source, 127) + jnp.right_shift(source, 7)
    spread = jnp.where(target == wanted, 1.0, 0.0).astype(BF16)
    for parity in range(2):
        for part, codes_ref in enumerate((left_ref, middle_ref, right_ref)):
            piece = codes_ref[pl.ds(parity, 256, 2), :]
            fields = []
            for field_index in range(4):
                negative, size = twice_fp4(piece, field_index)
                fields.append(jnp.where(negative, -size, size))
            natural = jnp.dot(
                jnp.concatenate(fields, axis=1), spread, preferred_element_type=F32
            )
            for block in range(16):
                scale = scales[part][block : block + 1, :]
                row = 256 * parity + 16 * block
                out_ref[0, row : row + 16, 512 * part : 512 * part + 512] = (
                    natural[16 * block : 16 * block + 16] * scale
                ).astype(BF16)


def decode_down(codes, exponents):
    return pl.pallas_call(
        decode_down_kernel,
        grid=(CHUNKS,),
        in_specs=[
            pl.BlockSpec((512, 128), lambda b: (b, 0)),
            pl.BlockSpec((512, 128), lambda b: (b, 1)),
            pl.BlockSpec((512, 128), lambda b: (b, 2)),
            pl.BlockSpec((16, 512), lambda b: (b, 0)),
            pl.BlockSpec((16, 512), lambda b: (b, 1)),
            pl.BlockSpec((16, 512), lambda b: (b, 2)),
        ],
        out_specs=pl.BlockSpec((1, 512, WIDE), lambda b: (b, 0, 0)),
        out_shape=jax.ShapeDtypeStruct((CHUNKS, 512, WIDE), BF16),
        compiler_params=pltpu.CompilerParams(vmem_limit_bytes=VMEM_LIMIT),
        cost_estimate=pl.CostEstimate(flops=60_000_000, bytes_accessed=20_000_000, transcendentals=0),
        name="decode_down",
    )(codes, codes, codes, exponents, exponents, exponents)


def pack_kernel(tokens_ref, ids_ref, level_ref, out_ref):
    for place in range(11):
        block = tokens_ref[128 * place : 128 * place + 128, :].astype(F32)
        out_ref[:, 128 * place : 128 * place + 128] = block.T.astype(BF16)
    expert = lax.broadcasted_iota(jnp.int32, (16, 128), 0)
    named = jnp.zeros((16, 128), F32)
    chosen = jnp.zeros((16, 128), F32)
    whole = jnp.zeros((1, 128), F32)
    for choice in range(4):
        raised = jnp.exp(level_ref[choice : choice + 1, :].astype(F32) / 4.0)
        same = ids_ref[choice : choice + 1, :] == expert
        named = jnp.where(same, 1.0, named)
        chosen = jnp.where(same, raised, chosen)
        whole = whole + raised
    row = lax.broadcasted_iota(jnp.int32, (128, 128), 0)
    column = lax.broadcasted_iota(jnp.int32, (128, 128), 1)
    before = jnp.where(row < column, 1.0, 0.0).astype(BF16)
    rank = jnp.dot(named.astype(BF16), before, preferred_element_type=F32)
    weight = chosen / whole * RETURN_SCALE
    high = weight.astype(BF16).astype(F32)
    last = jnp.concatenate(
        [
            tokens_ref[1408:, :].astype(F32),
            jnp.where(named > 0.0, rank, 128.0),
            high,
            weight - high,
            jnp.zeros((48, 128), F32),
        ],
        axis=0,
    )
    out_ref[:, 1408:] = last.T.astype(BF16)


def pack(tokens, route_ids, route_level):
    return pl.pallas_call(
        pack_kernel,
        out_shape=jax.ShapeDtypeStruct((128, WIDE), BF16),
        compiler_params=pltpu.CompilerParams(vmem_limit_bytes=VMEM_LIMIT),
        name="pack",
    )(tokens.T, route_ids.T, route_level.T)


def relay(block, after):
    return lax.optimization_barrier((block, after))[0]


def combine_weights(shard_ref, place_ref):
    lane = lax.broadcasted_iota(jnp.int32, (128, 384), 1)
    source = lax.broadcasted_iota(jnp.int32, (128, 384), 0)
    expert = jnp.where(jnp.bitwise_and(lane, 127) < MOST, place_ref[0], place_ref[1])
    wanted = 32 + 16 * jnp.right_shift(lane, 7) + expert
    spread = jnp.where(source == wanted, 1.0, 0.0).astype(BF16)
    slot = jnp.bitwise_and(lane[:, :128], MOST - 1).astype(F32)
    meta = jnp.dot(shard_ref[:, 1408:1536], spread, preferred_element_type=F32)
    keep = meta[:, :128] == slot
    parts = [jnp.where(keep, meta[:, 128 * i : 128 * i + 128], 0.0) for i in (1, 2)]
    return jnp.concatenate(parts, axis=1).astype(BF16)


def expert_kernel(count, place_ref, *refs):
    shards = refs[:count]
    (
        first_ref,
        second_ref,
        first_bias_ref,
        second_bias_ref,
        mine_ref,
        other_ref,
        weight_ref,
        rows_ref,
        total_ref,
    ) = refs[count:]
    chunk = pl.program_id(0)
    half = count // 2 * MOST

    @pl.when(chunk == 0)
    def _():
        lane = lax.broadcasted_iota(jnp.int32, (128, 128), 1)
        source = lax.broadcasted_iota(jnp.int32, (128, 128), 0)
        spread = jnp.where(source == 32 + place_ref[0], 1.0, 0.0).astype(BF16)
        slot = jnp.bitwise_and(lane, MOST - 1).astype(F32)
        lower = lane < MOST
        for j in range(0, count, 2):
            picks = []
            for i in range(2):
                at = jnp.dot(shards[j + i][:, 1408:1536], spread, preferred_element_type=F32)
                keep = (at == slot) & (lower if i == 0 else jnp.logical_not(lower))
                picks.append(jnp.where(keep, 1.0, 0.0).astype(BF16))
                if j + i < count // 2:
                    weight_ref[j + i] = combine_weights(shards[j + i], place_ref)
            rows = lax.dot_general(
                jnp.concatenate(picks, axis=0),
                jnp.concatenate([shards[j][...], shards[j + 1][...]], axis=0),
                (((0,), (0,)), ((), ())),
                preferred_element_type=F32,
            )
            rows_ref[MOST * j : MOST * j + 2 * MOST, :] = rows.astype(BF16)

    pre = jnp.dot(rows_ref[:, :1440], first_ref[0], preferred_element_type=F32)
    pre = pre + first_bias_ref[chunk]
    gate = jnp.minimum(pre[:, :512], 7.0)
    up = jnp.clip(pre[:, 512:], -7.0, 7.0)
    activated = ((up + 1.0) * gate * (0.5 + 0.5 * jnp.tanh(0.851 * gate))).astype(BF16)
    product = jnp.dot(activated, second_ref[0], preferred_element_type=F32)

    @pl.when(chunk == 0)
    def _():
        total_ref[...] = product + second_bias_ref[...]

    @pl.when(chunk == 1)
    def _():
        total_ref[...] += product

    @pl.when(chunk == CHUNKS - 1)
    def _():
        done = (total_ref[...] + product).astype(BF16)
        mine_ref[...] = done[:half]
        other_ref[...] = done[half:]


def run_experts(shards, experts, first, second, first_bias, second_bias):
    count = len(shards)
    rows = count * MOST
    half = jax.ShapeDtypeStruct((rows // 2, WIDE), BF16)
    half_spec = pl.BlockSpec(memory_space=pltpu.VMEM)
    return pl.pallas_call(
        functools.partial(expert_kernel, count),
        grid_spec=pltpu.PrefetchScalarGridSpec(
            num_scalar_prefetch=1,
            grid=(CHUNKS,),
            in_specs=[pl.BlockSpec(memory_space=pltpu.VMEM)] * count
            + [
                pl.BlockSpec((1, 1440, 1024), lambda b, place: (b, 0, 0)),
                pl.BlockSpec((1, 512, WIDE), lambda b, place: (b, 0, 0)),
                pl.BlockSpec((CHUNKS, 1, 1024), lambda b, place: (0, 0, 0)),
                pl.BlockSpec((1, WIDE), lambda b, place: (0, 0)),
            ],
            out_specs=[half_spec] * 3,
            scratch_shapes=[pltpu.VMEM((rows, WIDE), BF16), pltpu.VMEM((rows, WIDE), F32)],
        ),
        out_shape=[half, half, jax.ShapeDtypeStruct((count // 2, 128, 256), BF16)],
        compiler_params=pltpu.CompilerParams(vmem_limit_bytes=VMEM_LIMIT),
        cost_estimate=pl.CostEstimate(
            flops=4 * rows * 1440 * 4320, bytes_accessed=30_000_000, transcendentals=0
        ),
        name="experts",
    )(experts, *shards, first, second, first_bias, second_bias)


def combine_kernel(count, weight_ref, mine_ref, other_ref, *outs):
    for j in range(count):
        mine = mine_ref[MOST * j : MOST * j + MOST, :]
        other = other_ref[MOST * j : MOST * j + MOST, :]
        outs[j][...] = jnp.dot(
            weight_ref[j],
            jnp.concatenate([mine, other, mine, other], axis=0),
            preferred_element_type=F32,
        )


def combine(weight, mine, other):
    count = weight.shape[0]
    return pl.pallas_call(
        functools.partial(combine_kernel, count),
        in_specs=[pl.BlockSpec(memory_space=pltpu.VMEM)] * 3,
        out_specs=[pl.BlockSpec(memory_space=pltpu.VMEM)] * count,
        out_shape=[jax.ShapeDtypeStruct((128, WIDE), F32)] * count,
        compiler_params=pltpu.CompilerParams(vmem_limit_bytes=SMALL_LIMIT),
        cost_estimate=pl.CostEstimate(
            flops=2 * count * 128 * 256 * WIDE, bytes_accessed=1_500_000 * count, transcendentals=0
        ),
        name="combine",
    )(weight, mine, other)


def turned(block, cosine, sine_part):
    width = block.shape[1]
    lane = lax.broadcasted_iota(jnp.int32, block.shape, 1)
    first = jnp.bitwise_and(lane, 63) < 32
    swapped = jnp.where(first, pltpu.roll(block, width - 32, 1), pltpu.roll(block, 32, 1))
    copies = width // 128
    cosine = jnp.concatenate([cosine] * copies, axis=1)
    sine_part = jnp.concatenate([sine_part] * copies, axis=1)
    return block * cosine + swapped * sine_part


def mix_kernel(
    tokens_ref, mixture_ref, gain_ref, key_ref, value_ref, cos_ref, sin_ref, out_ref, normed_ref, kv_ref
):
    block_out = (tokens_ref[:, :1440].astype(F32) + mixture_ref[...]).astype(BF16)
    out_ref[...] = block_out
    widened = block_out.astype(F32)
    squares = jnp.sum(widened * widened, axis=1, keepdims=True) / 1440.0
    normed = (widened * lax.rsqrt(squares + 1e-05) * gain_ref[...].astype(F32)).astype(BF16)
    normed_ref[...] = normed
    keys = jnp.dot(normed, key_ref[...], preferred_element_type=F32)
    kv_ref[:, :256] = turned(keys, cos_ref[...], sin_ref[...]).astype(BF16)
    kv_ref[:, 256:] = jnp.dot(normed, value_ref[...], preferred_element_type=F32).astype(BF16)


def mix(tokens, mixture, gain, key_matrix, value_matrix, cosine, sine_part):
    return pl.pallas_call(
        mix_kernel,
        out_shape=[
            jax.ShapeDtypeStruct((128, 1440), BF16),
            jax.ShapeDtypeStruct((128, 1440), BF16),
            jax.ShapeDtypeStruct((128, 512), BF16),
        ],
        compiler_params=pltpu.CompilerParams(vmem_limit_bytes=VMEM_LIMIT),
        cost_estimate=pl.CostEstimate(
            flops=2 * 128 * 1440 * 512, bytes_accessed=3_000_000, transcendentals=0
        ),
        name="mix",
    )(tokens, mixture, gain, key_matrix, value_matrix, cosine, sine_part)


def queries_kernel(normed_ref, weight_ref, cos_ref, sin_ref, out_ref):
    projected = jnp.dot(normed_ref[...], weight_ref[...], preferred_element_type=F32)
    rotated = turned(projected, cos_ref[...], sin_ref[...])
    scaled = (rotated.astype(BF16).astype(F32) * 0.125).astype(BF16)
    for pair in range(4):
        out_ref[0, 128 * pair : 128 * pair + 128, :] = scaled[:, 128 * pair : 128 * pair + 128]


def queries(normed, weight, cosine, sine_part):
    return pl.pallas_call(
        queries_kernel,
        grid=(4,),
        in_specs=[
            pl.BlockSpec((128, 1440), lambda g: (0, 0)),
            pl.BlockSpec((1440, 512), lambda g: (0, g)),
            pl.BlockSpec((128, 128), lambda g: (0, 0)),
            pl.BlockSpec((128, 128), lambda g: (0, 0)),
        ],
        out_specs=pl.BlockSpec((1, 512, 128), lambda g: (g, 0, 0)),
        out_shape=jax.ShapeDtypeStruct((4, 512, 128), BF16),
        compiler_params=pltpu.CompilerParams(vmem_limit_bytes=VMEM_LIMIT),
        cost_estimate=pl.CostEstimate(
            flops=2 * 128 * 1440 * 2048, bytes_accessed=7_000_000, transcendentals=0
        ),
        name="queries",
    )(normed, weight, cosine, sine_part)


def attend_kernel(index_ref, sinks_ref, queries_ref, own_ref, halo_ref, out_ref):
    lane = lax.broadcasted_iota(jnp.int32, (128, 128), 1)
    lower = lane < 64

    def doubled(block, odd):
        block = block.astype(F32)
        if odd:
            high = jnp.where(lower, 0.0, block)
            low = pltpu.roll(high, 64, 1)
        else:
            low = jnp.where(lower, block, 0.0)
            high = pltpu.roll(low, 64, 1)
        return jnp.concatenate([low, high], axis=0).astype(BF16)

    row = lax.broadcasted_iota(jnp.int32, (128, 256), 0)
    column = jnp.bitwise_and(lax.broadcasted_iota(jnp.int32, (128, 256), 1), 127)
    mine = column <= row
    allowed = mine | jnp.broadcast_to(index_ref[0] > 0, mine.shape)
    for group in range(4):
        start = 128 * (group // 2)
        odd = group % 2 == 1
        query = queries_ref[group]
        across = (((1,), (1,)), ((), ()))
        here = lax.dot_general(
            query, doubled(own_ref[:, start : start + 128], odd), across, preferred_element_type=F32
        )
        there = lax.dot_general(
            query, doubled(halo_ref[:, start : start + 128], odd), across, preferred_element_type=F32
        )
        here_probs = []
        there_probs = []
        for pair in range(4):
            rows = slice(128 * pair, 128 * pair + 128)
            scores = jnp.where(mine, here[rows], there[rows])
            scores = jnp.where(allowed, scores, -1e30)
            halves = []
            for side in range(2):
                part = scores[:, 128 * side : 128 * side + 128]
                sink = sinks_ref[8 * group + 2 * pair + side]
                top = jnp.maximum(jnp.max(part, axis=1, keepdims=True), sink)
                weights = jnp.exp(part - top)
                whole = jnp.exp(sink - top) + jnp.sum(weights, axis=1, keepdims=True)
                halves.append(weights * (1.0 / whole))
            probs = jnp.where(allowed, jnp.concatenate(halves, axis=1), 0.0)
            here_probs.append(jnp.where(mine, probs, 0.0).astype(BF16))
            there_probs.append(jnp.where(mine, 0.0, probs).astype(BF16))
        mixed = jnp.dot(
            jnp.concatenate(here_probs, axis=0),
            doubled(own_ref[:, 256 + start : 384 + start], odd),
            preferred_element_type=F32,
        ) + jnp.dot(
            jnp.concatenate(there_probs, axis=0),
            doubled(halo_ref[:, 256 + start : 384 + start], odd),
            preferred_element_type=F32,
        )
        for pair in range(4):
            place = 512 * group + 128 * pair
            out_ref[:, place : place + 128] = mixed[128 * pair : 128 * pair + 128].astype(BF16)


def attend(index, sinks, query, own, halo):
    return pl.pallas_call(
        attend_kernel,
        in_specs=[
            pl.BlockSpec(memory_space=pltpu.SMEM),
            pl.BlockSpec(memory_space=pltpu.SMEM),
            pl.BlockSpec(memory_space=pltpu.VMEM),
            pl.BlockSpec(memory_space=pltpu.VMEM),
            pl.BlockSpec(memory_space=pltpu.VMEM),
        ],
        out_specs=pl.BlockSpec(memory_space=pltpu.VMEM),
        out_shape=jax.ShapeDtypeStruct((128, 2048), BF16),
        compiler_params=pltpu.CompilerParams(vmem_limit_bytes=VMEM_LIMIT),
        cost_estimate=pl.CostEstimate(
            flops=2 * 32 * 128 * 256 * 128, bytes_accessed=1_500_000, transcendentals=1_000_000
        ),
        name="attend",
    )(index, sinks, query, own, halo)


def body(
    tokens,
    route_ids,
    route_level,
    gate_up_codes,
    gate_up_scale,
    gate_up_bias,
    down_codes,
    down_scale,
    down_bias,
    attn_gain,
    query_weight,
    key_matrix,
    value_matrix,
    sinks,
):
    own_tokens, width = tokens.shape
    group_size = lax.axis_size("expert")
    far = group_size // 4
    device_index = lax.axis_index("expert")
    core = device_index % 2

    partner = [(i, i ^ 1) for i in range(group_size)]

    def swap(block):
        return lax.ppermute(block, "expert", partner)

    def inward(block, across):
        route = []
        for i in range(group_size):
            goal = (i + (-2 if i % 2 else 2)) % group_size
            route.append((i ^ 1 if across else i, goal))
        return lax.ppermute(block, "expert", route)

    packed = pack(tokens, route_ids, route_level)

    second = decode_down(down_codes[0], down_scale[0])
    first, first_bias = decode_up(gate_up_codes[0], gate_up_scale[0], gate_up_bias)
    second_bias = jnp.pad(down_bias.astype(F32), ((0, 0), (0, WIDE - width)))
    experts = jnp.stack([device_index, device_index + 1 - 2 * core]).astype(jnp.int32)

    def serve(blocks, after):
        return run_experts(
            blocks + [swap(block) for block in blocks],
            relay(experts, after),
            first,
            second,
            first_bias,
            second_bias,
        )

    def gather(served):
        rows, given, weight = served
        return combine(weight, rows, swap(given))

    same = [packed, inward(packed, False)]
    cross = [packed, inward(packed, True)]
    same[1] = relay(same[1], second)
    same.append(inward(same[1], False))
    cross.append(inward(cross[1], False))
    same[2] = relay(same[2], first)
    same.append(inward(same[2], False))
    cross.append(inward(cross[2], False))
    served_near = serve([same[1], cross[1], packed], packed)
    same[3] = relay(same[3], served_near)
    same.append(inward(same[3], False))
    served_middle = serve([same[2], cross[2]], served_near)
    same[far] = relay(same[far], served_middle)
    served_far = serve([same[far], same[far - 1], cross[far - 1]], served_middle)
    same_far, same_third, cross_third = gather(served_far)
    same_near = [None, None, None]
    cross_near = [None, None, None]
    same_near[2], cross_near[2] = gather(relay(served_middle, same_far))
    same_near[1], cross_near[1], own = gather(relay(served_near, same_far))

    half_dim = HEAD_SIZE // 2
    frequency = jnp.power(
        jnp.float32(150000.0), -2.0 * jnp.arange(half_dim, dtype=F32) / (2 * half_dim)
    )
    token_positions = device_index * own_tokens + jnp.arange(own_tokens, dtype=jnp.int32)
    angles = token_positions.astype(F32)[:, None] * frequency[None, :]
    cosine = jnp.tile(jnp.cos(angles), (1, 4))
    sine_part = jnp.sin(angles)
    sine_part = jnp.concatenate([-sine_part, sine_part, -sine_part, sine_part], axis=1)

    def onward(block, across):
        route = []
        for i in range(group_size):
            goal = (i + (2 if i % 2 else -2)) % group_size
            route.append((i, goal ^ 1 if across else goal))
        return lax.ppermute(block.astype(jnp.float16), "expert", route).astype(F32)

    from_same = onward(same_far, False)
    from_cross = onward(cross_third, False)
    from_same = onward(same_third + from_same, False)
    from_same = onward(same_near[2] + from_same, False)
    from_cross = onward(cross_near[2] + from_cross, False)
    from_same = onward(same_near[1] + from_same, False)
    from_cross = onward(cross_near[1] + from_cross, True)
    mixture = (own + from_same + from_cross)[:, :width] * (1.0 / RETURN_SCALE)

    block_out, normed, own_kv = mix(
        packed, mixture, attn_gain[None], key_matrix, value_matrix, cosine, sine_part
    )
    ahead = [(i, i + 1) for i in range(group_size - 1)]
    halo_kv = lax.ppermute(own_kv, "expert", ahead)
    query = queries(normed, query_weight, cosine, sine_part)
    attended = attend(device_index.reshape(1), sinks, query, own_kv, halo_kv)
    return (block_out, attended)


def solution(mesh):
    in_specs = (
        P(("dp", "expert"), None),
        P(("dp", "expert"), None),
        P(("dp", "expert"), None),
        P("expert", None, None),
        P("expert", None, None),
        P("expert", None),
        P("expert", None, None),
        P("expert", None, None),
        P("expert", None),
        P(),
        P(),
        P(),
        P(),
        P(),
    )
    out_specs = (P(("dp", "expert"), None), P(("dp", "expert"), None))
    return jax.shard_map(body, mesh=mesh, in_specs=in_specs, out_specs=out_specs, check_vma=False)
```

time: 175 us -> 132 us (0.75)
  Pallas kernels: 79.5 us -> 54.2 us
  starting transfers between devices: 6.62 us -> 23.5 us
  waiting for transfers between devices: 43.8 us -> 28.2 us
  between operations: 14.4 us -> 0.93 us
  other arithmetic: 8.61 us -> 5.53 us
  local copies, waits for them, and re-layouts: 20.5 us -> 17.8 us
    all_gather x1 -> x0, waiting for transfers between devices: 22.1 us -> none  [body(): gathered = lax.all_gather(packed, 'expert', axis=0, tiled=True)]
    ppermute x2 -> x18, starting transfers between devices: 1.48 us -> 17.6 us  [the longest x7 12 us: inward(): return lax.ppermute(block, 'expert', route)]
    pallas_call x3 -> x4, Pallas kernels: 24.8 us -> 11.4 us  [the longest x1 10.1 us: decode_up(): pl.pallas_call(decode_up_kernel, grid=(CHUNKS,), in_specs=[pl.BlockSpec((...]
    unnamed x23 -> x39, local copies, waits for them, and re-layouts: 10.1 us -> 17.7 us
    ppermute x5 -> x7, waiting for transfers between devices: 20.6 us -> 25.2 us  [onward(): return lax.ppermute(block.astype(jnp.float16), 'expert', route).astype(F32)]
    another operation x5 -> x1, other arithmetic: 4.15 us -> 0.07 us  [body(): jnp.stack([device_index, device_index + 1 - 2 * core]).astype(jnp.int32)]
    slice x4 -> x0, local copies, waits for them, and re-layouts: 3.18 us -> none  [the longest x1 2.08 us: body(): moving = late[here:here + 2].reshape(2 * own_tokens, WIDE) + moving]
    pallas_call x1, Pallas kernels: 5.37 us -> 2.73 us  [queries(): pl.pallas_call(queries_kernel, grid=(4,), in_specs=[pl.BlockSpec((128, 14...]
  transfers between devices with their start and end apart: 9 -> 26, of which waited for: 7 -> 9; matrix products, arithmetic and copies ran while one was open for 10% -> 6% of each run, Pallas kernels for 30% -> 29%
where the time goes in v1:
time: 132 us; the launch traced here: 130 us
  Pallas kernels  54.2 us (41%)
  waiting for transfers between devices  28.2 us (21%)
  starting transfers between devices  23.5 us (18%)
  local copies, waits for them, and re-layouts  17.8 us (13%)
  other arithmetic  5.53 us (4%)
    pallas_call x3, Pallas kernels, run_experts(): pl.pallas_call(functools.partial(expert_kernel, count), grid_spec=pltpu.P...  29.5 us
    ppermute x7, waiting for transfers between devices, onward(): return lax.ppermute(block.astype(jnp.float16), 'expert', route).astype(F32)  25.2 us
    unnamed x39, local copies, waits for them, and re-layouts  17.7 us
    ppermute x7, starting transfers between devices, inward(): return lax.ppermute(block, 'expert', route)  12 us
    pallas_call x1, Pallas kernels, decode_up(): pl.pallas_call(decode_up_kernel, grid=(CHUNKS,), in_specs=[pl.BlockSpec((...  10.1 us
    ppermute x11, starting transfers between devices, swap(): return lax.ppermute(block, 'expert', partner)  5.66 us
    pallas_call x1, Pallas kernels, decode_down(): pl.pallas_call(decode_down_kernel, grid=(CHUNKS,), in_specs=[pl.BlockSpec...  5.55 us
    pallas_call x1, Pallas kernels, attend(): pl.pallas_call(attend_kernel, in_specs=[pl.BlockSpec(memory_space=pltpu.S...  4.08 us
  transfers between devices with their start and end apart: 26, of which 9 were waited for; matrix products, arithmetic and copies ran while one was open for 6% of the time, Pallas kernels for 29%

profile of v1, /device:TPU:1, one launch (start us, length us, event | category | flops | bytes accessed | tf_op | source)
XLA Modules:
  0.0 130.2 jit_solution(2792207932564785491)
XLA Ops:
  0.6 1.0 copy-done.6
  1.6 0.7 copy-done.9
  2.3 0.7 copy-done.10
  3.0 0.2 pack.1.refs_2_.tokens_ref
  3.2 6.5 %collective-permute-start = (bf16[128,1536]{1,0:T(8,128)(2,1)S(1)}, bf16[128,1536]{1,0:T(8,128)(2,1)S(1)}, u32[]{:S(2)}, u32[]{:S(2)}) collective-permute-start(bf16[128,1536]{1,0:T(8,128)(2,1)S(1)} %pack.1.refs_2_.tokens_ref), channel_id=1, source_target_pairs={{0,2},{1,15},{2,4},{3,1},{4,6},{5,3},{6,8},{7,5},{8,10},{9,7},{10,... | collective-permute-start | bytes 1179656 | tf_op jit(solution)/shard_map/ppermute | solution.py:499
  9.7 1.0 copy.31
  10.7 1.6 %copy-done = s32[1,1440,360]{2,1,0:T(8,128)S(1)} copy-done((s32[1,1440,360]{2,1,0:T(8,128)S(1)}, s32[1,1440,360]{2,1,0:T(8,128)}, u32[]{:S(2)}) %copy-start) | copy-done | bytes 2073624
  12.3 5.6 %decode_down.1.refs_7_.refs_5_ = bf16[3,512,1536]{2,1,0:T(8,128)(2,1)S(1)} custom-call(s32[1440,360]{1,0:T(8,128)S(1)} %bitcast.14, s32[1440,360]{1,0:T(8,128)S(1)} %bitcast.15, s32[1440,360]{1,0:T(8,128)S(1)} %bitcast.16, s32[45,1440]{1,0:T(8,128)S(1)} %bitcast.17, s32[45,1440]{1,0:T(8,128)S(1)} %bitcast.18, s32[45,1440]{1,0:T(8,128)S(1)} %bitcast.19), custom_call_target="tpu_custom_call" | custom-call | flops 60000000 | bytes 20000000 | tf_op jit(solution)/shard_map/decode_down/pallas_call | solution.py:124
  17.9 2.2 %copy-done.2 = bf16[3,512,1536]{2,1,0:T(8,128)(2,1)} copy-done((bf16[3,512,1536]{2,1,0:T(8,128)(2,1)}, bf16[3,512,1536]{2,1,0:T(8,128)(2,1)S(1)}, u32[]{:S(2)}) %copy-start.2) | copy-done | bytes 4718616
  20.1 0.7 collective-permute-start.5
  20.8 1.4 %collective-permute-start.4 = (bf16[128,1536]{1,0:T(8,128)(2,1)S(1)}, bf16[128,1536]{1,0:T(8,128)(2,1)S(1)}, u32[]{:S(2)}, u32[]{:S(2)}) collective-permute-start(bf16[128,1536]{1,0:T(8,128)(2,1)S(1)} %pack.1.refs_2_.tokens_ref), channel_id=1, source_target_pairs={{0,1},{1,0},{2,3},{3,2},{4,5},{5,4},{6,7},{7,6},{8,9},{9,8},{10,11... | collective-permute-start | bytes 1179656 | tf_op jit(solution)/shard_map/ppermute | solution.py:492
  22.3 1.9 %collective-permute-start.6 = (bf16[128,1536]{1,0:T(8,128)(2,1)S(1)}, bf16[128,1536]{1,0:T(8,128)(2,1)S(1)}, u32[]{:S(2)}, u32[]{:S(2)}) collective-permute-start(bf16[128,1536]{1,0:T(8,128)(2,1)S(1)} %collective-permute-done.1.refs_1_), channel_id=1, source_target_pairs={{0,2},{1,15},{2,4},{3,1},{4,6},{5,3},{6,8},{7,5},{8,10},{9,7},{10,... | collective-permute-start | bytes 1179656 | tf_op jit(solution)/shard_map/ppermute | solution.py:499
  24.2 0.5 collective-permute-start.3
  24.8 2.1 %copy.30 = s32[1,45,2880]{2,1,0:T(8,128)} copy(s32[1,45,2880]{2,0,1:T(1,128)} %param.18) | data formatting | bytes 1036800
  26.8 10.1 %decode_up.1 = (bf16[3,1440,1024]{2,1,0:T(8,128)(2,1)}, f32[3,1,1024]{2,1,0:T(1,128)}) custom-call(s32[1440,720]{1,0:T(8,128)} %bitcast.23, s32[45,2880]{1,0:T(8,128)} %bitcast.24, bf16[1,2880]{1,0:T(2,128)(2,1)} %bias_ref.1), custom_call_target="tpu_custom_call" | custom-call | flops 60000000 | bytes 30000000 | tf_op jit(solution)/shard_map/decode_up/pallas_call | solution.py:69
  37.0 0.6 collective-permute-start.9
  37.6 0.5 collective-permute-start.8
  38.1 2.2 %collective-permute-start.11 = (bf16[128,1536]{1,0:T(8,128)(2,1)S(1)}, bf16[128,1536]{1,0:T(8,128)(2,1)S(1)}, u32[]{:S(2)}, u32[]{:S(2)}) collective-permute-start(bf16[128,1536]{1,0:T(8,128)(2,1)S(1)} %collective-permute-done.6.refs_1_), channel_id=1, source_target_pairs={{0,2},{1,15},{2,4},{3,1},{4,6},{5,3},{6,8},{7,5},{8,10},{9,7},{10,... | collective-permute-start | bytes 1179656 | tf_op jit(solution)/shard_map/ppermute | solution.py:499
  40.3 0.7 copy-done.12
  41.0 1.0 copy-done.13
  42.0 0.7 copy-done.14
  42.7 10.6 %experts.3 = (bf16[192,1536]{1,0:T(8,128)(2,1)S(1)}, bf16[192,1536]{1,0:T(8,128)(2,1)S(1)}, bf16[3,128,256]{2,1,0:T(8,128)(2,1)S(1)}) custom-call(s32[2]{0:T(128)S(1)} %pad_add_fusion.place_ref, bf16[128,1536]{1,0:T(8,128)(2,1)S(1)} %collective-permute-done.refs_0_, bf16[128,1536]{1,0:T(8,128)(2,1)S(1)} %collective-permute-done.1.refs_1_, ...), custom_call_target="tpu_custom_call" | custom-call | flops 9555148800 | bytes 30000000 | tf_op jit(solution)/shard_map/experts/pallas_call | solution.py:268
  53.4 0.8 copy-done.11
  54.2 1.3 collective-permute-start.13
  55.5 8.3 %experts.4 = (bf16[128,1536]{1,0:T(8,128)(2,1)S(1)}, bf16[128,1536]{1,0:T(8,128)(2,1)S(1)}, bf16[2,128,256]{2,1,0:T(8,128)(2,1)S(1)}) custom-call(s32[2]{0:T(128)S(1)} %pad_add_fusion.place_ref, bf16[128,1536]{1,0:T(8,128)(2,1)S(1)} %collective-permute-done.5.refs_0_, bf16[128,1536]{1,0:T(8,128)(2,1)S(1)} %collective-permute-done.6.refs_1_, ...), custom_call_target="tpu_custom_call" | custom-call | flops 6370099200 | bytes 30000000 | tf_op jit(solution)/shard_map/experts/pallas_call | solution.py:268
  63.8 0.6 copy-done.7
  64.5 0.5 collective-permute-start.12
  65.0 1.3 %collective-permute-done.12.refs_3_ = bf16[128,1536]{1,0:T(8,128)(2,1)S(1)} collective-permute-done((bf16[128,1536]{1,0:T(8,128)(2,1)S(1)}, bf16[128,1536]{1,0:T(8,128)(2,1)S(1)}, u32[]{:S(2)}, u32[]{:S(2)}) %collective-permute-start.12) | collective-permute-done | bytes 393248 | tf_op jit(solution)/shard_map/ppermute | solution.py:492
  66.3 10.6 %experts.5 = (bf16[192,1536]{1,0:T(8,128)(2,1)S(1)}, bf16[192,1536]{1,0:T(8,128)(2,1)S(1)}, bf16[3,128,256]{2,1,0:T(8,128)(2,1)S(1)}) custom-call(s32[2]{0:T(128)S(1)} %pad_add_fusion.place_ref, bf16[128,1536]{1,0:T(8,128)(2,1)S(1)} %collective-permute-done.10.refs_0_, bf16[128,1536]{1,0:T(8,128)(2,1)S(1)} %collective-permute-done.9.refs_1_, ...), custom_call_target="tpu_custom_call" | custom-call | flops 9555148800 | bytes 30000000 | tf_op jit(solution)/shard_map/experts/pallas_call | solution.py:268
  76.9 0.5 collective-permute-start.15
  77.4 1.6 %collective-permute-done.15.other_ref = bf16[192,1536]{1,0:T(8,128)(2,1)S(1)} collective-permute-done((bf16[192,1536]{1,0:T(8,128)(2,1)S(1)}, bf16[192,1536]{1,0:T(8,128)(2,1)S(1)}, u32[]{:S(2)}, u32[]{:S(2)}) %collective-permute-start.15) | collective-permute-done | bytes 589856 | tf_op jit(solution)/shard_map/ppermute | solution.py:492
  79.0 0.5 combine.3
  79.5 0.8 convert_element_type.52
  80.3 1.0 collective-permute-start.18
  81.3 0.9 collective-permute-start.17
  82.4 0.7 collective-permute-start.22
  83.1 5.3 %collective-permute-done.18 = f16[128,1536]{1,0:T(8,128)(2,1)} collective-permute-done((f16[128,1536]{1,0:T(8,128)(2,1)}, f16[128,1536]{1,0:T(8,128)(2,1)}, u32[]{:S(2)}, u32[]{:S(2)}) %collective-permute-start.18) | collective-permute-done | bytes 393248 | tf_op jit(solution)/shard_map/ppermute | solution.py:557
  88.5 1.1 add_convert_fusion.4
  89.6 0.2 collective-permute-start.19
  89.7 0.9 copy-done.8
  90.6 0.4 combine.5
  91.0 1.5 %collective-permute-done.22 = f16[128,1536]{1,0:T(8,128)(2,1)S(1)} collective-permute-done((f16[128,1536]{1,0:T(8,128)(2,1)S(1)}, f16[128,1536]{1,0:T(8,128)(2,1)S(1)}, u32[]{:S(2)}, u32[]{:S(2)}) %collective-permute-start.22) | collective-permute-done | bytes 393248 | tf_op jit(solution)/shard_map/ppermute | solution.py:557
  92.6 0.1 add_convert_fusion.1
  92.7 0.2 collective-permute-start.23
  92.9 0.5 combine.4
  93.3 4.1 %collective-permute-done.19 = f16[128,1536]{1,0:T(8,128)(2,1)S(1)} collective-permute-done((f16[128,1536]{1,0:T(8,128)(2,1)S(1)}, f16[128,1536]{1,0:T(8,128)(2,1)S(1)}, u32[]{:S(2)}, u32[]{:S(2)}) %collective-permute-start.19) | collective-permute-done | bytes 393248 | tf_op jit(solution)/shard_map/ppermute | solution.py:557
  97.5 0.1 add_convert_fusion.3
  97.7 4.0 %collective-permute-done.23 = f16[128,1536]{1,0:T(8,128)(2,1)S(1)} collective-permute-done((f16[128,1536]{1,0:T(8,128)(2,1)S(1)}, f16[128,1536]{1,0:T(8,128)(2,1)S(1)}, u32[]{:S(2)}, u32[]{:S(2)}) %collective-permute-start.23) | collective-permute-done | bytes 393248 | tf_op jit(solution)/shard_map/ppermute | solution.py:557
  101.7 0.8 add_convert_fusion
  102.5 1.1 collective-permute-start.24
  103.7 2.2 %collective-permute-done.20 = f16[128,1536]{1,0:T(8,128)(2,1)S(1)} collective-permute-done((f16[128,1536]{1,0:T(8,128)(2,1)S(1)}, f16[128,1536]{1,0:T(8,128)(2,1)S(1)}, u32[]{:S(2)}, u32[]{:S(2)}) %collective-permute-start.20) | collective-permute-done | bytes 393248 | tf_op jit(solution)/shard_map/ppermute | solution.py:557
  105.9 0.9 add_convert_fusion.2
  106.8 0.3 fusion.2
  107.2 0.1 copy.23.cos_ref
  107.3 0.1 pad_maximum_fusion.sin_ref
  107.4 2.8 %collective-permute-done.24 = f16[128,1536]{1,0:T(8,128)(2,1)S(1)} collective-permute-done((f16[128,1536]{1,0:T(8,128)(2,1)}, f16[128,1536]{1,0:T(8,128)(2,1)S(1)}, u32[]{:S(2)}, u32[]{:S(2)}) %collective-permute-start.24) | collective-permute-done | bytes 393248 | tf_op jit(solution)/shard_map/ppermute | solution.py:557
  110.2 5.1 %collective-permute-done.21 = f16[128,1536]{1,0:T(8,128)(2,1)} collective-permute-done((f16[128,1536]{1,0:T(8,128)(2,1)}, f16[128,1536]{1,0:T(8,128)(2,1)}, u32[]{:S(2)}, u32[]{:S(2)}) %collective-permute-start.21) | collective-permute-done | bytes 393248 | tf_op jit(solution)/shard_map/ppermute | solution.py:557
  115.3 1.2 fusion.1.mixture_ref
  116.6 0.6 mix.1
  117.2 2.6 %collective-permute-start.25 = (bf16[128,512]{1,0:T(8,128)(2,1)S(1)}, bf16[128,512]{1,0:T(8,128)(2,1)S(1)}, u32[]{:S(2)}, u32[]{:S(2)}) collective-permute-start(bf16[128,512]{1,0:T(8,128)(2,1)S(1)} %get-tuple-element.71.own_ref), channel_id=1, source_target_pairs={{0,1},{1,2},{2,3},{3,4},{4,5},{5,6},{6,7},{7,8},{8,9},{9,10},{10,1... | collective-permute-start | bytes 393224 | tf_op jit(solution)/shard_map/ppermute | solution.py:572
  119.8 0.9 copy.25
  120.7 2.7 %copy-done.1 = bf16[1440,2048]{1,0:T(8,128)(2,1)S(1)} copy-done((bf16[1440,2048]{1,0:T(8,128)(2,1)S(1)}, bf16[1440,2048]{1,0:T(8,128)(2,1)}, u32[]{:S(2)}) %copy-start.1) | copy-done | bytes 5898264
  123.4 2.7 %queries.1.queries_ref = bf16[4,512,128]{2,1,0:T(8,128)(2,1)S(1)} custom-call(bf16[128,1440]{1,0:T(8,128)(2,1)S(1)} %get-tuple-element.70.normed_ref, bf16[1440,2048]{1,0:T(8,128)(2,1)S(1)} %copy-done.1, f32[128,128]{1,0:T(8,128)S(1)} %copy.23.cos_ref, f32[128,128]{1,0:T(8,128)S(1)} %pad_maximum_fusion.sin_ref), custom_call_target="tpu_custom_call" | custom-call | flops 754974720 | bytes 7000000 | tf_op jit(solution)/shard_map/queries/pallas_call | solution.py:368
  126.1 4.1 %attend.1 = bf16[128,2048]{1,0:T(8,128)(2,1)} custom-call(s32[1]{0:T(128)} %bitcast.3.index_ref, f32[32]{0:T(128)S(1)} %copy-done.15, bf16[4,512,128]{2,1,0:T(8,128)(2,1)S(1)} %queries.1.queries_ref, bf16[128,512]{1,0:T(8,128)(2,1)S(1)} %get-tuple-element.71.own_ref, bf16[128,512]{1,0:T(8,128)(2,1)S(1)} %collective-permute-done.25.halo_ref), custom_call_target="tpu_custom_call" | custom-call | flops 268435456 | bytes 1500000 | tf_op jit(solution)/shard_map/attend/pallas_call | solution.py:448
  (57 shorter events, 0.5 us)
Async XLA Ops:
  0.6 1.0 copy-start.6
  1.6 0.7 copy-start.9
  2.3 0.7 copy-start.10
  3.2 16.9 %collective-permute-start = (bf16[128,1536]{1,0:T(8,128)(2,1)S(1)}, bf16[128,1536]{1,0:T(8,128)(2,1)S(1)}, u32[]{:S(2)}, u32[]{:S(2)}) collective-permute-start(bf16[128,1536]{1,0:T(8,128)(2,1)S(1)} %pack.1.refs_2_.tokens_ref), channel_id=1, source_target_pairs={{0,2},{1,15},{2,4},{3,1},{4,6},{5,3},{6,8},{7,5},{8,10},{9,7},{10,... | collective-permute-start | bytes 1179656 | tf_op jit(solution)/shard_map/ppermute | solution.py:499
  9.7 12.6 %collective-permute-start.1 = (bf16[128,1536]{1,0:T(8,128)(2,1)S(1)}, bf16[128,1536]{1,0:T(8,128)(2,1)S(1)}, u32[]{:S(2)}, u32[]{:S(2)}) collective-permute-start(bf16[128,1536]{1,0:T(8,128)(2,1)S(1)} %pack.1.refs_2_.tokens_ref), channel_id=1, source_target_pairs={{1,2},{0,15},{3,4},{2,1},{5,6},{4,3},{7,8},{6,5},{9,10},{8,7},{11,... | collective-permute-start | bytes 1179656 | tf_op jit(solution)/shard_map/ppermute | solution.py:499
  10.7 1.6 %copy-start = (s32[1,1440,360]{2,1,0:T(8,128)S(1)}, s32[1,1440,360]{2,1,0:T(8,128)}, u32[]{:S(2)}) copy-start(s32[1,1440,360]{2,1,0:T(8,128)} %param.20) | copy-start | bytes 6220804
  17.9 2.2 %copy-start.2 = (bf16[3,512,1536]{2,1,0:T(8,128)(2,1)}, bf16[3,512,1536]{2,1,0:T(8,128)(2,1)S(1)}, u32[]{:S(2)}) copy-start(bf16[3,512,1536]{2,1,0:T(8,128)(2,1)S(1)} %decode_down.1.refs_7_.refs_5_) | copy-start | bytes 14155780
  20.1 16.8 %copy-start.16 = (bf16[1,1440]{1,0:T(2,128)(2,1)S(1)}, bf16[1,1440]{1,0:T(2,128)(2,1)}, u32[]{:S(2)}) copy-start(bf16[1,1440]{1,0:T(2,128)(2,1)} %param.22) | copy-start | bytes 8644
  20.1 16.9 %collective-permute-start.5 = (bf16[128,1536]{1,0:T(8,128)(2,1)S(1)}, bf16[128,1536]{1,0:T(8,128)(2,1)S(1)}, u32[]{:S(2)}, u32[]{:S(2)}) collective-permute-start(bf16[128,1536]{1,0:T(8,128)(2,1)S(1)} %collective-permute-done.refs_0_), channel_id=1, source_target_pairs={{0,2},{1,15},{2,4},{3,1},{4,6},{5,3},{6,8},{7,5},{8,10},{9,7},{10,... | collective-permute-start | bytes 1179656 | tf_op jit(solution)/shard_map/ppermute | solution.py:499
  20.8 16.7 %collective-permute-start.4 = (bf16[128,1536]{1,0:T(8,128)(2,1)S(1)}, bf16[128,1536]{1,0:T(8,128)(2,1)S(1)}, u32[]{:S(2)}, u32[]{:S(2)}) collective-permute-start(bf16[128,1536]{1,0:T(8,128)(2,1)S(1)} %pack.1.refs_2_.tokens_ref), channel_id=1, source_target_pairs={{0,1},{1,0},{2,3},{3,2},{4,5},{5,4},{6,7},{7,6},{8,9},{9,8},{10,11... | collective-permute-start | bytes 1179656 | tf_op jit(solution)/shard_map/ppermute | solution.py:492
  22.3 15.3 %collective-permute-start.6 = (bf16[128,1536]{1,0:T(8,128)(2,1)S(1)}, bf16[128,1536]{1,0:T(8,128)(2,1)S(1)}, u32[]{:S(2)}, u32[]{:S(2)}) collective-permute-start(bf16[128,1536]{1,0:T(8,128)(2,1)S(1)} %collective-permute-done.1.refs_1_), channel_id=1, source_target_pairs={{0,2},{1,15},{2,4},{3,1},{4,6},{5,3},{6,8},{7,5},{8,10},{9,7},{10,... | collective-permute-start | bytes 1179656 | tf_op jit(solution)/shard_map/ppermute | solution.py:499
  24.2 13.9 %collective-permute-start.2 = (bf16[128,1536]{1,0:T(8,128)(2,1)S(1)}, bf16[128,1536]{1,0:T(8,128)(2,1)S(1)}, u32[]{:S(2)}, u32[]{:S(2)}) collective-permute-start(bf16[128,1536]{1,0:T(8,128)(2,1)S(1)} %collective-permute-done.refs_0_), channel_id=1, source_target_pairs={{0,1},{1,0},{2,3},{3,2},{4,5},{5,4},{6,7},{7,6},{8,9},{9,8},{10,11... | collective-permute-start | bytes 1179656 | tf_op jit(solution)/shard_map/ppermute | solution.py:492
  24.2 16.1 %collective-permute-start.3 = (bf16[128,1536]{1,0:T(8,128)(2,1)S(1)}, bf16[128,1536]{1,0:T(8,128)(2,1)S(1)}, u32[]{:S(2)}, u32[]{:S(2)}) collective-permute-start(bf16[128,1536]{1,0:T(8,128)(2,1)S(1)} %collective-permute-done.1.refs_1_), channel_id=1, source_target_pairs={{0,1},{1,0},{2,3},{3,2},{4,5},{5,4},{6,7},{7,6},{8,9},{9,8},{10,11... | collective-permute-start | bytes 1179656 | tf_op jit(solution)/shard_map/ppermute | solution.py:492
  24.7 16.3 %copy-start.3 = (bf16[3,512,1536]{2,1,0:T(8,128)(2,1)S(1)}, bf16[3,512,1536]{2,1,0:T(8,128)(2,1)}, u32[]{:S(2)}) copy-start(bf16[3,512,1536]{2,1,0:T(8,128)(2,1)} %copy-done.2) | copy-start | bytes 14155780
  37.0 17.2 %collective-permute-start.9 = (bf16[128,1536]{1,0:T(8,128)(2,1)S(1)}, bf16[128,1536]{1,0:T(8,128)(2,1)S(1)}, u32[]{:S(2)}, u32[]{:S(2)}) collective-permute-start(bf16[128,1536]{1,0:T(8,128)(2,1)S(1)} %collective-permute-done.5.refs_0_), channel_id=1, source_target_pairs={{0,2},{1,15},{2,4},{3,1},{4,6},{5,3},{6,8},{7,5},{8,10},{9,7},{10,... | collective-permute-start | bytes 1179656 | tf_op jit(solution)/shard_map/ppermute | solution.py:499
  37.6 17.9 %collective-permute-start.7 = (bf16[128,1536]{1,0:T(8,128)(2,1)S(1)}, bf16[128,1536]{1,0:T(8,128)(2,1)S(1)}, u32[]{:S(2)}, u32[]{:S(2)}) collective-permute-start(bf16[128,1536]{1,0:T(8,128)(2,1)S(1)} %collective-permute-done.5.refs_0_), channel_id=1, source_target_pairs={{0,1},{1,0},{2,3},{3,2},{4,5},{5,4},{6,7},{7,6},{8,9},{9,8},{10,11... | collective-permute-start | bytes 1179656 | tf_op jit(solution)/shard_map/ppermute | solution.py:492
  37.6 17.9 %collective-permute-start.8 = (bf16[128,1536]{1,0:T(8,128)(2,1)S(1)}, bf16[128,1536]{1,0:T(8,128)(2,1)S(1)}, u32[]{:S(2)}, u32[]{:S(2)}) collective-permute-start(bf16[128,1536]{1,0:T(8,128)(2,1)S(1)} %collective-permute-done.6.refs_1_), channel_id=1, source_target_pairs={{0,1},{1,0},{2,3},{3,2},{4,5},{5,4},{6,7},{7,6},{8,9},{9,8},{10,11... | collective-permute-start | bytes 1179656 | tf_op jit(solution)/shard_map/ppermute | solution.py:492
  38.1 17.4 %collective-permute-start.11 = (bf16[128,1536]{1,0:T(8,128)(2,1)S(1)}, bf16[128,1536]{1,0:T(8,128)(2,1)S(1)}, u32[]{:S(2)}, u32[]{:S(2)}) collective-permute-start(bf16[128,1536]{1,0:T(8,128)(2,1)S(1)} %collective-permute-done.6.refs_1_), channel_id=1, source_target_pairs={{0,2},{1,15},{2,4},{3,1},{4,6},{5,3},{6,8},{7,5},{8,10},{9,7},{10,... | collective-permute-start | bytes 1179656 | tf_op jit(solution)/shard_map/ppermute | solution.py:499
  40.3 0.7 copy-start.12
  41.0 1.0 copy-start.13
  42.0 0.7 copy-start.14
  53.4 0.8 copy-start.11
  54.2 10.3 %collective-permute-start.10 = (bf16[128,1536]{1,0:T(8,128)(2,1)S(1)}, bf16[128,1536]{1,0:T(8,128)(2,1)S(1)}, u32[]{:S(2)}, u32[]{:S(2)}) collective-permute-start(bf16[128,1536]{1,0:T(8,128)(2,1)S(1)} %collective-permute-done.9.refs_1_), channel_id=1, source_target_pairs={{0,2},{1,15},{2,4},{3,1},{4,6},{5,3},{6,8},{7,5},{8,10},{9,7},{10,... | collective-permute-start | bytes 1179656 | tf_op jit(solution)/shard_map/ppermute | solution.py:499
  54.2 10.7 %collective-permute-start.13 = (bf16[128,1536]{1,0:T(8,128)(2,1)S(1)}, bf16[128,1536]{1,0:T(8,128)(2,1)S(1)}, u32[]{:S(2)}, u32[]{:S(2)}) collective-permute-start(bf16[128,1536]{1,0:T(8,128)(2,1)S(1)} %collective-permute-done.9.refs_1_), channel_id=1, source_target_pairs={{0,1},{1,0},{2,3},{3,2},{4,5},{5,4},{6,7},{7,6},{8,9},{9,8},{10,11... | collective-permute-start | bytes 1179656 | tf_op jit(solution)/shard_map/ppermute | solution.py:492
  55.5 9.5 %collective-permute-start.14 = (bf16[128,1536]{1,0:T(8,128)(2,1)S(1)}, bf16[128,1536]{1,0:T(8,128)(2,1)S(1)}, u32[]{:S(2)}, u32[]{:S(2)}) collective-permute-start(bf16[128,1536]{1,0:T(8,128)(2,1)S(1)} %collective-permute-done.11.refs_2_), channel_id=1, source_target_pairs={{0,1},{1,0},{2,3},{3,2},{4,5},{5,4},{6,7},{7,6},{8,9},{9,8},{10,11... | collective-permute-start | bytes 1179656 | tf_op jit(solution)/shard_map/ppermute | solution.py:492
  63.8 0.7 copy-start.7
  64.5 1.8 %collective-permute-start.12 = (bf16[128,1536]{1,0:T(8,128)(2,1)S(1)}, bf16[128,1536]{1,0:T(8,128)(2,1)S(1)}, u32[]{:S(2)}, u32[]{:S(2)}) collective-permute-start(bf16[128,1536]{1,0:T(8,128)(2,1)S(1)} %collective-permute-done.10.refs_0_), channel_id=1, source_target_pairs={{0,1},{1,0},{2,3},{3,2},{4,5},{5,4},{6,7},{7,6},{8,9},{9,8},{10,11... | collective-permute-start | bytes 1179656 | tf_op jit(solution)/shard_map/ppermute | solution.py:492
  76.9 2.1 %collective-permute-start.15 = (bf16[192,1536]{1,0:T(8,128)(2,1)S(1)}, bf16[192,1536]{1,0:T(8,128)(2,1)S(1)}, u32[]{:S(2)}, u32[]{:S(2)}) collective-permute-start(bf16[192,1536]{1,0:T(8,128)(2,1)S(1)} %get-tuple-element.54), channel_id=1, source_target_pairs={{0,1},{1,0},{2,3},{3,2},{4,5},{5,4},{6,7},{7,6},{8,9},{9,8},{10,11... | collective-permute-start | bytes 1769480 | tf_op jit(solution)/shard_map/ppermute | solution.py:492
  80.3 8.2 %collective-permute-start.18 = (f16[128,1536]{1,0:T(8,128)(2,1)}, f16[128,1536]{1,0:T(8,128)(2,1)}, u32[]{:S(2)}, u32[]{:S(2)}) collective-permute-start(f16[128,1536]{1,0:T(8,128)(2,1)} %convert_element_type.52), channel_id=1, source_target_pairs={{0,14},{1,3},{2,0},{3,5},{4,2},{5,7},{6,4},{7,9},{8,6},{9,11},{10,... | collective-permute-start | bytes 1179656 | tf_op jit(solution)/shard_map/ppermute | solution.py:557
  81.3 8.4 %collective-permute-start.17 = (bf16[128,1536]{1,0:T(8,128)(2,1)S(1)}, bf16[128,1536]{1,0:T(8,128)(2,1)S(1)}, u32[]{:S(2)}, u32[]{:S(2)}) collective-permute-start(bf16[128,1536]{1,0:T(8,128)(2,1)S(1)} %get-tuple-element.63), channel_id=1, source_target_pairs={{0,1},{1,0},{2,3},{3,2},{4,5},{5,4},{6,7},{7,6},{8,9},{9,8},{10,11... | collective-permute-start | bytes 1179656 | tf_op jit(solution)/shard_map/ppermute | solution.py:492
  82.3 10.6 %collective-permute-start.16 = (bf16[192,1536]{1,0:T(8,128)(2,1)}, bf16[192,1536]{1,0:T(8,128)(2,1)S(1)}, u32[]{:S(2)}, u32[]{:S(2)}) collective-permute-start(bf16[192,1536]{1,0:T(8,128)(2,1)} %copy-done.11), channel_id=1, source_target_pairs={{0,1},{1,0},{2,3},{3,2},{4,5},{5,4},{6,7},{7,6},{8,9},{9,8},{10,11... | collective-permute-start | bytes 1769480 | tf_op jit(solution)/shard_map/ppermute | solution.py:492
  82.4 10.2 %collective-permute-start.22 = (f16[128,1536]{1,0:T(8,128)(2,1)S(1)}, f16[128,1536]{1,0:T(8,128)(2,1)S(1)}, u32[]{:S(2)}, u32[]{:S(2)}) collective-permute-start(f16[128,1536]{1,0:T(8,128)(2,1)S(1)} %convert_element_type.60), channel_id=1, source_target_pairs={{0,14},{1,3},{2,0},{3,5},{4,2},{5,7},{6,4},{7,9},{8,6},{9,11},{10,... | collective-permute-start | bytes 1179656 | tf_op jit(solution)/shard_map/ppermute | solution.py:557
  88.5 18.8 %copy-start.17 = (bf16[1440]{0:T(1024)(128)(2,1)S(1)}, bf16[1440]{0:T(1024)(128)(2,1)}, u32[]{:S(2)}) copy-start(bf16[1440]{0:T(1024)(128)(2,1)} %param.23) | copy-start | bytes 8644
  89.6 7.9 %collective-permute-start.19 = (f16[128,1536]{1,0:T(8,128)(2,1)S(1)}, f16[128,1536]{1,0:T(8,128)(2,1)S(1)}, u32[]{:S(2)}, u32[]{:S(2)}) collective-permute-start(f16[128,1536]{1,0:T(8,128)(2,1)S(1)} %add_convert_fusion.4), channel_id=1, source_target_pairs={{0,14},{1,3},{2,0},{3,5},{4,2},{5,7},{6,4},{7,9},{8,6},{9,11},{10,... | collective-permute-start | bytes 1179656 | tf_op jit(solution)/shard_map/ppermute | solution.py:557
  89.7 0.9 copy-start.8
  92.7 23.9 %copy-start.4 = (bf16[1440,256]{1,0:T(8,128)(2,1)S(1)}, bf16[1440,256]{1,0:T(8,128)(2,1)}, u32[]{:S(2)}) copy-start(bf16[1440,256]{1,0:T(8,128)(2,1)} %key_ref.1) | copy-start | bytes 2211844
  92.7 23.9 %copy-start.5 = (bf16[1440,256]{1,0:T(8,128)(2,1)S(1)}, bf16[1440,256]{1,0:T(8,128)(2,1)}, u32[]{:S(2)}) copy-start(bf16[1440,256]{1,0:T(8,128)(2,1)} %value_ref.1) | copy-start | bytes 2211844
  92.7 9.0 %collective-permute-start.23 = (f16[128,1536]{1,0:T(8,128)(2,1)S(1)}, f16[128,1536]{1,0:T(8,128)(2,1)S(1)}, u32[]{:S(2)}, u32[]{:S(2)}) collective-permute-start(f16[128,1536]{1,0:T(8,128)(2,1)S(1)} %add_convert_fusion.1), channel_id=1, source_target_pairs={{0,14},{1,3},{2,0},{3,5},{4,2},{5,7},{6,4},{7,9},{8,6},{9,11},{10,... | collective-permute-start | bytes 1179656 | tf_op jit(solution)/shard_map/ppermute | solution.py:557
  97.6 8.3 %collective-permute-start.20 = (f16[128,1536]{1,0:T(8,128)(2,1)S(1)}, f16[128,1536]{1,0:T(8,128)(2,1)S(1)}, u32[]{:S(2)}, u32[]{:S(2)}) collective-permute-start(f16[128,1536]{1,0:T(8,128)(2,1)S(1)} %add_convert_fusion.3), channel_id=1, source_target_pairs={{0,14},{1,3},{2,0},{3,5},{4,2},{5,7},{6,4},{7,9},{8,6},{9,11},{10,... | collective-permute-start | bytes 1179656 | tf_op jit(solution)/shard_map/ppermute | solution.py:557
  102.5 7.7 %collective-permute-start.24 = (f16[128,1536]{1,0:T(8,128)(2,1)}, f16[128,1536]{1,0:T(8,128)(2,1)S(1)}, u32[]{:S(2)}, u32[]{:S(2)}) collective-permute-start(f16[128,1536]{1,0:T(8,128)(2,1)} %add_convert_fusion), channel_id=1, source_target_pairs={{0,15},{1,2},{2,1},{3,4},{4,3},{5,6},{6,5},{7,8},{8,7},{9,10},{10,... | collective-permute-start | bytes 1179656 | tf_op jit(solution)/shard_map/ppermute | solution.py:557
  106.8 8.6 %collective-permute-start.21 = (f16[128,1536]{1,0:T(8,128)(2,1)}, f16[128,1536]{1,0:T(8,128)(2,1)}, u32[]{:S(2)}, u32[]{:S(2)}) collective-permute-start(f16[128,1536]{1,0:T(8,128)(2,1)} %add_convert_fusion.2), channel_id=1, source_target_pairs={{0,14},{1,3},{2,0},{3,5},{4,2},{5,7},{6,4},{7,9},{8,6},{9,11},{10,... | collective-permute-start | bytes 1179656 | tf_op jit(solution)/shard_map/ppermute | solution.py:557
  116.5 9.6 %copy-start.15 = (f32[32]{0:T(128)S(1)}, f32[32]{0:T(128)}, u32[]{:S(2)}) copy-start(f32[32]{0:T(128)} %sinks_ref.1) | copy-start | bytes 388
  117.2 8.9 %collective-permute-start.25 = (bf16[128,512]{1,0:T(8,128)(2,1)S(1)}, bf16[128,512]{1,0:T(8,128)(2,1)S(1)}, u32[]{:S(2)}, u32[]{:S(2)}) collective-permute-start(bf16[128,512]{1,0:T(8,128)(2,1)S(1)} %get-tuple-element.71.own_ref), channel_id=1, source_target_pairs={{0,1},{1,2},{2,3},{3,4},{4,5},{5,6},{6,7},{7,8},{8,9},{9,10},{10,1... | collective-permute-start | bytes 393224 | tf_op jit(solution)/shard_map/ppermute | solution.py:572
  120.7 2.7 %copy-start.1 = (bf16[1440,2048]{1,0:T(8,128)(2,1)S(1)}, bf16[1440,2048]{1,0:T(8,128)(2,1)}, u32[]{:S(2)}) copy-start(bf16[1440,2048]{1,0:T(8,128)(2,1)} %weight_ref.1) | copy-start | bytes 17694724

commit v2 on v1

--- a/solution.py
+++ b/solution.py
@@ -14,8 +14,8 @@
 CHUNKS = 3
 RETURN_SCALE = 8.0
 LARGE_LIMIT = 56 * 1024 * 1024
-VMEM_LIMIT = 40 * 1024 * 1024
-SMALL_LIMIT = 24 * 1024 * 1024
+VMEM_LIMIT = 22 * 1024 * 1024
+SMALL_LIMIT = 16 * 1024 * 1024
 F32 = jnp.float32
 BF16 = jnp.bfloat16
 
@@ -34,13 +34,14 @@
 
 
 def decode_up_kernel(codes_ref, exponent_ref, bias_ref, out_ref, bias_out_ref, scale_ref):
+    chunk = pl.program_id(0)
     source = lax.broadcasted_iota(jnp.int32, (512, 512), 0)
     target = lax.broadcasted_iota(jnp.int32, (512, 512), 1)
     wanted = 128 * jnp.bitwise_and(source, 3) + jnp.right_shift(source, 2)
     spread = jnp.where(target == wanted, 1.0, 0.0).astype(BF16)
     for half in range(2):
         lanes = slice(512 * half, 512 * half + 512)
-        left = 2880 - 1024 * pl.program_id(0) - 512 * half
+        left = 2880 - 1024 * chunk - 512 * half
         column = lax.broadcasted_iota(jnp.int32, (45, 512), 1)
         scale = power_of_two(exponent_ref[:, lanes], 119, column < left)
         scale = jnp.dot(scale.astype(BF16), spread, preferred_element_type=F32)
@@ -115,7 +116,7 @@
             for block in range(16):
                 scale = scales[part][block : block + 1, :]
                 row = 256 * parity + 16 * block
-                out_ref[0, row : row + 16, 512 * part : 512 * part + 512] = (
+                out_ref[pl.program_id(0), row : row + 16, 512 * part : 512 * part + 512] = (
                     natural[16 * block : 16 * block + 16] * scale
                 ).astype(BF16)
 
@@ -132,9 +133,9 @@
             pl.BlockSpec((16, 512), lambda b: (b, 1)),
             pl.BlockSpec((16, 512), lambda b: (b, 2)),
         ],
-        out_specs=pl.BlockSpec((1, 512, WIDE), lambda b: (b, 0, 0)),
+        out_specs=pl.BlockSpec(memory_space=pltpu.VMEM),
         out_shape=jax.ShapeDtypeStruct((CHUNKS, 512, WIDE), BF16),
-        compiler_params=pltpu.CompilerParams(vmem_limit_bytes=VMEM_LIMIT),
+        compiler_params=pltpu.CompilerParams(vmem_limit_bytes=SMALL_LIMIT),
         cost_estimate=pl.CostEstimate(flops=60_000_000, bytes_accessed=20_000_000, transcendentals=0),
         name="decode_down",
     )(codes, codes, codes, exponents, exponents, exponents)
@@ -176,8 +177,15 @@
 def pack(tokens, route_ids, route_level):
     return pl.pallas_call(
         pack_kernel,
+        grid=(1,),
+        in_specs=[
+            pl.BlockSpec((1440, 128), lambda i: (0, 0)),
+            pl.BlockSpec((4, 128), lambda i: (0, 0)),
+            pl.BlockSpec((4, 128), lambda i: (0, 0)),
+        ],
+        out_specs=pl.BlockSpec(memory_space=pltpu.VMEM),
         out_shape=jax.ShapeDtypeStruct((128, WIDE), BF16),
-        compiler_params=pltpu.CompilerParams(vmem_limit_bytes=VMEM_LIMIT),
+        compiler_params=pltpu.CompilerParams(vmem_limit_bytes=LARGE_LIMIT),
         name="pack",
     )(tokens.T, route_ids.T, route_level.T)
 
@@ -238,12 +246,24 @@
             )
             rows_ref[MOST * j : MOST * j + 2 * MOST, :] = rows.astype(BF16)
 
-    pre = jnp.dot(rows_ref[:, :1440], first_ref[0], preferred_element_type=F32)
-    pre = pre + first_bias_ref[chunk]
-    gate = jnp.minimum(pre[:, :512], 7.0)
-    up = jnp.clip(pre[:, 512:], -7.0, 7.0)
-    activated = ((up + 1.0) * gate * (0.5 + 0.5 * jnp.tanh(0.851 * gate))).astype(BF16)
-    product = jnp.dot(activated, second_ref[0], preferred_element_type=F32)
+    rows = rows_ref[:, :1440]
+    activated = []
+    for part in range(2):
+        pre = []
+        for start in (256 * part, 512 + 256 * part):
+            lanes = slice(start, start + 256)
+            pre.append(
+                jnp.dot(rows, first_ref[chunk, :, lanes], preferred_element_type=F32)
+                + first_bias_ref[chunk, :, lanes]
+            )
+        gate = jnp.minimum(pre[0], 7.0)
+        up = jnp.clip(pre[1], -7.0, 7.0)
+        activated.append(
+            ((up + 1.0) * gate * (0.5 + 0.5 * jnp.tanh(0.851 * gate))).astype(BF16)
+        )
+    product = jnp.dot(
+        jnp.concatenate(activated, axis=1), second_ref[chunk], preferred_element_type=F32
+    )
 
     @pl.when(chunk == 0)
     def _():
@@ -272,8 +292,8 @@
             grid=(CHUNKS,),
             in_specs=[pl.BlockSpec(memory_space=pltpu.VMEM)] * count
             + [
-                pl.BlockSpec((1, 1440, 1024), lambda b, place: (b, 0, 0)),
-                pl.BlockSpec((1, 512, WIDE), lambda b, place: (b, 0, 0)),
+                pl.BlockSpec(memory_space=pltpu.VMEM),
+                pl.BlockSpec(memory_space=pltpu.VMEM),
                 pl.BlockSpec((CHUNKS, 1, 1024), lambda b, place: (0, 0, 0)),
                 pl.BlockSpec((1, WIDE), lambda b, place: (0, 0)),
             ],
@@ -348,7 +368,7 @@
             jax.ShapeDtypeStruct((128, 1440), BF16),
             jax.ShapeDtypeStruct((128, 512), BF16),
         ],
-        compiler_params=pltpu.CompilerParams(vmem_limit_bytes=VMEM_LIMIT),
+        compiler_params=pltpu.CompilerParams(vmem_limit_bytes=SMALL_LIMIT),
         cost_estimate=pl.CostEstimate(
             flops=2 * 128 * 1440 * 512, bytes_accessed=3_000_000, transcendentals=0
         ),
@@ -376,7 +396,7 @@
         ],
         out_specs=pl.BlockSpec((1, 512, 128), lambda g: (g, 0, 0)),
         out_shape=jax.ShapeDtypeStruct((4, 512, 128), BF16),
-        compiler_params=pltpu.CompilerParams(vmem_limit_bytes=VMEM_LIMIT),
+        compiler_params=pltpu.CompilerParams(vmem_limit_bytes=SMALL_LIMIT),
         cost_estimate=pl.CostEstimate(
             flops=2 * 128 * 1440 * 2048, bytes_accessed=7_000_000, transcendentals=0
         ),
@@ -456,7 +476,7 @@
         ],
         out_specs=pl.BlockSpec(memory_space=pltpu.VMEM),
         out_shape=jax.ShapeDtypeStruct((128, 2048), BF16),
-        compiler_params=pltpu.CompilerParams(vmem_limit_bytes=VMEM_LIMIT),
+        compiler_params=pltpu.CompilerParams(vmem_limit_bytes=SMALL_LIMIT),
         cost_estimate=pl.CostEstimate(
             flops=2 * 32 * 128 * 256 * 128, bytes_accessed=1_500_000, transcendentals=1_000_000
         ),
@@ -521,10 +541,10 @@
 
     same = [packed, inward(packed, False)]
     cross = [packed, inward(packed, True)]
-    same[1] = relay(same[1], second)
+    same[1] = relay(same[1], first)
     same.append(inward(same[1], False))
     cross.append(inward(cross[1], False))
-    same[2] = relay(same[2], first)
+    same[2] = relay(same[2], second)
     same.append(inward(same[2], False))
     cross.append(inward(cross[2], False))
     served_near = serve([same[1], cross[1], packed], packed)

time: 132 us -> 121 us (0.917)
  local copies, waits for them, and re-layouts: 17.8 us -> 8.25 us
  Pallas kernels: 54.2 us -> 51.6 us
  waiting for transfers between devices: 28.2 us -> 29.6 us
    unnamed x39 -> x27, local copies, waits for them, and re-layouts: 17.7 us -> 8.08 us
    pallas_call x3, Pallas kernels: 29.5 us -> 25 us  [run_experts(): pl.pallas_call(functools.partial(expert_kernel, count), grid_spec=pltpu.P...]
    ppermute x11, starting transfers between devices: 5.66 us -> 8.13 us  [swap(): return lax.ppermute(block, 'expert', partner)]
    ppermute x7, starting transfers between devices: 12 us -> 10.1 us  [inward(): return lax.ppermute(block, 'expert', route)]
    pallas_call x1, Pallas kernels: 0.22 us -> 2.13 us  [pack(): pl.pallas_call(pack_kernel, grid=(1,), in_specs=[pl.BlockSpec((1440, 128)...]
    ppermute x7, waiting for transfers between devices: 25.2 us -> 26.6 us  [onward(): return lax.ppermute(block.astype(jnp.float16), 'expert', route).astype(F32)]
  transfers between devices with their start and end apart: 26 -> 26, of which waited for: 9 -> 9; matrix products, arithmetic and copies ran while one was open for 6% -> 6% of each run, Pallas kernels for 29% -> 30%
where the time goes in v2:
time: 121 us; the launch traced here: 119 us
  Pallas kernels  51.6 us (43%)
  waiting for transfers between devices  29.6 us (24%)
  starting transfers between devices  23.2 us (19%)
  local copies, waits for them, and re-layouts  8.25 us (7%)
  other arithmetic  5.47 us (5%)
    ppermute x7, waiting for transfers between devices, onward(): return lax.ppermute(block.astype(jnp.float16), 'expert', route).astype(F32)  26.6 us
    pallas_call x3, Pallas kernels, run_experts(): pl.pallas_call(functools.partial(expert_kernel, count), grid_spec=pltpu.P...  25 us
    pallas_call x1, Pallas kernels, decode_up(): pl.pallas_call(decode_up_kernel, grid=(CHUNKS,), in_specs=[pl.BlockSpec((...  10.1 us
    ppermute x7, starting transfers between devices, inward(): return lax.ppermute(block, 'expert', route)  10.1 us
    ppermute x11, starting transfers between devices, swap(): return lax.ppermute(block, 'expert', partner)  8.13 us
    unnamed x27, local copies, waits for them, and re-layouts  8.08 us
    pallas_call x1, Pallas kernels, decode_down(): pl.pallas_call(decode_down_kernel, grid=(CHUNKS,), in_specs=[pl.BlockSpec...  5.57 us
    pallas_call x1, Pallas kernels, attend(): pl.pallas_call(attend_kernel, in_specs=[pl.BlockSpec(memory_space=pltpu.S...  4.07 us
  transfers between devices with their start and end apart: 26, of which 9 were waited for; matrix products, arithmetic and copies ran while one was open for 6% of the time, Pallas kernels for 30%

profile of v2, /device:TPU:1, one launch (start us, length us, event | category | flops | bytes accessed | tf_op | source)
XLA Modules:
  0.0 119.1 jit_solution(15263083740361616549)
XLA Ops:
  0.6 2.1 %pack.1.refs_2_.tokens_ref = bf16[128,1536]{1,0:T(8,128)(2,1)} custom-call(bf16[1440,128]{1,0:T(8,128)(2,1)} %bitcast.22, s32[4,128]{1,0:T(4,128)} %bitcast.24, s32[4,128]{1,0:T(4,128)} %bitcast.25), custom_call_target="tpu_custom_call" | custom-call | tf_op jit(solution)/shard_map/pack/pallas_call | solution.py:178
  2.8 6.4 %collective-permute-start = (bf16[128,1536]{1,0:T(8,128)(2,1)}, bf16[128,1536]{1,0:T(8,128)(2,1)}, u32[]{:S(2)}, u32[]{:S(2)}) collective-permute-start(bf16[128,1536]{1,0:T(8,128)(2,1)} %pack.1.refs_2_.tokens_ref), channel_id=1, source_target_pairs={{0,2},{1,15},{2,4},{3,1},{4,6},{5,3},{6,8},{7,5},{8,10},{9,7},{10,... | collective-permute-start | bytes 1179656 | tf_op jit(solution)/shard_map/ppermute | solution.py:519
  9.2 1.9 %copy.30 = s32[1,45,2880]{2,1,0:T(8,128)} copy(s32[1,45,2880]{2,0,1:T(1,128)} %param.18) | data formatting | bytes 1036800
  11.1 10.1 %decode_up.1 = (bf16[3,1440,1024]{2,1,0:T(8,128)(2,1)}, f32[3,1,1024]{2,1,0:T(1,128)}) custom-call(s32[1440,720]{1,0:T(8,128)} %bitcast.20, s32[45,2880]{1,0:T(8,128)} %bitcast.21, bf16[1,2880]{1,0:T(2,128)(2,1)} %bias_ref.1), custom_call_target="tpu_custom_call" | custom-call | flops 60000000 | bytes 30000000 | tf_op jit(solution)/shard_map/decode_up/pallas_call | solution.py:70
  21.2 0.8 collective-permute-start.5
  22.0 1.4 %collective-permute-start.4 = (bf16[128,1536]{1,0:T(8,128)(2,1)S(1)}, bf16[128,1536]{1,0:T(8,128)(2,1)}, u32[]{:S(2)}, u32[]{:S(2)}) collective-permute-start(bf16[128,1536]{1,0:T(8,128)(2,1)S(1)} %copy-done.2), channel_id=1, source_target_pairs={{0,1},{1,0},{2,3},{3,2},{4,5},{5,4},{6,7},{7,6},{8,9},{9,8},{10,11... | collective-permute-start | bytes 1179656 | tf_op jit(solution)/shard_map/ppermute | solution.py:512
  23.4 1.9 %collective-permute-start.6 = (bf16[128,1536]{1,0:T(8,128)(2,1)}, bf16[128,1536]{1,0:T(8,128)(2,1)S(1)}, u32[]{:S(2)}, u32[]{:S(2)}) collective-permute-start(bf16[128,1536]{1,0:T(8,128)(2,1)} %collective-permute-done.1.refs_1_), channel_id=1, source_target_pairs={{0,2},{1,15},{2,4},{3,1},{4,6},{5,3},{6,8},{7,5},{8,10},{9,7},{10,... | collective-permute-start | bytes 1179656 | tf_op jit(solution)/shard_map/ppermute | solution.py:519
  25.4 0.5 collective-permute-start.3
  25.9 0.1 pad_add_fusion.place_ref
  26.0 1.0 copy.31
  27.0 0.0 copy-start.10
  27.0 0.0 copy-start.8
  27.0 5.6 %decode_down.1.refs_7_.refs_5_ = bf16[3,512,1536]{2,1,0:T(8,128)(2,1)S(1)} custom-call(s32[1440,360]{1,0:T(8,128)S(1)} %bitcast.14, s32[1440,360]{1,0:T(8,128)S(1)} %bitcast.15, s32[1440,360]{1,0:T(8,128)S(1)} %bitcast.16, s32[45,1440]{1,0:T(8,128)S(1)} %bitcast.17, s32[45,1440]{1,0:T(8,128)S(1)} %bitcast.18, s32[45,1440]{1,0:T(8,128)S(1)} %bitcast.19), custom_call_target="tpu_custom_call" | custom-call | flops 60000000 | bytes 20000000 | tf_op jit(solution)/shard_map/decode_down/pallas_call | solution.py:125
  32.6 0.7 collective-permute-start.9
  33.3 2.5 %collective-permute-start.8 = (bf16[128,1536]{1,0:T(8,128)(2,1)S(1)}, bf16[128,1536]{1,0:T(8,128)(2,1)S(1)}, u32[]{:S(2)}, u32[]{:S(2)}) collective-permute-start(bf16[128,1536]{1,0:T(8,128)(2,1)S(1)} %collective-permute-done.6.refs_1_), channel_id=1, source_target_pairs={{0,1},{1,0},{2,3},{3,2},{4,5},{5,4},{6,7},{7,6},{8,9},{9,8},{10,11... | collective-permute-start | bytes 1179656 | tf_op jit(solution)/shard_map/ppermute | solution.py:512
  35.8 0.1 collective-permute-start.11
  35.9 10.1 %experts.3 = (bf16[192,1536]{1,0:T(8,128)(2,1)S(1)}, bf16[192,1536]{1,0:T(8,128)(2,1)S(1)}, bf16[3,128,256]{2,1,0:T(8,128)(2,1)S(1)}) custom-call(s32[2]{0:T(128)S(1)} %pad_add_fusion.place_ref, bf16[128,1536]{1,0:T(8,128)(2,1)} %collective-permute-done.refs_0_, bf16[128,1536]{1,0:T(8,128)(2,1)} %collective-permute-done.1.refs_1_, ...), custom_call_target="tpu_custom_call" | custom-call | flops 9555148800 | bytes 30000000 | tf_op jit(solution)/shard_map/experts/pallas_call | solution.py:288
  46.1 0.8 copy-done.6
  46.9 0.2 collective-permute-start.10
  47.1 1.1 collective-permute-start.13
  48.2 6.2 %experts.4 = (bf16[128,1536]{1,0:T(8,128)(2,1)S(1)}, bf16[128,1536]{1,0:T(8,128)(2,1)S(1)}, bf16[2,128,256]{2,1,0:T(8,128)(2,1)S(1)}) custom-call(s32[2]{0:T(128)S(1)} %pad_add_fusion.place_ref, bf16[128,1536]{1,0:T(8,128)(2,1)S(1)} %collective-permute-done.5.refs_0_, bf16[128,1536]{1,0:T(8,128)(2,1)S(1)} %collective-permute-done.6.refs_1_, ...), custom_call_target="tpu_custom_call" | custom-call | flops 6370099200 | bytes 30000000 | tf_op jit(solution)/shard_map/experts/pallas_call | solution.py:288
  54.4 0.0 copy-start.7
  54.4 0.7 copy-done.7
  55.2 0.6 collective-permute-start.12
  55.8 1.3 %collective-permute-done.12.refs_3_ = bf16[128,1536]{1,0:T(8,128)(2,1)S(1)} collective-permute-done((bf16[128,1536]{1,0:T(8,128)(2,1)S(1)}, bf16[128,1536]{1,0:T(8,128)(2,1)S(1)}, u32[]{:S(2)}, u32[]{:S(2)}) %collective-permute-start.12) | collective-permute-done | bytes 393248 | tf_op jit(solution)/shard_map/ppermute | solution.py:512
  57.2 8.6 %experts.5 = (bf16[192,1536]{1,0:T(8,128)(2,1)S(1)}, bf16[192,1536]{1,0:T(8,128)(2,1)S(1)}, bf16[3,128,256]{2,1,0:T(8,128)(2,1)S(1)}) custom-call(s32[2]{0:T(128)S(1)} %pad_add_fusion.place_ref, bf16[128,1536]{1,0:T(8,128)(2,1)S(1)} %collective-permute-done.10.refs_0_, bf16[128,1536]{1,0:T(8,128)(2,1)S(1)} %collective-permute-done.9.refs_1_, ...), custom_call_target="tpu_custom_call" | custom-call | flops 9555148800 | bytes 30000000 | tf_op jit(solution)/shard_map/experts/pallas_call | solution.py:288
  65.8 0.5 collective-permute-start.15
  66.3 1.6 %collective-permute-done.15.other_ref = bf16[192,1536]{1,0:T(8,128)(2,1)S(1)} collective-permute-done((bf16[192,1536]{1,0:T(8,128)(2,1)S(1)}, bf16[192,1536]{1,0:T(8,128)(2,1)S(1)}, u32[]{:S(2)}, u32[]{:S(2)}) %collective-permute-start.15) | collective-permute-done | bytes 589856 | tf_op jit(solution)/shard_map/ppermute | solution.py:512
  67.9 0.5 combine.3
  68.4 0.8 convert_element_type.52
  69.2 1.0 collective-permute-start.18
  70.3 1.3 %collective-permute-start.17 = (bf16[128,1536]{1,0:T(8,128)(2,1)}, bf16[128,1536]{1,0:T(8,128)(2,1)S(1)}, u32[]{:S(2)}, u32[]{:S(2)}) collective-permute-start(bf16[128,1536]{1,0:T(8,128)(2,1)} %copy-done.7), channel_id=1, source_target_pairs={{0,1},{1,0},{2,3},{3,2},{4,5},{5,4},{6,7},{7,6},{8,9},{9,8},{10,11... | collective-permute-start | bytes 1179656 | tf_op jit(solution)/shard_map/ppermute | solution.py:512
  71.6 0.1 collective-permute-start.16
  71.7 0.2 collective-permute-start.22
  71.9 5.5 %collective-permute-done.18 = f16[128,1536]{1,0:T(8,128)(2,1)} collective-permute-done((f16[128,1536]{1,0:T(8,128)(2,1)}, f16[128,1536]{1,0:T(8,128)(2,1)}, u32[]{:S(2)}, u32[]{:S(2)}) %collective-permute-start.18) | collective-permute-done | bytes 393248 | tf_op jit(solution)/shard_map/ppermute | solution.py:577
  77.3 1.1 add_convert_fusion.4
  78.5 0.2 collective-permute-start.19
  78.7 0.4 combine.5
  79.0 2.4 %collective-permute-done.22 = f16[128,1536]{1,0:T(8,128)(2,1)S(1)} collective-permute-done((f16[128,1536]{1,0:T(8,128)(2,1)S(1)}, f16[128,1536]{1,0:T(8,128)(2,1)S(1)}, u32[]{:S(2)}, u32[]{:S(2)}) %collective-permute-start.22) | collective-permute-done | bytes 393248 | tf_op jit(solution)/shard_map/ppermute | solution.py:577
  81.5 0.1 add_convert_fusion.1
  81.6 0.0 copy-start.4
  81.6 0.2 collective-permute-start.23
  81.8 0.5 combine.4
  82.3 4.1 %collective-permute-done.19 = f16[128,1536]{1,0:T(8,128)(2,1)S(1)} collective-permute-done((f16[128,1536]{1,0:T(8,128)(2,1)S(1)}, f16[128,1536]{1,0:T(8,128)(2,1)S(1)}, u32[]{:S(2)}, u32[]{:S(2)}) %collective-permute-start.19) | collective-permute-done | bytes 393248 | tf_op jit(solution)/shard_map/ppermute | solution.py:577
  86.4 0.1 add_convert_fusion.3
  86.5 0.1 collective-permute-start.20
  86.6 4.0 %collective-permute-done.23 = f16[128,1536]{1,0:T(8,128)(2,1)S(1)} collective-permute-done((f16[128,1536]{1,0:T(8,128)(2,1)S(1)}, f16[128,1536]{1,0:T(8,128)(2,1)S(1)}, u32[]{:S(2)}, u32[]{:S(2)}) %collective-permute-start.23) | collective-permute-done | bytes 393248 | tf_op jit(solution)/shard_map/ppermute | solution.py:577
  90.6 0.8 add_convert_fusion
  91.4 1.2 collective-permute-start.24
  92.6 2.2 %collective-permute-done.20 = f16[128,1536]{1,0:T(8,128)(2,1)S(1)} collective-permute-done((f16[128,1536]{1,0:T(8,128)(2,1)S(1)}, f16[128,1536]{1,0:T(8,128)(2,1)S(1)}, u32[]{:S(2)}, u32[]{:S(2)}) %collective-permute-start.20) | collective-permute-done | bytes 393248 | tf_op jit(solution)/shard_map/ppermute | solution.py:577
  94.8 0.8 add_convert_fusion.2
  95.6 0.3 fusion.2
  96.0 0.1 copy.22
  96.0 0.1 copy.23.cos_ref
  96.2 0.1 pad_maximum_fusion.sin_ref
  96.3 2.8 %collective-permute-done.24 = f16[128,1536]{1,0:T(8,128)(2,1)S(1)} collective-permute-done((f16[128,1536]{1,0:T(8,128)(2,1)}, f16[128,1536]{1,0:T(8,128)(2,1)S(1)}, u32[]{:S(2)}, u32[]{:S(2)}) %collective-permute-start.24) | collective-permute-done | bytes 393248 | tf_op jit(solution)/shard_map/ppermute | solution.py:577
  99.1 5.5 %collective-permute-done.21 = f16[128,1536]{1,0:T(8,128)(2,1)} collective-permute-done((f16[128,1536]{1,0:T(8,128)(2,1)}, f16[128,1536]{1,0:T(8,128)(2,1)}, u32[]{:S(2)}, u32[]{:S(2)}) %collective-permute-start.21) | collective-permute-done | bytes 393248 | tf_op jit(solution)/shard_map/ppermute | solution.py:577
  104.7 1.1 fusion.1.mixture_ref
  105.8 0.6 mix.1
  106.5 2.2 %collective-permute-start.25 = (bf16[128,512]{1,0:T(8,128)(2,1)S(1)}, bf16[128,512]{1,0:T(8,128)(2,1)S(1)}, u32[]{:S(2)}, u32[]{:S(2)}) collective-permute-start(bf16[128,512]{1,0:T(8,128)(2,1)S(1)} %get-tuple-element.71.own_ref), channel_id=1, source_target_pairs={{0,1},{1,2},{2,3},{3,4},{4,5},{5,6},{6,7},{7,8},{8,9},{9,10},{10,1... | collective-permute-start | bytes 393224 | tf_op jit(solution)/shard_map/ppermute | solution.py:592
  108.6 0.9 copy.25
  109.6 2.7 %copy-done.1 = bf16[1440,2048]{1,0:T(8,128)(2,1)S(1)} copy-done((bf16[1440,2048]{1,0:T(8,128)(2,1)S(1)}, bf16[1440,2048]{1,0:T(8,128)(2,1)}, u32[]{:S(2)}) %copy-start.1) | copy-done | bytes 5898264
  112.3 2.7 %queries.1.queries_ref = bf16[4,512,128]{2,1,0:T(8,128)(2,1)S(1)} custom-call(bf16[128,1440]{1,0:T(8,128)(2,1)S(1)} %get-tuple-element.70.normed_ref, bf16[1440,2048]{1,0:T(8,128)(2,1)S(1)} %copy-done.1, f32[128,128]{1,0:T(8,128)S(1)} %copy.23.cos_ref, f32[128,128]{1,0:T(8,128)S(1)} %pad_maximum_fusion.sin_ref), custom_call_target="tpu_custom_call" | custom-call | flops 754974720 | bytes 7000000 | tf_op jit(solution)/shard_map/queries/pallas_call | solution.py:388
  115.0 4.1 %attend.1 = bf16[128,2048]{1,0:T(8,128)(2,1)} custom-call(s32[1]{0:T(128)} %bitcast.3.index_ref, f32[32]{0:T(128)S(1)} %copy-done.9, bf16[4,512,128]{2,1,0:T(8,128)(2,1)S(1)} %queries.1.queries_ref, bf16[128,512]{1,0:T(8,128)(2,1)S(1)} %get-tuple-element.71.own_ref, bf16[128,512]{1,0:T(8,128)(2,1)S(1)} %collective-permute-done.25.halo_ref), custom_call_target="tpu_custom_call" | custom-call | flops 268435456 | bytes 1500000 | tf_op jit(solution)/shard_map/attend/pallas_call | solution.py:468
  (45 shorter events, 0.2 us)
Async XLA Ops:
  0.6 26.3 %copy-start = (s32[1,1440,360]{2,1,0:T(8,128)S(1)}, s32[1,1440,360]{2,1,0:T(8,128)}, u32[]{:S(2)}) copy-start(s32[1,1440,360]{2,1,0:T(8,128)} %param.20) | copy-start | bytes 6220804
  2.8 19.3 %copy-start.2 = (bf16[128,1536]{1,0:T(8,128)(2,1)S(1)}, bf16[128,1536]{1,0:T(8,128)(2,1)}, u32[]{:S(2)}) copy-start(bf16[128,1536]{1,0:T(8,128)(2,1)} %pack.1.refs_2_.tokens_ref) | copy-start | bytes 1179652
  2.8 18.5 %collective-permute-start = (bf16[128,1536]{1,0:T(8,128)(2,1)}, bf16[128,1536]{1,0:T(8,128)(2,1)}, u32[]{:S(2)}, u32[]{:S(2)}) collective-permute-start(bf16[128,1536]{1,0:T(8,128)(2,1)} %pack.1.refs_2_.tokens_ref), channel_id=1, source_target_pairs={{0,2},{1,15},{2,4},{3,1},{4,6},{5,3},{6,8},{7,5},{8,10},{9,7},{10,... | collective-permute-start | bytes 1179656 | tf_op jit(solution)/shard_map/ppermute | solution.py:519
  9.2 14.3 %collective-permute-start.1 = (bf16[128,1536]{1,0:T(8,128)(2,1)}, bf16[128,1536]{1,0:T(8,128)(2,1)}, u32[]{:S(2)}, u32[]{:S(2)}) collective-permute-start(bf16[128,1536]{1,0:T(8,128)(2,1)} %pack.1.refs_2_.tokens_ref), channel_id=1, source_target_pairs={{1,2},{0,15},{3,4},{2,1},{5,6},{4,3},{7,8},{6,5},{9,10},{8,7},{11,... | collective-permute-start | bytes 1179656 | tf_op jit(solution)/shard_map/ppermute | solution.py:519
  21.2 11.4 %collective-permute-start.5 = (bf16[128,1536]{1,0:T(8,128)(2,1)}, bf16[128,1536]{1,0:T(8,128)(2,1)S(1)}, u32[]{:S(2)}, u32[]{:S(2)}) collective-permute-start(bf16[128,1536]{1,0:T(8,128)(2,1)} %collective-permute-done.refs_0_), channel_id=1, source_target_pairs={{0,2},{1,15},{2,4},{3,1},{4,6},{5,3},{6,8},{7,5},{8,10},{9,7},{10,... | collective-permute-start | bytes 1179656 | tf_op jit(solution)/shard_map/ppermute | solution.py:519
  22.0 11.3 %collective-permute-start.4 = (bf16[128,1536]{1,0:T(8,128)(2,1)S(1)}, bf16[128,1536]{1,0:T(8,128)(2,1)}, u32[]{:S(2)}, u32[]{:S(2)}) collective-permute-start(bf16[128,1536]{1,0:T(8,128)(2,1)S(1)} %copy-done.2), channel_id=1, source_target_pairs={{0,1},{1,0},{2,3},{3,2},{4,5},{5,4},{6,7},{7,6},{8,9},{9,8},{10,11... | collective-permute-start | bytes 1179656 | tf_op jit(solution)/shard_map/ppermute | solution.py:512
  23.4 9.8 %collective-permute-start.6 = (bf16[128,1536]{1,0:T(8,128)(2,1)}, bf16[128,1536]{1,0:T(8,128)(2,1)S(1)}, u32[]{:S(2)}, u32[]{:S(2)}) collective-permute-start(bf16[128,1536]{1,0:T(8,128)(2,1)} %collective-permute-done.1.refs_1_), channel_id=1, source_target_pairs={{0,2},{1,15},{2,4},{3,1},{4,6},{5,3},{6,8},{7,5},{8,10},{9,7},{10,... | collective-permute-start | bytes 1179656 | tf_op jit(solution)/shard_map/ppermute | solution.py:519
  25.4 10.5 %collective-permute-start.2 = (bf16[128,1536]{1,0:T(8,128)(2,1)}, bf16[128,1536]{1,0:T(8,128)(2,1)}, u32[]{:S(2)}, u32[]{:S(2)}) collective-permute-start(bf16[128,1536]{1,0:T(8,128)(2,1)} %collective-permute-done.refs_0_), channel_id=1, source_target_pairs={{0,1},{1,0},{2,3},{3,2},{4,5},{5,4},{6,7},{7,6},{8,9},{9,8},{10,11... | collective-permute-start | bytes 1179656 | tf_op jit(solution)/shard_map/ppermute | solution.py:512
  25.4 10.5 %collective-permute-start.3 = (bf16[128,1536]{1,0:T(8,128)(2,1)}, bf16[128,1536]{1,0:T(8,128)(2,1)}, u32[]{:S(2)}, u32[]{:S(2)}) collective-permute-start(bf16[128,1536]{1,0:T(8,128)(2,1)} %collective-permute-done.1.refs_1_), channel_id=1, source_target_pairs={{0,1},{1,0},{2,3},{3,2},{4,5},{5,4},{6,7},{7,6},{8,9},{9,8},{10,11... | collective-permute-start | bytes 1179656 | tf_op jit(solution)/shard_map/ppermute | solution.py:512
  27.0 5.6 %copy-start.10 = (bf16[1,1440]{1,0:T(2,128)(2,1)S(1)}, bf16[1,1440]{1,0:T(2,128)(2,1)}, u32[]{:S(2)}) copy-start(bf16[1,1440]{1,0:T(2,128)(2,1)} %param.22) | copy-start | bytes 8644
  27.0 9.0 %copy-start.5 = (bf16[3,1440,1024]{2,1,0:T(8,128)(2,1)S(1)}, bf16[3,1440,1024]{2,1,0:T(8,128)(2,1)}, u32[]{:S(2)}) copy-start(bf16[3,1440,1024]{2,1,0:T(8,128)(2,1)} %get-tuple-element.38.refs_6_.refs_4_) | copy-start | bytes 26542084
  27.0 9.0 %copy-start.8 = (f32[3,1,1024]{2,1,0:T(1,128)S(1)}, f32[3,1,1024]{2,1,0:T(1,128)}, u32[]{:S(2)}) copy-start(f32[3,1,1024]{2,1,0:T(1,128)} %get-tuple-element.40.refs_8_.refs_6_) | copy-start | bytes 36868
  32.6 14.3 %collective-permute-start.9 = (bf16[128,1536]{1,0:T(8,128)(2,1)S(1)}, bf16[128,1536]{1,0:T(8,128)(2,1)S(1)}, u32[]{:S(2)}, u32[]{:S(2)}) collective-permute-start(bf16[128,1536]{1,0:T(8,128)(2,1)S(1)} %collective-permute-done.5.refs_0_), channel_id=1, source_target_pairs={{0,2},{1,15},{2,4},{3,1},{4,6},{5,3},{6,8},{7,5},{8,10},{9,7},{10,... | collective-permute-start | bytes 1179656 | tf_op jit(solution)/shard_map/ppermute | solution.py:519
  33.3 14.9 %collective-permute-start.7 = (bf16[128,1536]{1,0:T(8,128)(2,1)S(1)}, bf16[128,1536]{1,0:T(8,128)(2,1)S(1)}, u32[]{:S(2)}, u32[]{:S(2)}) collective-permute-start(bf16[128,1536]{1,0:T(8,128)(2,1)S(1)} %collective-permute-done.5.refs_0_), channel_id=1, source_target_pairs={{0,1},{1,0},{2,3},{3,2},{4,5},{5,4},{6,7},{7,6},{8,9},{9,8},{10,11... | collective-permute-start | bytes 1179656 | tf_op jit(solution)/shard_map/ppermute | solution.py:512
  33.3 14.9 %collective-permute-start.8 = (bf16[128,1536]{1,0:T(8,128)(2,1)S(1)}, bf16[128,1536]{1,0:T(8,128)(2,1)S(1)}, u32[]{:S(2)}, u32[]{:S(2)}) collective-permute-start(bf16[128,1536]{1,0:T(8,128)(2,1)S(1)} %collective-permute-done.6.refs_1_), channel_id=1, source_target_pairs={{0,1},{1,0},{2,3},{3,2},{4,5},{5,4},{6,7},{7,6},{8,9},{9,8},{10,11... | collective-permute-start | bytes 1179656 | tf_op jit(solution)/shard_map/ppermute | solution.py:512
  35.8 12.3 %collective-permute-start.11 = (bf16[128,1536]{1,0:T(8,128)(2,1)S(1)}, bf16[128,1536]{1,0:T(8,128)(2,1)S(1)}, u32[]{:S(2)}, u32[]{:S(2)}) collective-permute-start(bf16[128,1536]{1,0:T(8,128)(2,1)S(1)} %collective-permute-done.6.refs_1_), channel_id=1, source_target_pairs={{0,2},{1,15},{2,4},{3,1},{4,6},{5,3},{6,8},{7,5},{8,10},{9,7},{10,... | collective-permute-start | bytes 1179656 | tf_op jit(solution)/shard_map/ppermute | solution.py:519
  46.1 0.8 copy-start.6
  46.9 8.3 %collective-permute-start.10 = (bf16[128,1536]{1,0:T(8,128)(2,1)S(1)}, bf16[128,1536]{1,0:T(8,128)(2,1)S(1)}, u32[]{:S(2)}, u32[]{:S(2)}) collective-permute-start(bf16[128,1536]{1,0:T(8,128)(2,1)S(1)} %collective-permute-done.9.refs_1_), channel_id=1, source_target_pairs={{0,2},{1,15},{2,4},{3,1},{4,6},{5,3},{6,8},{7,5},{8,10},{9,7},{10,... | collective-permute-start | bytes 1179656 | tf_op jit(solution)/shard_map/ppermute | solution.py:519
  47.1 8.8 %collective-permute-start.13 = (bf16[128,1536]{1,0:T(8,128)(2,1)S(1)}, bf16[128,1536]{1,0:T(8,128)(2,1)S(1)}, u32[]{:S(2)}, u32[]{:S(2)}) collective-permute-start(bf16[128,1536]{1,0:T(8,128)(2,1)S(1)} %collective-permute-done.9.refs_1_), channel_id=1, source_target_pairs={{0,1},{1,0},{2,3},{3,2},{4,5},{5,4},{6,7},{7,6},{8,9},{9,8},{10,11... | collective-permute-start | bytes 1179656 | tf_op jit(solution)/shard_map/ppermute | solution.py:512
  48.2 7.7 %collective-permute-start.14 = (bf16[128,1536]{1,0:T(8,128)(2,1)S(1)}, bf16[128,1536]{1,0:T(8,128)(2,1)S(1)}, u32[]{:S(2)}, u32[]{:S(2)}) collective-permute-start(bf16[128,1536]{1,0:T(8,128)(2,1)S(1)} %collective-permute-done.11.refs_2_), channel_id=1, source_target_pairs={{0,1},{1,0},{2,3},{3,2},{4,5},{5,4},{6,7},{7,6},{8,9},{9,8},{10,11... | collective-permute-start | bytes 1179656 | tf_op jit(solution)/shard_map/ppermute | solution.py:512
  54.4 0.7 copy-start.7
  55.2 2.0 %collective-permute-start.12 = (bf16[128,1536]{1,0:T(8,128)(2,1)S(1)}, bf16[128,1536]{1,0:T(8,128)(2,1)S(1)}, u32[]{:S(2)}, u32[]{:S(2)}) collective-permute-start(bf16[128,1536]{1,0:T(8,128)(2,1)S(1)} %collective-permute-done.10.refs_0_), channel_id=1, source_target_pairs={{0,1},{1,0},{2,3},{3,2},{4,5},{5,4},{6,7},{7,6},{8,9},{9,8},{10,11... | collective-permute-start | bytes 1179656 | tf_op jit(solution)/shard_map/ppermute | solution.py:512
  65.8 2.1 %collective-permute-start.15 = (bf16[192,1536]{1,0:T(8,128)(2,1)S(1)}, bf16[192,1536]{1,0:T(8,128)(2,1)S(1)}, u32[]{:S(2)}, u32[]{:S(2)}) collective-permute-start(bf16[192,1536]{1,0:T(8,128)(2,1)S(1)} %get-tuple-element.54), channel_id=1, source_target_pairs={{0,1},{1,0},{2,3},{3,2},{4,5},{5,4},{6,7},{7,6},{8,9},{9,8},{10,11... | collective-permute-start | bytes 1769480 | tf_op jit(solution)/shard_map/ppermute | solution.py:512
  69.2 8.2 %collective-permute-start.18 = (f16[128,1536]{1,0:T(8,128)(2,1)}, f16[128,1536]{1,0:T(8,128)(2,1)}, u32[]{:S(2)}, u32[]{:S(2)}) collective-permute-start(f16[128,1536]{1,0:T(8,128)(2,1)} %convert_element_type.52), channel_id=1, source_target_pairs={{0,14},{1,3},{2,0},{3,5},{4,2},{5,7},{6,4},{7,9},{8,6},{9,11},{10,... | collective-permute-start | bytes 1179656 | tf_op jit(solution)/shard_map/ppermute | solution.py:577
  70.3 8.4 %collective-permute-start.17 = (bf16[128,1536]{1,0:T(8,128)(2,1)}, bf16[128,1536]{1,0:T(8,128)(2,1)S(1)}, u32[]{:S(2)}, u32[]{:S(2)}) collective-permute-start(bf16[128,1536]{1,0:T(8,128)(2,1)} %copy-done.7), channel_id=1, source_target_pairs={{0,1},{1,0},{2,3},{3,2},{4,5},{5,4},{6,7},{7,6},{8,9},{9,8},{10,11... | collective-permute-start | bytes 1179656 | tf_op jit(solution)/shard_map/ppermute | solution.py:512
  71.6 10.2 %collective-permute-start.16 = (bf16[192,1536]{1,0:T(8,128)(2,1)}, bf16[192,1536]{1,0:T(8,128)(2,1)S(1)}, u32[]{:S(2)}, u32[]{:S(2)}) collective-permute-start(bf16[192,1536]{1,0:T(8,128)(2,1)} %copy-done.6), channel_id=1, source_target_pairs={{0,1},{1,0},{2,3},{3,2},{4,5},{5,4},{6,7},{7,6},{8,9},{9,8},{10,11... | collective-permute-start | bytes 1769480 | tf_op jit(solution)/shard_map/ppermute | solution.py:512
  71.7 9.7 %collective-permute-start.22 = (f16[128,1536]{1,0:T(8,128)(2,1)S(1)}, f16[128,1536]{1,0:T(8,128)(2,1)S(1)}, u32[]{:S(2)}, u32[]{:S(2)}) collective-permute-start(f16[128,1536]{1,0:T(8,128)(2,1)S(1)} %convert_element_type.60), channel_id=1, source_target_pairs={{0,14},{1,3},{2,0},{3,5},{4,2},{5,7},{6,4},{7,9},{8,6},{9,11},{10,... | collective-permute-start | bytes 1179656 | tf_op jit(solution)/shard_map/ppermute | solution.py:577
  78.4 17.7 %copy-start.11 = (bf16[1440]{0:T(1024)(128)(2,1)S(1)}, bf16[1440]{0:T(1024)(128)(2,1)}, u32[]{:S(2)}) copy-start(bf16[1440]{0:T(1024)(128)(2,1)} %param.23) | copy-start | bytes 8644
  78.5 7.9 %collective-permute-start.19 = (f16[128,1536]{1,0:T(8,128)(2,1)S(1)}, f16[128,1536]{1,0:T(8,128)(2,1)S(1)}, u32[]{:S(2)}, u32[]{:S(2)}) collective-permute-start(f16[128,1536]{1,0:T(8,128)(2,1)S(1)} %add_convert_fusion.4), channel_id=1, source_target_pairs={{0,14},{1,3},{2,0},{3,5},{4,2},{5,7},{6,4},{7,9},{8,6},{9,11},{10,... | collective-permute-start | bytes 1179656 | tf_op jit(solution)/shard_map/ppermute | solution.py:577
  81.6 24.2 %copy-start.3 = (bf16[1440,256]{1,0:T(8,128)(2,1)S(1)}, bf16[1440,256]{1,0:T(8,128)(2,1)}, u32[]{:S(2)}) copy-start(bf16[1440,256]{1,0:T(8,128)(2,1)} %key_ref.1) | copy-start | bytes 2211844
  81.6 24.2 %copy-start.4 = (bf16[1440,256]{1,0:T(8,128)(2,1)S(1)}, bf16[1440,256]{1,0:T(8,128)(2,1)}, u32[]{:S(2)}) copy-start(bf16[1440,256]{1,0:T(8,128)(2,1)} %value_ref.1) | copy-start | bytes 2211844
  81.6 9.0 %collective-permute-start.23 = (f16[128,1536]{1,0:T(8,128)(2,1)S(1)}, f16[128,1536]{1,0:T(8,128)(2,1)S(1)}, u32[]{:S(2)}, u32[]{:S(2)}) collective-permute-start(f16[128,1536]{1,0:T(8,128)(2,1)S(1)} %add_convert_fusion.1), channel_id=1, source_target_pairs={{0,14},{1,3},{2,0},{3,5},{4,2},{5,7},{6,4},{7,9},{8,6},{9,11},{10,... | collective-permute-start | bytes 1179656 | tf_op jit(solution)/shard_map/ppermute | solution.py:577
  86.5 8.3 %collective-permute-start.20 = (f16[128,1536]{1,0:T(8,128)(2,1)S(1)}, f16[128,1536]{1,0:T(8,128)(2,1)S(1)}, u32[]{:S(2)}, u32[]{:S(2)}) collective-permute-start(f16[128,1536]{1,0:T(8,128)(2,1)S(1)} %add_convert_fusion.3), channel_id=1, source_target_pairs={{0,14},{1,3},{2,0},{3,5},{4,2},{5,7},{6,4},{7,9},{8,6},{9,11},{10,... | collective-permute-start | bytes 1179656 | tf_op jit(solution)/shard_map/ppermute | solution.py:577
  91.4 7.7 %collective-permute-start.24 = (f16[128,1536]{1,0:T(8,128)(2,1)}, f16[128,1536]{1,0:T(8,128)(2,1)S(1)}, u32[]{:S(2)}, u32[]{:S(2)}) collective-permute-start(f16[128,1536]{1,0:T(8,128)(2,1)} %add_convert_fusion), channel_id=1, source_target_pairs={{0,15},{1,2},{2,1},{3,4},{4,3},{5,6},{6,5},{7,8},{8,7},{9,10},{10,... | collective-permute-start | bytes 1179656 | tf_op jit(solution)/shard_map/ppermute | solution.py:577
  95.6 9.0 %collective-permute-start.21 = (f16[128,1536]{1,0:T(8,128)(2,1)}, f16[128,1536]{1,0:T(8,128)(2,1)}, u32[]{:S(2)}, u32[]{:S(2)}) collective-permute-start(f16[128,1536]{1,0:T(8,128)(2,1)} %add_convert_fusion.2), channel_id=1, source_target_pairs={{0,14},{1,3},{2,0},{3,5},{4,2},{5,7},{6,4},{7,9},{8,6},{9,11},{10,... | collective-permute-start | bytes 1179656 | tf_op jit(solution)/shard_map/ppermute | solution.py:577
  105.8 9.2 %copy-start.9 = (f32[32]{0:T(128)S(1)}, f32[32]{0:T(128)}, u32[]{:S(2)}) copy-start(f32[32]{0:T(128)} %sinks_ref.1) | copy-start | bytes 388
  106.5 8.5 %collective-permute-start.25 = (bf16[128,512]{1,0:T(8,128)(2,1)S(1)}, bf16[128,512]{1,0:T(8,128)(2,1)S(1)}, u32[]{:S(2)}, u32[]{:S(2)}) collective-permute-start(bf16[128,512]{1,0:T(8,128)(2,1)S(1)} %get-tuple-element.71.own_ref), channel_id=1, source_target_pairs={{0,1},{1,2},{2,3},{3,4},{4,5},{5,6},{6,7},{7,8},{8,9},{9,10},{10,1... | collective-permute-start | bytes 393224 | tf_op jit(solution)/shard_map/ppermute | solution.py:592
  109.6 2.7 %copy-start.1 = (bf16[1440,2048]{1,0:T(8,128)(2,1)S(1)}, bf16[1440,2048]{1,0:T(8,128)(2,1)}, u32[]{:S(2)}) copy-start(bf16[1440,2048]{1,0:T(8,128)(2,1)} %weight_ref.1) | copy-start | bytes 17694724

commit v3 on v2

--- a/solution.py
+++ b/solution.py
@@ -43,7 +43,7 @@
         lanes = slice(512 * half, 512 * half + 512)
         left = 2880 - 1024 * chunk - 512 * half
         column = lax.broadcasted_iota(jnp.int32, (45, 512), 1)
-        scale = power_of_two(exponent_ref[:, lanes], 119, column < left)
+        scale = power_of_two(exponent_ref[:, 0, lanes], 119, column < left)
         scale = jnp.dot(scale.astype(BF16), spread, preferred_element_type=F32)
         bias = jnp.where(column[:1] < left, bias_ref[:, lanes].astype(F32), 0.0)
         bias = jnp.broadcast_to(bias, (16, 512)).astype(BF16)
@@ -72,7 +72,7 @@
         grid=(CHUNKS,),
         in_specs=[
             pl.BlockSpec((1440, 256), lambda b: (0, b)),
-            pl.BlockSpec((45, 1024), lambda b: (0, b)),
+            pl.BlockSpec((45, 1, 1024), lambda b: (0, 0, b)),
             pl.BlockSpec((1, 1024), lambda b: (0, b)),
         ],
         out_specs=[
@@ -96,7 +96,7 @@
     row = lax.broadcasted_iota(jnp.int32, (16, 512), 0) + 16 * pl.program_id(0)
     column = lax.broadcasted_iota(jnp.int32, (16, 512), 1)
     scales = [
-        power_of_two(exponent_ref[...], 117, (row < 45) & (column < 1440 - 512 * part))
+        power_of_two(exponent_ref[:, 0, :], 117, (row < 45) & (column < 1440 - 512 * part))
         for part, exponent_ref in enumerate((left_exp_ref, middle_exp_ref, right_exp_ref))
     ]
     source = lax.broadcasted_iota(jnp.int32, (512, 512), 0)
@@ -129,9 +129,9 @@
             pl.BlockSpec((512, 128), lambda b: (b, 0)),
             pl.BlockSpec((512, 128), lambda b: (b, 1)),
             pl.BlockSpec((512, 128), lambda b: (b, 2)),
-            pl.BlockSpec((16, 512), lambda b: (b, 0)),
-            pl.BlockSpec((16, 512), lambda b: (b, 1)),
-            pl.BlockSpec((16, 512), lambda b: (b, 2)),
+            pl.BlockSpec((16, 1, 512), lambda b: (b, 0, 0)),
+            pl.BlockSpec((16, 1, 512), lambda b: (b, 0, 1)),
+            pl.BlockSpec((16, 1, 512), lambda b: (b, 0, 2)),
         ],
         out_specs=pl.BlockSpec(memory_space=pltpu.VMEM),
         out_shape=jax.ShapeDtypeStruct((CHUNKS, 512, WIDE), BF16),
@@ -349,9 +349,12 @@
 def mix_kernel(
     tokens_ref, mixture_ref, gain_ref, key_ref, value_ref, cos_ref, sin_ref, out_ref, normed_ref, kv_ref
 ):
-    block_out = (tokens_ref[:, :1440].astype(F32) + mixture_ref[...]).astype(BF16)
-    out_ref[...] = block_out
-    widened = block_out.astype(F32)
+    rounded = (tokens_ref[...].astype(F32) + mixture_ref[...]).astype(BF16).astype(F32)
+    for place in range(11):
+        rows = slice(128 * place, 128 * place + 128)
+        out_ref[rows, :] = rounded[:, rows].T.astype(BF16)
+    out_ref[1408:, :] = rounded[:, 1408:].T[:32].astype(BF16)
+    widened = rounded[:, :1440]
     squares = jnp.sum(widened * widened, axis=1, keepdims=True) / 1440.0
     normed = (widened * lax.rsqrt(squares + 1e-05) * gain_ref[...].astype(F32)).astype(BF16)
     normed_ref[...] = normed
@@ -364,7 +367,7 @@
     return pl.pallas_call(
         mix_kernel,
         out_shape=[
-            jax.ShapeDtypeStruct((128, 1440), BF16),
+            jax.ShapeDtypeStruct((1440, 128), BF16),
             jax.ShapeDtypeStruct((128, 1440), BF16),
             jax.ShapeDtypeStruct((128, 512), BF16),
         ],
@@ -447,7 +450,7 @@
                 weights = jnp.exp(part - top)
                 whole = jnp.exp(sink - top) + jnp.sum(weights, axis=1, keepdims=True)
                 halves.append(weights * (1.0 / whole))
-            probs = jnp.where(allowed, jnp.concatenate(halves, axis=1), 0.0)
+            probs = jnp.concatenate(halves, axis=1)
             here_probs.append(jnp.where(mine, probs, 0.0).astype(BF16))
             there_probs.append(jnp.where(mine, 0.0, probs).astype(BF16))
         mixed = jnp.dot(
@@ -520,8 +523,10 @@
 
     packed = pack(tokens, route_ids, route_level)
 
-    second = decode_down(down_codes[0], down_scale[0])
-    first, first_bias = decode_up(gate_up_codes[0], gate_up_scale[0], gate_up_bias)
+    second = decode_down(down_codes[0], down_scale.transpose(1, 0, 2))
+    first, first_bias = decode_up(
+        gate_up_codes[0], gate_up_scale.transpose(1, 0, 2), gate_up_bias
+    )
     second_bias = jnp.pad(down_bias.astype(F32), ((0, 0), (0, WIDE - width)))
     experts = jnp.stack([device_index, device_index + 1 - 2 * core]).astype(jnp.int32)
 
@@ -583,7 +588,7 @@
     from_cross = onward(cross_near[2] + from_cross, False)
     from_same = onward(same_near[1] + from_same, False)
     from_cross = onward(cross_near[1] + from_cross, True)
-    mixture = (own + from_same + from_cross)[:, :width] * (1.0 / RETURN_SCALE)
+    mixture = (own + from_same + from_cross) * (1.0 / RETURN_SCALE)
 
     block_out, normed, own_kv = mix(
         packed, mixture, attn_gain[None], key_matrix, value_matrix, cosine, sine_part
@@ -592,7 +597,7 @@
     halo_kv = lax.ppermute(own_kv, "expert", ahead)
     query = queries(normed, query_weight, cosine, sine_part)
     attended = attend(device_index.reshape(1), sinks, query, own_kv, halo_kv)
-    return (block_out, attended)
+    return (block_out.T, attended)
 
 
 def solution(mesh):

time: 121 us -> 121 us (level)
  waiting for transfers between devices: 29.6 us -> 22.7 us
  starting transfers between devices: 23.2 us -> 28.7 us
  Pallas kernels: 51.6 us -> 53.8 us
    ppermute x7, waiting for transfers between devices: 26.6 us -> 19.9 us  [onward(): return lax.ppermute(block.astype(jnp.float16), 'expert', route).astype(F32)]
    ppermute x7, starting transfers between devices: 2.88 us -> 8 us  [onward(): return lax.ppermute(block.astype(jnp.float16), 'expert', route).astype(F32)]
    unnamed x27 -> x36, local copies, waits for them, and re-layouts: 8.08 us -> 7.31 us
  transfers between devices with their start and end apart: 26 -> 26, of which waited for: 9 -> 9; matrix products, arithmetic and copies ran while one was open for 6% -> 3% of each run, Pallas kernels for 30% -> 31%
where the time goes in v3:
time: 121 us; the launch traced here: 119 us
  Pallas kernels  53.8 us (44%)
  starting transfers between devices  28.7 us (24%)
  waiting for transfers between devices  22.7 us (19%)
  local copies, waits for them, and re-layouts  7.49 us (6%)
  other arithmetic  5.55 us (5%)
    pallas_call x3, Pallas kernels, run_experts(): pl.pallas_call(functools.partial(expert_kernel, count), grid_spec=pltpu.P...  25.6 us
    ppermute x7, waiting for transfers between devices, onward(): return lax.ppermute(block.astype(jnp.float16), 'expert', route).astype(F32)  19.9 us
    pallas_call x1, Pallas kernels, decode_up(): pl.pallas_call(decode_up_kernel, grid=(CHUNKS,), in_specs=[pl.BlockSpec((...  10.4 us
    ppermute x7, starting transfers between devices, inward(): return lax.ppermute(block, 'expert', route)  10.2 us
    ppermute x7, starting transfers between devices, onward(): return lax.ppermute(block.astype(jnp.float16), 'expert', route).astype(F32)  8 us
    ppermute x11, starting transfers between devices, swap(): return lax.ppermute(block, 'expert', partner)  7.52 us
    unnamed x36, local copies, waits for them, and re-layouts  7.31 us
    pallas_call x1, Pallas kernels, decode_down(): pl.pallas_call(decode_down_kernel, grid=(CHUNKS,), in_specs=[pl.BlockSpec...  6.21 us
  transfers between devices with their start and end apart: 26, of which 9 were waited for; matrix products, arithmetic and copies ran while one was open for 3% of the time, Pallas kernels for 31%

profile of v3, /device:TPU:1, one launch (start us, length us, event | category | flops | bytes accessed | tf_op | source)
XLA Modules:
  0.0 119.2 jit_solution(14910060935514265419)
XLA Ops:
  0.7 2.1 %pack.1.refs_2_.tokens_ref = bf16[128,1536]{1,0:T(8,128)(2,1)} custom-call(bf16[1440,128]{1,0:T(8,128)(2,1)} %bitcast.19, s32[4,128]{1,0:T(4,128)} %bitcast.21, s32[4,128]{1,0:T(4,128)} %bitcast.22), custom_call_target="tpu_custom_call" | custom-call | tf_op jit(solution)/shard_map/pack/pallas_call | solution.py:178
  2.8 6.4 %collective-permute-start = (bf16[128,1536]{1,0:T(8,128)(2,1)}, bf16[128,1536]{1,0:T(8,128)(2,1)S(1)}, u32[]{:S(2)}, u32[]{:S(2)}) collective-permute-start(bf16[128,1536]{1,0:T(8,128)(2,1)} %pack.1.refs_2_.tokens_ref), channel_id=1, source_target_pairs={{0,2},{1,15},{2,4},{3,1},{4,6},{5,3},{6,8},{7,5},{8,10},{9,7},{10,... | collective-permute-start | bytes 1179656 | tf_op jit(solution)/shard_map/ppermute | solution.py:522
  9.2 10.4 %decode_up.1 = (bf16[3,1440,1024]{2,1,0:T(8,128)(2,1)}, f32[3,1,1024]{2,1,0:T(1,128)}) custom-call(s32[1440,720]{1,0:T(8,128)} %bitcast.17, s32[45,1,2880]{2,1,0:T(1,128)} %bitcast.18, bf16[1,2880]{1,0:T(2,128)(2,1)} %bias_ref.1), custom_call_target="tpu_custom_call" | custom-call | flops 60000000 | bytes 30000000 | tf_op jit(solution)/shard_map/decode_up/pallas_call | solution.py:70
  19.6 0.8 collective-permute-start.5
  20.4 1.4 %collective-permute-start.4 = (bf16[128,1536]{1,0:T(8,128)(2,1)S(1)}, bf16[128,1536]{1,0:T(8,128)(2,1)}, u32[]{:S(2)}, u32[]{:S(2)}) collective-permute-start(bf16[128,1536]{1,0:T(8,128)(2,1)S(1)} %copy-done.3), channel_id=1, source_target_pairs={{0,1},{1,0},{2,3},{3,2},{4,5},{5,4},{6,7},{7,6},{8,9},{9,8},{10,11... | collective-permute-start | bytes 1179656 | tf_op jit(solution)/shard_map/ppermute | solution.py:515
  21.8 1.9 %collective-permute-start.6 = (bf16[128,1536]{1,0:T(8,128)(2,1)}, bf16[128,1536]{1,0:T(8,128)(2,1)}, u32[]{:S(2)}, u32[]{:S(2)}) collective-permute-start(bf16[128,1536]{1,0:T(8,128)(2,1)} %collective-permute-done.1.refs_1_), channel_id=1, source_target_pairs={{0,2},{1,15},{2,4},{3,1},{4,6},{5,3},{6,8},{7,5},{8,10},{9,7},{10,... | collective-permute-start | bytes 1179656 | tf_op jit(solution)/shard_map/ppermute | solution.py:522
  23.8 0.5 collective-permute-start.3
  24.3 0.1 pad_add_fusion.place_ref
  24.4 6.2 %decode_down.1.refs_7_.refs_5_ = bf16[3,512,1536]{2,1,0:T(8,128)(2,1)S(1)} custom-call(s32[1440,360]{1,0:T(8,128)S(1)} %bitcast.11, s32[1440,360]{1,0:T(8,128)S(1)} %bitcast.12, s32[1440,360]{1,0:T(8,128)S(1)} %bitcast.13, s32[45,1,1440]{2,1,0:T(1,128)S(1)} %bitcast.14, s32[45,1,1440]{2,1,0:T(1,128)S(1)} %bitcast.15, s32[45,1,1440]{2,1,0:T(1,128)S(1)} %bitcast.16), custom_call_target="tpu_custom_call" | custom-call | flops 60000000 | bytes 20000000 | tf_op jit(solution)/shard_map/decode_down/pallas_call | solution.py:125
  30.6 0.7 collective-permute-start.9
  31.3 2.8 %collective-permute-start.8 = (bf16[128,1536]{1,0:T(8,128)(2,1)}, bf16[128,1536]{1,0:T(8,128)(2,1)S(1)}, u32[]{:S(2)}, u32[]{:S(2)}) collective-permute-start(bf16[128,1536]{1,0:T(8,128)(2,1)} %collective-permute-done.6.refs_1_), channel_id=1, source_target_pairs={{0,1},{1,0},{2,3},{3,2},{4,5},{5,4},{6,7},{7,6},{8,9},{9,8},{10,11... | collective-permute-start | bytes 1179656 | tf_op jit(solution)/shard_map/ppermute | solution.py:515
  34.1 1.0 copy-done.12
  35.1 9.9 %experts.3 = (bf16[192,1536]{1,0:T(8,128)(2,1)S(1)}, bf16[192,1536]{1,0:T(8,128)(2,1)S(1)}, bf16[3,128,256]{2,1,0:T(8,128)(2,1)S(1)}) custom-call(s32[2]{0:T(128)S(1)} %pad_add_fusion.place_ref, bf16[128,1536]{1,0:T(8,128)(2,1)S(1)} %copy-done.12, bf16[128,1536]{1,0:T(8,128)(2,1)} %collective-permute-done.1.refs_1_, bf16[128,1536]{1,0:T(8,128)(2,1)S(1)} %copy-done.3, ...), custom_call_target="tpu_custom_call" | custom-call | flops 9555148800 | bytes 30000000 | tf_op jit(solution)/shard_map/experts/pallas_call | solution.py:288
  45.0 0.7 copy-done.8
  45.7 0.4 collective-permute-start.10
  46.1 0.7 collective-permute-start.13
  46.8 7.3 %experts.4 = (bf16[128,1536]{1,0:T(8,128)(2,1)S(1)}, bf16[128,1536]{1,0:T(8,128)(2,1)S(1)}, bf16[2,128,256]{2,1,0:T(8,128)(2,1)S(1)}) custom-call(s32[2]{0:T(128)S(1)} %pad_add_fusion.place_ref, bf16[128,1536]{1,0:T(8,128)(2,1)} %collective-permute-done.5.refs_0_, bf16[128,1536]{1,0:T(8,128)(2,1)} %collective-permute-done.6.refs_1_, ...), custom_call_target="tpu_custom_call" | custom-call | flops 6370099200 | bytes 30000000 | tf_op jit(solution)/shard_map/experts/pallas_call | solution.py:288
  54.1 0.7 copy-done.6
  54.9 0.5 collective-permute-start.12
  55.4 0.2 copy-done.13
  55.6 1.1 collective-permute-done.12.refs_3_
  56.7 8.5 %experts.5 = (bf16[192,1536]{1,0:T(8,128)(2,1)S(1)}, bf16[192,1536]{1,0:T(8,128)(2,1)S(1)}, bf16[3,128,256]{2,1,0:T(8,128)(2,1)S(1)}) custom-call(s32[2]{0:T(128)S(1)} %pad_add_fusion.place_ref, bf16[128,1536]{1,0:T(8,128)(2,1)S(1)} %collective-permute-done.10.refs_0_, bf16[128,1536]{1,0:T(8,128)(2,1)S(1)} %collective-permute-done.9.refs_1_, ...), custom_call_target="tpu_custom_call" | custom-call | flops 9555148800 | bytes 30000000 | tf_op jit(solution)/shard_map/experts/pallas_call | solution.py:288
  65.2 0.5 collective-permute-start.15
  65.7 1.6 %collective-permute-done.15.other_ref = bf16[192,1536]{1,0:T(8,128)(2,1)S(1)} collective-permute-done((bf16[192,1536]{1,0:T(8,128)(2,1)S(1)}, bf16[192,1536]{1,0:T(8,128)(2,1)S(1)}, u32[]{:S(2)}, u32[]{:S(2)}) %collective-permute-start.15) | collective-permute-done | bytes 589856 | tf_op jit(solution)/shard_map/ppermute | solution.py:515
  67.3 0.5 combine.3
  67.8 0.8 convert_element_type.52
  68.6 1.4 %collective-permute-start.18 = (f16[128,1536]{1,0:T(8,128)(2,1)}, f16[128,1536]{1,0:T(8,128)(2,1)}, u32[]{:S(2)}, u32[]{:S(2)}) collective-permute-start(f16[128,1536]{1,0:T(8,128)(2,1)} %convert_element_type.52), channel_id=1, source_target_pairs={{0,14},{1,3},{2,0},{3,5},{4,2},{5,7},{6,4},{7,9},{8,6},{9,11},{10,... | collective-permute-start | bytes 1179656 | tf_op jit(solution)/shard_map/ppermute | solution.py:582
  70.0 1.1 collective-permute-start.17
  71.1 0.1 collective-permute-start.16
  71.2 1.7 %collective-permute-start.22 = (f16[128,1536]{1,0:T(8,128)(2,1)S(1)}, f16[128,1536]{1,0:T(8,128)(2,1)S(1)}, u32[]{:S(2)}, u32[]{:S(2)}) collective-permute-start(f16[128,1536]{1,0:T(8,128)(2,1)S(1)} %convert_element_type.60), channel_id=1, source_target_pairs={{0,14},{1,3},{2,0},{3,5},{4,2},{5,7},{6,4},{7,9},{8,6},{9,11},{10,... | collective-permute-start | bytes 1179656 | tf_op jit(solution)/shard_map/ppermute | solution.py:582
  73.0 3.8 %collective-permute-done.18 = f16[128,1536]{1,0:T(8,128)(2,1)} collective-permute-done((f16[128,1536]{1,0:T(8,128)(2,1)}, f16[128,1536]{1,0:T(8,128)(2,1)}, u32[]{:S(2)}, u32[]{:S(2)}) %collective-permute-start.18) | collective-permute-done | bytes 393248 | tf_op jit(solution)/shard_map/ppermute | solution.py:582
  76.7 1.1 add_convert_fusion.4
  77.9 0.7 collective-permute-start.19
  78.6 1.0 copy-done.7
  79.6 0.4 combine.5
  79.9 0.9 collective-permute-done.22
  80.8 0.1 add_convert_fusion.1
  80.9 0.0 copy-start.4
  81.0 0.0 copy-start.5
  81.0 1.4 %collective-permute-start.23 = (f16[128,1536]{1,0:T(8,128)(2,1)S(1)}, f16[128,1536]{1,0:T(8,128)(2,1)S(1)}, u32[]{:S(2)}, u32[]{:S(2)}) collective-permute-start(f16[128,1536]{1,0:T(8,128)(2,1)S(1)} %add_convert_fusion.1), channel_id=1, source_target_pairs={{0,14},{1,3},{2,0},{3,5},{4,2},{5,7},{6,4},{7,9},{8,6},{9,11},{10,... | collective-permute-start | bytes 1179656 | tf_op jit(solution)/shard_map/ppermute | solution.py:582
  82.4 0.9 copy-done.9
  83.3 0.5 combine.4
  83.8 2.0 %collective-permute-done.19 = f16[128,1536]{1,0:T(8,128)(2,1)S(1)} collective-permute-done((f16[128,1536]{1,0:T(8,128)(2,1)S(1)}, f16[128,1536]{1,0:T(8,128)(2,1)S(1)}, u32[]{:S(2)}, u32[]{:S(2)}) %collective-permute-start.19) | collective-permute-done | bytes 393248 | tf_op jit(solution)/shard_map/ppermute | solution.py:582
  85.8 0.1 add_convert_fusion.3
  85.9 0.1 collective-permute-start.20
  86.0 4.0 %collective-permute-done.23 = f16[128,1536]{1,0:T(8,128)(2,1)S(1)} collective-permute-done((f16[128,1536]{1,0:T(8,128)(2,1)S(1)}, f16[128,1536]{1,0:T(8,128)(2,1)S(1)}, u32[]{:S(2)}, u32[]{:S(2)}) %collective-permute-start.23) | collective-permute-done | bytes 393248 | tf_op jit(solution)/shard_map/ppermute | solution.py:582
  90.0 0.8 add_convert_fusion
  90.8 2.1 %collective-permute-start.24 = (f16[128,1536]{1,0:T(8,128)(2,1)}, f16[128,1536]{1,0:T(8,128)(2,1)S(1)}, u32[]{:S(2)}, u32[]{:S(2)}) collective-permute-start(f16[128,1536]{1,0:T(8,128)(2,1)} %add_convert_fusion), channel_id=1, source_target_pairs={{0,15},{1,2},{2,1},{3,4},{4,3},{5,6},{6,5},{7,8},{8,7},{9,10},{10,... | collective-permute-start | bytes 1179656 | tf_op jit(solution)/shard_map/ppermute | solution.py:582
  93.0 1.2 %collective-permute-done.20 = f16[128,1536]{1,0:T(8,128)(2,1)S(1)} collective-permute-done((f16[128,1536]{1,0:T(8,128)(2,1)S(1)}, f16[128,1536]{1,0:T(8,128)(2,1)S(1)}, u32[]{:S(2)}, u32[]{:S(2)}) %collective-permute-start.20) | collective-permute-done | bytes 393248 | tf_op jit(solution)/shard_map/ppermute | solution.py:582
  94.2 0.9 add_convert_fusion.2
  95.0 0.5 collective-permute-start.21
  95.6 0.3 fusion
  95.9 0.1 copy.20
  96.0 0.1 copy.21.cos_ref
  96.1 0.1 pad_maximum_fusion.sin_ref
  96.2 2.8 %collective-permute-done.24 = f16[128,1536]{1,0:T(8,128)(2,1)S(1)} collective-permute-done((f16[128,1536]{1,0:T(8,128)(2,1)}, f16[128,1536]{1,0:T(8,128)(2,1)S(1)}, u32[]{:S(2)}, u32[]{:S(2)}) %collective-permute-start.24) | collective-permute-done | bytes 393248 | tf_op jit(solution)/shard_map/ppermute | solution.py:582
  99.0 5.2 %collective-permute-done.21 = f16[128,1536]{1,0:T(8,128)(2,1)} collective-permute-done((f16[128,1536]{1,0:T(8,128)(2,1)}, f16[128,1536]{1,0:T(8,128)(2,1)}, u32[]{:S(2)}, u32[]{:S(2)}) %collective-permute-start.21) | collective-permute-done | bytes 393248 | tf_op jit(solution)/shard_map/ppermute | solution.py:582
  104.2 1.2 add_multiply_fusion.mixture_ref
  105.4 0.0 copy-start.15
  105.4 1.3 %mix.1 = (bf16[1440,128]{1,0:T(8,128)(2,1)}, bf16[128,1440]{1,0:T(8,128)(2,1)S(1)}, bf16[128,512]{1,0:T(8,128)(2,1)S(1)}) custom-call(bf16[128,1536]{1,0:T(8,128)(2,1)S(1)} %copy-done.3, f32[128,1536]{1,0:T(8,128)S(1)} %add_multiply_fusion.mixture_ref, bf16[1,1440]{1,0:T(2,128)(2,1)S(1)} %broadcast_in_dim.2.gain_ref, bf16[1440,256]{1,0:T(8,128)(2,1)S(1)} %copy-done.4, ...), custom_call_target="tpu_custom_call" | custom-call | flops 188743680 | bytes 3000000 | tf_op jit(solution)/shard_map/mix/pallas_call | solution.py:367
  106.8 3.0 %collective-permute-start.25 = (bf16[128,512]{1,0:T(8,128)(2,1)S(1)}, bf16[128,512]{1,0:T(8,128)(2,1)S(1)}, u32[]{:S(2)}, u32[]{:S(2)}) collective-permute-start(bf16[128,512]{1,0:T(8,128)(2,1)S(1)} %get-tuple-element.71.own_ref), channel_id=1, source_target_pairs={{0,1},{1,2},{2,3},{3,4},{4,5},{5,6},{6,7},{7,8},{8,9},{9,10},{10,1... | collective-permute-start | bytes 393224 | tf_op jit(solution)/shard_map/ppermute | solution.py:597
  109.8 2.7 %copy-done.1 = bf16[1440,2048]{1,0:T(8,128)(2,1)S(1)} copy-done((bf16[1440,2048]{1,0:T(8,128)(2,1)S(1)}, bf16[1440,2048]{1,0:T(8,128)(2,1)}, u32[]{:S(2)}) %copy-start.1) | copy-done | bytes 5898264
  112.4 2.7 %queries.1.queries_ref = bf16[4,512,128]{2,1,0:T(8,128)(2,1)S(1)} custom-call(bf16[128,1440]{1,0:T(8,128)(2,1)S(1)} %get-tuple-element.70.normed_ref, bf16[1440,2048]{1,0:T(8,128)(2,1)S(1)} %copy-done.1, f32[128,128]{1,0:T(8,128)S(1)} %copy.21.cos_ref, f32[128,128]{1,0:T(8,128)S(1)} %pad_maximum_fusion.sin_ref), custom_call_target="tpu_custom_call" | custom-call | flops 754974720 | bytes 7000000 | tf_op jit(solution)/shard_map/queries/pallas_call | solution.py:391
  115.2 4.0 %attend.1 = bf16[128,2048]{1,0:T(8,128)(2,1)} custom-call(s32[1]{0:T(128)} %bitcast.3.index_ref, f32[32]{0:T(128)S(1)} %copy-done.15, bf16[4,512,128]{2,1,0:T(8,128)(2,1)S(1)} %queries.1.queries_ref, bf16[128,512]{1,0:T(8,128)(2,1)S(1)} %get-tuple-element.71.own_ref, bf16[128,512]{1,0:T(8,128)(2,1)S(1)} %collective-permute-done.25.halo_ref), custom_call_target="tpu_custom_call" | custom-call | flops 268435456 | bytes 1500000 | tf_op jit(solution)/shard_map/attend/pallas_call | solution.py:471
  (54 shorter events, 0.2 us)
Async XLA Ops:
  0.6 23.7 %copy-start = (s32[1,1440,360]{2,1,0:T(8,128)S(1)}, s32[1,1440,360]{2,1,0:T(8,128)}, u32[]{:S(2)}) copy-start(s32[1,1440,360]{2,1,0:T(8,128)} %param.20) | copy-start | bytes 6220804
  0.6 23.7 %copy-start.2 = (s32[1,45,1440]{2,0,1:T(1,128)S(1)}, s32[1,45,1440]{2,0,1:T(1,128)}, u32[]{:S(2)}) copy-start(s32[1,45,1440]{2,0,1:T(1,128)} %param.21) | copy-start | bytes 777604
  2.8 17.6 %copy-start.3 = (bf16[128,1536]{1,0:T(8,128)(2,1)S(1)}, bf16[128,1536]{1,0:T(8,128)(2,1)}, u32[]{:S(2)}) copy-start(bf16[128,1536]{1,0:T(8,128)(2,1)} %pack.1.refs_2_.tokens_ref) | copy-start | bytes 1179652
  2.8 16.8 %collective-permute-start = (bf16[128,1536]{1,0:T(8,128)(2,1)}, bf16[128,1536]{1,0:T(8,128)(2,1)S(1)}, u32[]{:S(2)}, u32[]{:S(2)}) collective-permute-start(bf16[128,1536]{1,0:T(8,128)(2,1)} %pack.1.refs_2_.tokens_ref), channel_id=1, source_target_pairs={{0,2},{1,15},{2,4},{3,1},{4,6},{5,3},{6,8},{7,5},{8,10},{9,7},{10,... | collective-permute-start | bytes 1179656 | tf_op jit(solution)/shard_map/ppermute | solution.py:522
  9.2 12.6 %collective-permute-start.1 = (bf16[128,1536]{1,0:T(8,128)(2,1)}, bf16[128,1536]{1,0:T(8,128)(2,1)}, u32[]{:S(2)}, u32[]{:S(2)}) collective-permute-start(bf16[128,1536]{1,0:T(8,128)(2,1)} %pack.1.refs_2_.tokens_ref), channel_id=1, source_target_pairs={{1,2},{0,15},{3,4},{2,1},{5,6},{4,3},{7,8},{6,5},{9,10},{8,7},{11,... | collective-permute-start | bytes 1179656 | tf_op jit(solution)/shard_map/ppermute | solution.py:522
  19.6 11.0 %copy-start.11 = (bf16[128,1536]{1,0:T(8,128)(2,1)}, bf16[128,1536]{1,0:T(8,128)(2,1)S(1)}, u32[]{:S(2)}) copy-start(bf16[128,1536]{1,0:T(8,128)(2,1)S(1)} %collective-permute-done.refs_0_) | copy-start | bytes 1179652
  19.6 11.0 %collective-permute-start.5 = (bf16[128,1536]{1,0:T(8,128)(2,1)S(1)}, bf16[128,1536]{1,0:T(8,128)(2,1)}, u32[]{:S(2)}, u32[]{:S(2)}) collective-permute-start(bf16[128,1536]{1,0:T(8,128)(2,1)S(1)} %collective-permute-done.refs_0_), channel_id=1, source_target_pairs={{0,2},{1,15},{2,4},{3,1},{4,6},{5,3},{6,8},{7,5},{8,10},{9,7},{10,... | collective-permute-start | bytes 1179656 | tf_op jit(solution)/shard_map/ppermute | solution.py:522
  20.4 10.9 %collective-permute-start.4 = (bf16[128,1536]{1,0:T(8,128)(2,1)S(1)}, bf16[128,1536]{1,0:T(8,128)(2,1)}, u32[]{:S(2)}, u32[]{:S(2)}) collective-permute-start(bf16[128,1536]{1,0:T(8,128)(2,1)S(1)} %copy-done.3), channel_id=1, source_target_pairs={{0,1},{1,0},{2,3},{3,2},{4,5},{5,4},{6,7},{7,6},{8,9},{9,8},{10,11... | collective-permute-start | bytes 1179656 | tf_op jit(solution)/shard_map/ppermute | solution.py:515
  21.8 9.5 %collective-permute-start.6 = (bf16[128,1536]{1,0:T(8,128)(2,1)}, bf16[128,1536]{1,0:T(8,128)(2,1)}, u32[]{:S(2)}, u32[]{:S(2)}) collective-permute-start(bf16[128,1536]{1,0:T(8,128)(2,1)} %collective-permute-done.1.refs_1_), channel_id=1, source_target_pairs={{0,2},{1,15},{2,4},{3,1},{4,6},{5,3},{6,8},{7,5},{8,10},{9,7},{10,... | collective-permute-start | bytes 1179656 | tf_op jit(solution)/shard_map/ppermute | solution.py:522
  23.8 10.3 %collective-permute-start.2 = (bf16[128,1536]{1,0:T(8,128)(2,1)S(1)}, bf16[128,1536]{1,0:T(8,128)(2,1)}, u32[]{:S(2)}, u32[]{:S(2)}) collective-permute-start(bf16[128,1536]{1,0:T(8,128)(2,1)S(1)} %collective-permute-done.refs_0_), channel_id=1, source_target_pairs={{0,1},{1,0},{2,3},{3,2},{4,5},{5,4},{6,7},{7,6},{8,9},{9,8},{10,11... | collective-permute-start | bytes 1179656 | tf_op jit(solution)/shard_map/ppermute | solution.py:515
  23.8 10.3 %collective-permute-start.3 = (bf16[128,1536]{1,0:T(8,128)(2,1)}, bf16[128,1536]{1,0:T(8,128)(2,1)}, u32[]{:S(2)}, u32[]{:S(2)}) collective-permute-start(bf16[128,1536]{1,0:T(8,128)(2,1)} %collective-permute-done.1.refs_1_), channel_id=1, source_target_pairs={{0,1},{1,0},{2,3},{3,2},{4,5},{5,4},{6,7},{7,6},{8,9},{9,8},{10,11... | collective-permute-start | bytes 1179656 | tf_op jit(solution)/shard_map/ppermute | solution.py:515
  24.3 6.2 %copy-start.16 = (bf16[1,1440]{1,0:T(2,128)(2,1)S(1)}, bf16[1,1440]{1,0:T(2,128)(2,1)}, u32[]{:S(2)}) copy-start(bf16[1,1440]{1,0:T(2,128)(2,1)} %param.22) | copy-start | bytes 8644
  24.4 9.8 %copy-start.10 = (bf16[3,1440,1024]{2,1,0:T(8,128)(2,1)S(1)}, bf16[3,1440,1024]{2,1,0:T(8,128)(2,1)}, u32[]{:S(2)}) copy-start(bf16[3,1440,1024]{2,1,0:T(8,128)(2,1)} %get-tuple-element.38.refs_6_.refs_4_) | copy-start | bytes 26542084
  24.4 9.8 %copy-start.14 = (f32[3,1,1024]{2,1,0:T(1,128)S(1)}, f32[3,1,1024]{2,1,0:T(1,128)}, u32[]{:S(2)}) copy-start(f32[3,1,1024]{2,1,0:T(1,128)} %get-tuple-element.40.refs_8_.refs_6_) | copy-start | bytes 36868
  30.6 15.1 %collective-permute-start.9 = (bf16[128,1536]{1,0:T(8,128)(2,1)}, bf16[128,1536]{1,0:T(8,128)(2,1)S(1)}, u32[]{:S(2)}, u32[]{:S(2)}) collective-permute-start(bf16[128,1536]{1,0:T(8,128)(2,1)} %collective-permute-done.5.refs_0_), channel_id=1, source_target_pairs={{0,2},{1,15},{2,4},{3,1},{4,6},{5,3},{6,8},{7,5},{8,10},{9,7},{10,... | collective-permute-start | bytes 1179656 | tf_op jit(solution)/shard_map/ppermute | solution.py:522
  31.3 15.5 %collective-permute-start.7 = (bf16[128,1536]{1,0:T(8,128)(2,1)}, bf16[128,1536]{1,0:T(8,128)(2,1)S(1)}, u32[]{:S(2)}, u32[]{:S(2)}) collective-permute-start(bf16[128,1536]{1,0:T(8,128)(2,1)} %collective-permute-done.5.refs_0_), channel_id=1, source_target_pairs={{0,1},{1,0},{2,3},{3,2},{4,5},{5,4},{6,7},{7,6},{8,9},{9,8},{10,11... | collective-permute-start | bytes 1179656 | tf_op jit(solution)/shard_map/ppermute | solution.py:515
  31.3 15.5 %collective-permute-start.8 = (bf16[128,1536]{1,0:T(8,128)(2,1)}, bf16[128,1536]{1,0:T(8,128)(2,1)S(1)}, u32[]{:S(2)}, u32[]{:S(2)}) collective-permute-start(bf16[128,1536]{1,0:T(8,128)(2,1)} %collective-permute-done.6.refs_1_), channel_id=1, source_target_pairs={{0,1},{1,0},{2,3},{3,2},{4,5},{5,4},{6,7},{7,6},{8,9},{9,8},{10,11... | collective-permute-start | bytes 1179656 | tf_op jit(solution)/shard_map/ppermute | solution.py:515
  34.1 12.7 %collective-permute-start.11 = (bf16[128,1536]{1,0:T(8,128)(2,1)}, bf16[128,1536]{1,0:T(8,128)(2,1)S(1)}, u32[]{:S(2)}, u32[]{:S(2)}) collective-permute-start(bf16[128,1536]{1,0:T(8,128)(2,1)} %collective-permute-done.6.refs_1_), channel_id=1, source_target_pairs={{0,2},{1,15},{2,4},{3,1},{4,6},{5,3},{6,8},{7,5},{8,10},{9,7},{10,... | collective-permute-start | bytes 1179656 | tf_op jit(solution)/shard_map/ppermute | solution.py:522
  34.1 1.0 copy-start.12
  45.0 0.7 copy-start.8
  45.7 9.2 %collective-permute-start.10 = (bf16[128,1536]{1,0:T(8,128)(2,1)S(1)}, bf16[128,1536]{1,0:T(8,128)(2,1)S(1)}, u32[]{:S(2)}, u32[]{:S(2)}) collective-permute-start(bf16[128,1536]{1,0:T(8,128)(2,1)S(1)} %collective-permute-done.9.refs_1_), channel_id=1, source_target_pairs={{0,2},{1,15},{2,4},{3,1},{4,6},{5,3},{6,8},{7,5},{8,10},{9,7},{10,... | collective-permute-start | bytes 1179656 | tf_op jit(solution)/shard_map/ppermute | solution.py:522
  46.1 9.2 %collective-permute-start.13 = (bf16[128,1536]{1,0:T(8,128)(2,1)S(1)}, bf16[128,1536]{1,0:T(8,128)(2,1)S(1)}, u32[]{:S(2)}, u32[]{:S(2)}) collective-permute-start(bf16[128,1536]{1,0:T(8,128)(2,1)S(1)} %collective-permute-done.9.refs_1_), channel_id=1, source_target_pairs={{0,1},{1,0},{2,3},{3,2},{4,5},{5,4},{6,7},{7,6},{8,9},{9,8},{10,11... | collective-permute-start | bytes 1179656 | tf_op jit(solution)/shard_map/ppermute | solution.py:515
  46.8 8.6 %collective-permute-start.14 = (bf16[128,1536]{1,0:T(8,128)(2,1)S(1)}, bf16[128,1536]{1,0:T(8,128)(2,1)S(1)}, u32[]{:S(2)}, u32[]{:S(2)}) collective-permute-start(bf16[128,1536]{1,0:T(8,128)(2,1)S(1)} %collective-permute-done.11.refs_2_), channel_id=1, source_target_pairs={{0,1},{1,0},{2,3},{3,2},{4,5},{5,4},{6,7},{7,6},{8,9},{9,8},{10,11... | collective-permute-start | bytes 1179656 | tf_op jit(solution)/shard_map/ppermute | solution.py:515
  54.1 0.7 copy-start.6
  54.8 0.8 copy-start.13
  54.9 1.8 %collective-permute-start.12 = (bf16[128,1536]{1,0:T(8,128)(2,1)S(1)}, bf16[128,1536]{1,0:T(8,128)(2,1)S(1)}, u32[]{:S(2)}, u32[]{:S(2)}) collective-permute-start(bf16[128,1536]{1,0:T(8,128)(2,1)S(1)} %collective-permute-done.10.refs_0_), channel_id=1, source_target_pairs={{0,1},{1,0},{2,3},{3,2},{4,5},{5,4},{6,7},{7,6},{8,9},{9,8},{10,11... | collective-permute-start | bytes 1179656 | tf_op jit(solution)/shard_map/ppermute | solution.py:515
  65.2 2.1 %collective-permute-start.15 = (bf16[192,1536]{1,0:T(8,128)(2,1)S(1)}, bf16[192,1536]{1,0:T(8,128)(2,1)S(1)}, u32[]{:S(2)}, u32[]{:S(2)}) collective-permute-start(bf16[192,1536]{1,0:T(8,128)(2,1)S(1)} %get-tuple-element.54), channel_id=1, source_target_pairs={{0,1},{1,0},{2,3},{3,2},{4,5},{5,4},{6,7},{7,6},{8,9},{9,8},{10,11... | collective-permute-start | bytes 1769480 | tf_op jit(solution)/shard_map/ppermute | solution.py:515
  68.6 8.2 %collective-permute-start.18 = (f16[128,1536]{1,0:T(8,128)(2,1)}, f16[128,1536]{1,0:T(8,128)(2,1)}, u32[]{:S(2)}, u32[]{:S(2)}) collective-permute-start(f16[128,1536]{1,0:T(8,128)(2,1)} %convert_element_type.52), channel_id=1, source_target_pairs={{0,14},{1,3},{2,0},{3,5},{4,2},{5,7},{6,4},{7,9},{8,6},{9,11},{10,... | collective-permute-start | bytes 1179656 | tf_op jit(solution)/shard_map/ppermute | solution.py:582
  70.0 8.5 %collective-permute-start.17 = (bf16[128,1536]{1,0:T(8,128)(2,1)}, bf16[128,1536]{1,0:T(8,128)(2,1)S(1)}, u32[]{:S(2)}, u32[]{:S(2)}) collective-permute-start(bf16[128,1536]{1,0:T(8,128)(2,1)} %copy-done.13), channel_id=1, source_target_pairs={{0,1},{1,0},{2,3},{3,2},{4,5},{5,4},{6,7},{7,6},{8,9},{9,8},{10,11... | collective-permute-start | bytes 1179656 | tf_op jit(solution)/shard_map/ppermute | solution.py:515
  71.1 11.2 %collective-permute-start.16 = (bf16[192,1536]{1,0:T(8,128)(2,1)S(1)}, bf16[192,1536]{1,0:T(8,128)(2,1)S(1)}, u32[]{:S(2)}, u32[]{:S(2)}) collective-permute-start(bf16[192,1536]{1,0:T(8,128)(2,1)S(1)} %get-tuple-element.58), channel_id=1, source_target_pairs={{0,1},{1,0},{2,3},{3,2},{4,5},{5,4},{6,7},{7,6},{8,9},{9,8},{10,11... | collective-permute-start | bytes 1769480 | tf_op jit(solution)/shard_map/ppermute | solution.py:515
  71.2 9.6 %collective-permute-start.22 = (f16[128,1536]{1,0:T(8,128)(2,1)S(1)}, f16[128,1536]{1,0:T(8,128)(2,1)S(1)}, u32[]{:S(2)}, u32[]{:S(2)}) collective-permute-start(f16[128,1536]{1,0:T(8,128)(2,1)S(1)} %convert_element_type.60), channel_id=1, source_target_pairs={{0,14},{1,3},{2,0},{3,5},{4,2},{5,7},{6,4},{7,9},{8,6},{9,11},{10,... | collective-permute-start | bytes 1179656 | tf_op jit(solution)/shard_map/ppermute | solution.py:582
  76.7 19.3 %copy-start.17 = (bf16[1440]{0:T(1024)(128)(2,1)S(1)}, bf16[1440]{0:T(1024)(128)(2,1)}, u32[]{:S(2)}) copy-start(bf16[1440]{0:T(1024)(128)(2,1)} %param.23) | copy-start | bytes 8644
  77.9 7.9 %collective-permute-start.19 = (f16[128,1536]{1,0:T(8,128)(2,1)S(1)}, f16[128,1536]{1,0:T(8,128)(2,1)S(1)}, u32[]{:S(2)}, u32[]{:S(2)}) collective-permute-start(f16[128,1536]{1,0:T(8,128)(2,1)S(1)} %add_convert_fusion.4), channel_id=1, source_target_pairs={{0,14},{1,3},{2,0},{3,5},{4,2},{5,7},{6,4},{7,9},{8,6},{9,11},{10,... | collective-permute-start | bytes 1179656 | tf_op jit(solution)/shard_map/ppermute | solution.py:582
  78.6 1.0 copy-start.7
  80.9 24.4 %copy-start.4 = (bf16[1440,256]{1,0:T(8,128)(2,1)S(1)}, bf16[1440,256]{1,0:T(8,128)(2,1)}, u32[]{:S(2)}) copy-start(bf16[1440,256]{1,0:T(8,128)(2,1)} %key_ref.1) | copy-start | bytes 2211844
  81.0 24.4 %copy-start.5 = (bf16[1440,256]{1,0:T(8,128)(2,1)S(1)}, bf16[1440,256]{1,0:T(8,128)(2,1)}, u32[]{:S(2)}) copy-start(bf16[1440,256]{1,0:T(8,128)(2,1)} %value_ref.1) | copy-start | bytes 2211844
  81.0 9.0 %collective-permute-start.23 = (f16[128,1536]{1,0:T(8,128)(2,1)S(1)}, f16[128,1536]{1,0:T(8,128)(2,1)S(1)}, u32[]{:S(2)}, u32[]{:S(2)}) collective-permute-start(f16[128,1536]{1,0:T(8,128)(2,1)S(1)} %add_convert_fusion.1), channel_id=1, source_target_pairs={{0,14},{1,3},{2,0},{3,5},{4,2},{5,7},{6,4},{7,9},{8,6},{9,11},{10,... | collective-permute-start | bytes 1179656 | tf_op jit(solution)/shard_map/ppermute | solution.py:582
  82.4 0.9 copy-start.9
  85.9 8.3 %collective-permute-start.20 = (f16[128,1536]{1,0:T(8,128)(2,1)S(1)}, f16[128,1536]{1,0:T(8,128)(2,1)S(1)}, u32[]{:S(2)}, u32[]{:S(2)}) collective-permute-start(f16[128,1536]{1,0:T(8,128)(2,1)S(1)} %add_convert_fusion.3), channel_id=1, source_target_pairs={{0,14},{1,3},{2,0},{3,5},{4,2},{5,7},{6,4},{7,9},{8,6},{9,11},{10,... | collective-permute-start | bytes 1179656 | tf_op jit(solution)/shard_map/ppermute | solution.py:582
  90.8 8.2 %collective-permute-start.24 = (f16[128,1536]{1,0:T(8,128)(2,1)}, f16[128,1536]{1,0:T(8,128)(2,1)S(1)}, u32[]{:S(2)}, u32[]{:S(2)}) collective-permute-start(f16[128,1536]{1,0:T(8,128)(2,1)} %add_convert_fusion), channel_id=1, source_target_pairs={{0,15},{1,2},{2,1},{3,4},{4,3},{5,6},{6,5},{7,8},{8,7},{9,10},{10,... | collective-permute-start | bytes 1179656 | tf_op jit(solution)/shard_map/ppermute | solution.py:582
  95.0 9.1 %collective-permute-start.21 = (f16[128,1536]{1,0:T(8,128)(2,1)}, f16[128,1536]{1,0:T(8,128)(2,1)}, u32[]{:S(2)}, u32[]{:S(2)}) collective-permute-start(f16[128,1536]{1,0:T(8,128)(2,1)} %add_convert_fusion.2), channel_id=1, source_target_pairs={{0,14},{1,3},{2,0},{3,5},{4,2},{5,7},{6,4},{7,9},{8,6},{9,11},{10,... | collective-permute-start | bytes 1179656 | tf_op jit(solution)/shard_map/ppermute | solution.py:582
  105.4 9.8 %copy-start.15 = (f32[32]{0:T(128)S(1)}, f32[32]{0:T(128)}, u32[]{:S(2)}) copy-start(f32[32]{0:T(128)} %sinks_ref.1) | copy-start | bytes 388
  106.8 8.4 %collective-permute-start.25 = (bf16[128,512]{1,0:T(8,128)(2,1)S(1)}, bf16[128,512]{1,0:T(8,128)(2,1)S(1)}, u32[]{:S(2)}, u32[]{:S(2)}) collective-permute-start(bf16[128,512]{1,0:T(8,128)(2,1)S(1)} %get-tuple-element.71.own_ref), channel_id=1, source_target_pairs={{0,1},{1,2},{2,3},{3,4},{4,5},{5,6},{6,7},{7,8},{8,9},{9,10},{10,1... | collective-permute-start | bytes 393224 | tf_op jit(solution)/shard_map/ppermute | solution.py:597
  109.7 2.7 %copy-start.1 = (bf16[1440,2048]{1,0:T(8,128)(2,1)S(1)}, bf16[1440,2048]{1,0:T(8,128)(2,1)}, u32[]{:S(2)}) copy-start(bf16[1440,2048]{1,0:T(8,128)(2,1)} %weight_ref.1) | copy-start | bytes 17694724

commit v4 on v2

--- a/solution.py
+++ b/solution.py
@@ -349,9 +349,12 @@
 def mix_kernel(
     tokens_ref, mixture_ref, gain_ref, key_ref, value_ref, cos_ref, sin_ref, out_ref, normed_ref, kv_ref
 ):
-    block_out = (tokens_ref[:, :1440].astype(F32) + mixture_ref[...]).astype(BF16)
-    out_ref[...] = block_out
-    widened = block_out.astype(F32)
+    rounded = (tokens_ref[...].astype(F32) + mixture_ref[...]).astype(BF16).astype(F32)
+    for place in range(11):
+        rows = slice(128 * place, 128 * place + 128)
+        out_ref[rows, :] = rounded[:, rows].T.astype(BF16)
+    out_ref[1408:, :] = rounded[:, 1408:].T[:32].astype(BF16)
+    widened = rounded[:, :1440]
     squares = jnp.sum(widened * widened, axis=1, keepdims=True) / 1440.0
     normed = (widened * lax.rsqrt(squares + 1e-05) * gain_ref[...].astype(F32)).astype(BF16)
     normed_ref[...] = normed
@@ -364,7 +367,7 @@
     return pl.pallas_call(
         mix_kernel,
         out_shape=[
-            jax.ShapeDtypeStruct((128, 1440), BF16),
+            jax.ShapeDtypeStruct((1440, 128), BF16),
             jax.ShapeDtypeStruct((128, 1440), BF16),
             jax.ShapeDtypeStruct((128, 512), BF16),
         ],
@@ -447,7 +450,7 @@
                 weights = jnp.exp(part - top)
                 whole = jnp.exp(sink - top) + jnp.sum(weights, axis=1, keepdims=True)
                 halves.append(weights * (1.0 / whole))
-            probs = jnp.where(allowed, jnp.concatenate(halves, axis=1), 0.0)
+            probs = jnp.concatenate(halves, axis=1)
             here_probs.append(jnp.where(mine, probs, 0.0).astype(BF16))
             there_probs.append(jnp.where(mine, 0.0, probs).astype(BF16))
         mixed = jnp.dot(
@@ -583,7 +586,7 @@
     from_cross = onward(cross_near[2] + from_cross, False)
     from_same = onward(same_near[1] + from_same, False)
     from_cross = onward(cross_near[1] + from_cross, True)
-    mixture = (own + from_same + from_cross)[:, :width] * (1.0 / RETURN_SCALE)
+    mixture = (own + from_same + from_cross) * (1.0 / RETURN_SCALE)
 
     block_out, normed, own_kv = mix(
         packed, mixture, attn_gain[None], key_matrix, value_matrix, cosine, sine_part
@@ -592,7 +595,7 @@
     halo_kv = lax.ppermute(own_kv, "expert", ahead)
     query = queries(normed, query_weight, cosine, sine_part)
     attended = attend(device_index.reshape(1), sinks, query, own_kv, halo_kv)
-    return (block_out, attended)
+    return (block_out.T, attended)
 
 
 def solution(mesh):

time: 121 us -> 120 us (level)
    unnamed x27 -> x26, local copies, waits for them, and re-layouts: 8.08 us -> 7.15 us
where the time goes in v4:
time: 120 us; the launch traced here: 119 us
  Pallas kernels  52.3 us (44%)
  waiting for transfers between devices  29.6 us (25%)
  starting transfers between devices  23.2 us (19%)
  local copies, waits for them, and re-layouts  7.33 us (6%)
  other arithmetic  5.47 us (5%)
    ppermute x7, waiting for transfers between devices, onward(): return lax.ppermute(block.astype(jnp.float16), 'expert', route).astype(F32)  26.6 us
    pallas_call x3, Pallas kernels, run_experts(): pl.pallas_call(functools.partial(expert_kernel, count), grid_spec=pltpu.P...  25 us
    pallas_call x1, Pallas kernels, decode_up(): pl.pallas_call(decode_up_kernel, grid=(CHUNKS,), in_specs=[pl.BlockSpec((...  10.1 us
    ppermute x7, starting transfers between devices, inward(): return lax.ppermute(block, 'expert', route)  10.1 us
    ppermute x11, starting transfers between devices, swap(): return lax.ppermute(block, 'expert', partner)  8.13 us
    unnamed x26, local copies, waits for them, and re-layouts  7.15 us
    pallas_call x1, Pallas kernels, decode_down(): pl.pallas_call(decode_down_kernel, grid=(CHUNKS,), in_specs=[pl.BlockSpec...  5.57 us
    pallas_call x1, Pallas kernels, attend(): pl.pallas_call(attend_kernel, in_specs=[pl.BlockSpec(memory_space=pltpu.S...  4.04 us
  transfers between devices with their start and end apart: 26, of which 9 were waited for; matrix products, arithmetic and copies ran while one was open for 6% of the time, Pallas kernels for 30%

profile of v4, /device:TPU:1, one launch (start us, length us, event | category | flops | bytes accessed | tf_op | source)
XLA Modules:
  0.0 118.8 jit_solution(9213793002061369049)
XLA Ops:
  0.6 2.1 %pack.1.refs_2_.tokens_ref = bf16[128,1536]{1,0:T(8,128)(2,1)} custom-call(bf16[1440,128]{1,0:T(8,128)(2,1)} %bitcast.23, s32[4,128]{1,0:T(4,128)} %bitcast.25, s32[4,128]{1,0:T(4,128)} %bitcast.26), custom_call_target="tpu_custom_call" | custom-call | tf_op jit(solution)/shard_map/pack/pallas_call | solution.py:178
  2.8 6.4 %collective-permute-start = (bf16[128,1536]{1,0:T(8,128)(2,1)}, bf16[128,1536]{1,0:T(8,128)(2,1)}, u32[]{:S(2)}, u32[]{:S(2)}) collective-permute-start(bf16[128,1536]{1,0:T(8,128)(2,1)} %pack.1.refs_2_.tokens_ref), channel_id=1, source_target_pairs={{0,2},{1,15},{2,4},{3,1},{4,6},{5,3},{6,8},{7,5},{8,10},{9,7},{10,... | collective-permute-start | bytes 1179656 | tf_op jit(solution)/shard_map/ppermute | solution.py:522
  9.2 1.9 %copy.27 = s32[1,45,2880]{2,1,0:T(8,128)} copy(s32[1,45,2880]{2,0,1:T(1,128)} %param.18) | data formatting | bytes 1036800
  11.1 10.1 %decode_up.1 = (bf16[3,1440,1024]{2,1,0:T(8,128)(2,1)}, f32[3,1,1024]{2,1,0:T(1,128)}) custom-call(s32[1440,720]{1,0:T(8,128)} %bitcast.21, s32[45,2880]{1,0:T(8,128)} %bitcast.22, bf16[1,2880]{1,0:T(2,128)(2,1)} %bias_ref.1), custom_call_target="tpu_custom_call" | custom-call | flops 60000000 | bytes 30000000 | tf_op jit(solution)/shard_map/decode_up/pallas_call | solution.py:70
  21.2 0.8 collective-permute-start.5
  22.0 1.4 %collective-permute-start.4 = (bf16[128,1536]{1,0:T(8,128)(2,1)S(1)}, bf16[128,1536]{1,0:T(8,128)(2,1)}, u32[]{:S(2)}, u32[]{:S(2)}) collective-permute-start(bf16[128,1536]{1,0:T(8,128)(2,1)S(1)} %copy-done.2), channel_id=1, source_target_pairs={{0,1},{1,0},{2,3},{3,2},{4,5},{5,4},{6,7},{7,6},{8,9},{9,8},{10,11... | collective-permute-start | bytes 1179656 | tf_op jit(solution)/shard_map/ppermute | solution.py:515
  23.4 1.9 %collective-permute-start.6 = (bf16[128,1536]{1,0:T(8,128)(2,1)}, bf16[128,1536]{1,0:T(8,128)(2,1)S(1)}, u32[]{:S(2)}, u32[]{:S(2)}) collective-permute-start(bf16[128,1536]{1,0:T(8,128)(2,1)} %collective-permute-done.1.refs_1_), channel_id=1, source_target_pairs={{0,2},{1,15},{2,4},{3,1},{4,6},{5,3},{6,8},{7,5},{8,10},{9,7},{10,... | collective-permute-start | bytes 1179656 | tf_op jit(solution)/shard_map/ppermute | solution.py:522
  25.4 0.5 collective-permute-start.3
  25.9 0.1 pad_add_fusion.place_ref
  26.0 1.0 copy.28
  27.0 0.0 copy-start.10
  27.0 5.6 %decode_down.1.refs_7_.refs_5_ = bf16[3,512,1536]{2,1,0:T(8,128)(2,1)S(1)} custom-call(s32[1440,360]{1,0:T(8,128)S(1)} %bitcast.15, s32[1440,360]{1,0:T(8,128)S(1)} %bitcast.16, s32[1440,360]{1,0:T(8,128)S(1)} %bitcast.17, s32[45,1440]{1,0:T(8,128)S(1)} %bitcast.18, s32[45,1440]{1,0:T(8,128)S(1)} %bitcast.19, s32[45,1440]{1,0:T(8,128)S(1)} %bitcast.20), custom_call_target="tpu_custom_call" | custom-call | flops 60000000 | bytes 20000000 | tf_op jit(solution)/shard_map/decode_down/pallas_call | solution.py:125
  32.6 0.7 collective-permute-start.9
  33.3 2.5 %collective-permute-start.8 = (bf16[128,1536]{1,0:T(8,128)(2,1)S(1)}, bf16[128,1536]{1,0:T(8,128)(2,1)S(1)}, u32[]{:S(2)}, u32[]{:S(2)}) collective-permute-start(bf16[128,1536]{1,0:T(8,128)(2,1)S(1)} %collective-permute-done.6.refs_1_), channel_id=1, source_target_pairs={{0,1},{1,0},{2,3},{3,2},{4,5},{5,4},{6,7},{7,6},{8,9},{9,8},{10,11... | collective-permute-start | bytes 1179656 | tf_op jit(solution)/shard_map/ppermute | solution.py:515
  35.8 0.1 collective-permute-start.11
  35.9 10.1 %experts.3 = (bf16[192,1536]{1,0:T(8,128)(2,1)S(1)}, bf16[192,1536]{1,0:T(8,128)(2,1)S(1)}, bf16[3,128,256]{2,1,0:T(8,128)(2,1)S(1)}) custom-call(s32[2]{0:T(128)S(1)} %pad_add_fusion.place_ref, bf16[128,1536]{1,0:T(8,128)(2,1)} %collective-permute-done.refs_0_, bf16[128,1536]{1,0:T(8,128)(2,1)} %collective-permute-done.1.refs_1_, ...), custom_call_target="tpu_custom_call" | custom-call | flops 9555148800 | bytes 30000000 | tf_op jit(solution)/shard_map/experts/pallas_call | solution.py:288
  46.1 0.8 copy-done.6
  46.9 0.2 collective-permute-start.10
  47.1 1.1 collective-permute-start.13
  48.2 6.2 %experts.4 = (bf16[128,1536]{1,0:T(8,128)(2,1)S(1)}, bf16[128,1536]{1,0:T(8,128)(2,1)S(1)}, bf16[2,128,256]{2,1,0:T(8,128)(2,1)S(1)}) custom-call(s32[2]{0:T(128)S(1)} %pad_add_fusion.place_ref, bf16[128,1536]{1,0:T(8,128)(2,1)S(1)} %collective-permute-done.5.refs_0_, bf16[128,1536]{1,0:T(8,128)(2,1)S(1)} %collective-permute-done.6.refs_1_, ...), custom_call_target="tpu_custom_call" | custom-call | flops 6370099200 | bytes 30000000 | tf_op jit(solution)/shard_map/experts/pallas_call | solution.py:288
  54.4 0.0 copy-start.7
  54.4 0.7 copy-done.7
  55.2 0.6 collective-permute-start.12
  55.8 1.3 %collective-permute-done.12.refs_3_ = bf16[128,1536]{1,0:T(8,128)(2,1)S(1)} collective-permute-done((bf16[128,1536]{1,0:T(8,128)(2,1)S(1)}, bf16[128,1536]{1,0:T(8,128)(2,1)S(1)}, u32[]{:S(2)}, u32[]{:S(2)}) %collective-permute-start.12) | collective-permute-done | bytes 393248 | tf_op jit(solution)/shard_map/ppermute | solution.py:515
  57.2 8.6 %experts.5 = (bf16[192,1536]{1,0:T(8,128)(2,1)S(1)}, bf16[192,1536]{1,0:T(8,128)(2,1)S(1)}, bf16[3,128,256]{2,1,0:T(8,128)(2,1)S(1)}) custom-call(s32[2]{0:T(128)S(1)} %pad_add_fusion.place_ref, bf16[128,1536]{1,0:T(8,128)(2,1)S(1)} %collective-permute-done.10.refs_0_, bf16[128,1536]{1,0:T(8,128)(2,1)S(1)} %collective-permute-done.9.refs_1_, ...), custom_call_target="tpu_custom_call" | custom-call | flops 9555148800 | bytes 30000000 | tf_op jit(solution)/shard_map/experts/pallas_call | solution.py:288
  65.8 0.5 collective-permute-start.15
  66.3 1.6 %collective-permute-done.15.other_ref = bf16[192,1536]{1,0:T(8,128)(2,1)S(1)} collective-permute-done((bf16[192,1536]{1,0:T(8,128)(2,1)S(1)}, bf16[192,1536]{1,0:T(8,128)(2,1)S(1)}, u32[]{:S(2)}, u32[]{:S(2)}) %collective-permute-start.15) | collective-permute-done | bytes 589856 | tf_op jit(solution)/shard_map/ppermute | solution.py:515
  67.9 0.5 combine.3
  68.4 0.8 convert_element_type.52
  69.2 1.0 collective-permute-start.18
  70.3 1.3 %collective-permute-start.17 = (bf16[128,1536]{1,0:T(8,128)(2,1)}, bf16[128,1536]{1,0:T(8,128)(2,1)S(1)}, u32[]{:S(2)}, u32[]{:S(2)}) collective-permute-start(bf16[128,1536]{1,0:T(8,128)(2,1)} %copy-done.7), channel_id=1, source_target_pairs={{0,1},{1,0},{2,3},{3,2},{4,5},{5,4},{6,7},{7,6},{8,9},{9,8},{10,11... | collective-permute-start | bytes 1179656 | tf_op jit(solution)/shard_map/ppermute | solution.py:515
  71.6 0.1 collective-permute-start.16
  71.7 0.2 collective-permute-start.22
  71.9 5.5 %collective-permute-done.18 = f16[128,1536]{1,0:T(8,128)(2,1)} collective-permute-done((f16[128,1536]{1,0:T(8,128)(2,1)}, f16[128,1536]{1,0:T(8,128)(2,1)}, u32[]{:S(2)}, u32[]{:S(2)}) %collective-permute-start.18) | collective-permute-done | bytes 393248 | tf_op jit(solution)/shard_map/ppermute | solution.py:580
  77.3 1.1 add_convert_fusion.4
  78.5 0.2 collective-permute-start.19
  78.7 0.4 combine.5
  79.0 2.4 %collective-permute-done.22 = f16[128,1536]{1,0:T(8,128)(2,1)S(1)} collective-permute-done((f16[128,1536]{1,0:T(8,128)(2,1)S(1)}, f16[128,1536]{1,0:T(8,128)(2,1)S(1)}, u32[]{:S(2)}, u32[]{:S(2)}) %collective-permute-start.22) | collective-permute-done | bytes 393248 | tf_op jit(solution)/shard_map/ppermute | solution.py:580
  81.5 0.1 add_convert_fusion.1
  81.6 0.0 copy-start.4
  81.6 0.2 collective-permute-start.23
  81.8 0.5 combine.4
  82.3 4.1 %collective-permute-done.19 = f16[128,1536]{1,0:T(8,128)(2,1)S(1)} collective-permute-done((f16[128,1536]{1,0:T(8,128)(2,1)S(1)}, f16[128,1536]{1,0:T(8,128)(2,1)S(1)}, u32[]{:S(2)}, u32[]{:S(2)}) %collective-permute-start.19) | collective-permute-done | bytes 393248 | tf_op jit(solution)/shard_map/ppermute | solution.py:580
  86.4 0.1 add_convert_fusion.3
  86.5 0.1 collective-permute-start.20
  86.6 4.0 %collective-permute-done.23 = f16[128,1536]{1,0:T(8,128)(2,1)S(1)} collective-permute-done((f16[128,1536]{1,0:T(8,128)(2,1)S(1)}, f16[128,1536]{1,0:T(8,128)(2,1)S(1)}, u32[]{:S(2)}, u32[]{:S(2)}) %collective-permute-start.23) | collective-permute-done | bytes 393248 | tf_op jit(solution)/shard_map/ppermute | solution.py:580
  90.6 0.8 add_convert_fusion
  91.4 1.2 collective-permute-start.24
  92.6 2.2 %collective-permute-done.20 = f16[128,1536]{1,0:T(8,128)(2,1)S(1)} collective-permute-done((f16[128,1536]{1,0:T(8,128)(2,1)S(1)}, f16[128,1536]{1,0:T(8,128)(2,1)S(1)}, u32[]{:S(2)}, u32[]{:S(2)}) %collective-permute-start.20) | collective-permute-done | bytes 393248 | tf_op jit(solution)/shard_map/ppermute | solution.py:580
  94.8 0.8 add_convert_fusion.2
  95.6 0.3 fusion
  96.0 0.1 copy.20
  96.0 0.1 copy.21.cos_ref
  96.2 0.1 pad_maximum_fusion.sin_ref
  96.3 2.8 %collective-permute-done.24 = f16[128,1536]{1,0:T(8,128)(2,1)S(1)} collective-permute-done((f16[128,1536]{1,0:T(8,128)(2,1)}, f16[128,1536]{1,0:T(8,128)(2,1)S(1)}, u32[]{:S(2)}, u32[]{:S(2)}) %collective-permute-start.24) | collective-permute-done | bytes 393248 | tf_op jit(solution)/shard_map/ppermute | solution.py:580
  99.1 5.5 %collective-permute-done.21 = f16[128,1536]{1,0:T(8,128)(2,1)} collective-permute-done((f16[128,1536]{1,0:T(8,128)(2,1)}, f16[128,1536]{1,0:T(8,128)(2,1)}, u32[]{:S(2)}, u32[]{:S(2)}) %collective-permute-start.21) | collective-permute-done | bytes 393248 | tf_op jit(solution)/shard_map/ppermute | solution.py:580
  104.7 1.1 add_multiply_fusion.mixture_ref
  105.8 0.0 copy-start.9
  105.8 1.3 %mix.1 = (bf16[1440,128]{1,0:T(8,128)(2,1)}, bf16[128,1440]{1,0:T(8,128)(2,1)S(1)}, bf16[128,512]{1,0:T(8,128)(2,1)S(1)}) custom-call(bf16[128,1536]{1,0:T(8,128)(2,1)S(1)} %copy-done.2, f32[128,1536]{1,0:T(8,128)S(1)} %add_multiply_fusion.mixture_ref, bf16[1,1440]{1,0:T(2,128)(2,1)S(1)} %broadcast_in_dim.2.gain_ref, bf16[1440,256]{1,0:T(8,128)(2,1)S(1)} %copy-done.3, ...), custom_call_target="tpu_custom_call" | custom-call | flops 188743680 | bytes 3000000 | tf_op jit(solution)/shard_map/mix/pallas_call | solution.py:367
  107.2 2.1 %collective-permute-start.25 = (bf16[128,512]{1,0:T(8,128)(2,1)S(1)}, bf16[128,512]{1,0:T(8,128)(2,1)S(1)}, u32[]{:S(2)}, u32[]{:S(2)}) collective-permute-start(bf16[128,512]{1,0:T(8,128)(2,1)S(1)} %get-tuple-element.71.own_ref), channel_id=1, source_target_pairs={{0,1},{1,2},{2,3},{3,4},{4,5},{5,6},{6,7},{7,8},{8,9},{9,10},{10,1... | collective-permute-start | bytes 393224 | tf_op jit(solution)/shard_map/ppermute | solution.py:595
  109.3 0.0 copy-start.1
  109.3 2.7 %copy-done.1 = bf16[1440,2048]{1,0:T(8,128)(2,1)S(1)} copy-done((bf16[1440,2048]{1,0:T(8,128)(2,1)S(1)}, bf16[1440,2048]{1,0:T(8,128)(2,1)}, u32[]{:S(2)}) %copy-start.1) | copy-done | bytes 5898264
  112.0 2.7 %queries.1.queries_ref = bf16[4,512,128]{2,1,0:T(8,128)(2,1)S(1)} custom-call(bf16[128,1440]{1,0:T(8,128)(2,1)S(1)} %get-tuple-element.70.normed_ref, bf16[1440,2048]{1,0:T(8,128)(2,1)S(1)} %copy-done.1, f32[128,128]{1,0:T(8,128)S(1)} %copy.21.cos_ref, f32[128,128]{1,0:T(8,128)S(1)} %pad_maximum_fusion.sin_ref), custom_call_target="tpu_custom_call" | custom-call | flops 754974720 | bytes 7000000 | tf_op jit(solution)/shard_map/queries/pallas_call | solution.py:391
  114.8 4.0 %attend.1 = bf16[128,2048]{1,0:T(8,128)(2,1)} custom-call(s32[1]{0:T(128)} %bitcast.3.index_ref, f32[32]{0:T(128)S(1)} %copy-done.9, bf16[4,512,128]{2,1,0:T(8,128)(2,1)S(1)} %queries.1.queries_ref, bf16[128,512]{1,0:T(8,128)(2,1)S(1)} %get-tuple-element.71.own_ref, bf16[128,512]{1,0:T(8,128)(2,1)S(1)} %collective-permute-done.25.halo_ref), custom_call_target="tpu_custom_call" | custom-call | flops 268435456 | bytes 1500000 | tf_op jit(solution)/shard_map/attend/pallas_call | solution.py:471
  (44 shorter events, 0.2 us)
Async XLA Ops:
  0.6 26.3 %copy-start = (s32[1,1440,360]{2,1,0:T(8,128)S(1)}, s32[1,1440,360]{2,1,0:T(8,128)}, u32[]{:S(2)}) copy-start(s32[1,1440,360]{2,1,0:T(8,128)} %param.20) | copy-start | bytes 6220804
  2.8 19.3 %copy-start.2 = (bf16[128,1536]{1,0:T(8,128)(2,1)S(1)}, bf16[128,1536]{1,0:T(8,128)(2,1)}, u32[]{:S(2)}) copy-start(bf16[128,1536]{1,0:T(8,128)(2,1)} %pack.1.refs_2_.tokens_ref) | copy-start | bytes 1179652
  2.8 18.5 %collective-permute-start = (bf16[128,1536]{1,0:T(8,128)(2,1)}, bf16[128,1536]{1,0:T(8,128)(2,1)}, u32[]{:S(2)}, u32[]{:S(2)}) collective-permute-start(bf16[128,1536]{1,0:T(8,128)(2,1)} %pack.1.refs_2_.tokens_ref), channel_id=1, source_target_pairs={{0,2},{1,15},{2,4},{3,1},{4,6},{5,3},{6,8},{7,5},{8,10},{9,7},{10,... | collective-permute-start | bytes 1179656 | tf_op jit(solution)/shard_map/ppermute | solution.py:522
  9.2 14.3 %collective-permute-start.1 = (bf16[128,1536]{1,0:T(8,128)(2,1)}, bf16[128,1536]{1,0:T(8,128)(2,1)}, u32[]{:S(2)}, u32[]{:S(2)}) collective-permute-start(bf16[128,1536]{1,0:T(8,128)(2,1)} %pack.1.refs_2_.tokens_ref), channel_id=1, source_target_pairs={{1,2},{0,15},{3,4},{2,1},{5,6},{4,3},{7,8},{6,5},{9,10},{8,7},{11,... | collective-permute-start | bytes 1179656 | tf_op jit(solution)/shard_map/ppermute | solution.py:522
  21.2 11.4 %collective-permute-start.5 = (bf16[128,1536]{1,0:T(8,128)(2,1)}, bf16[128,1536]{1,0:T(8,128)(2,1)S(1)}, u32[]{:S(2)}, u32[]{:S(2)}) collective-permute-start(bf16[128,1536]{1,0:T(8,128)(2,1)} %collective-permute-done.refs_0_), channel_id=1, source_target_pairs={{0,2},{1,15},{2,4},{3,1},{4,6},{5,3},{6,8},{7,5},{8,10},{9,7},{10,... | collective-permute-start | bytes 1179656 | tf_op jit(solution)/shard_map/ppermute | solution.py:522
  22.0 11.3 %collective-permute-start.4 = (bf16[128,1536]{1,0:T(8,128)(2,1)S(1)}, bf16[128,1536]{1,0:T(8,128)(2,1)}, u32[]{:S(2)}, u32[]{:S(2)}) collective-permute-start(bf16[128,1536]{1,0:T(8,128)(2,1)S(1)} %copy-done.2), channel_id=1, source_target_pairs={{0,1},{1,0},{2,3},{3,2},{4,5},{5,4},{6,7},{7,6},{8,9},{9,8},{10,11... | collective-permute-start | bytes 1179656 | tf_op jit(solution)/shard_map/ppermute | solution.py:515
  23.4 9.8 %collective-permute-start.6 = (bf16[128,1536]{1,0:T(8,128)(2,1)}, bf16[128,1536]{1,0:T(8,128)(2,1)S(1)}, u32[]{:S(2)}, u32[]{:S(2)}) collective-permute-start(bf16[128,1536]{1,0:T(8,128)(2,1)} %collective-permute-done.1.refs_1_), channel_id=1, source_target_pairs={{0,2},{1,15},{2,4},{3,1},{4,6},{5,3},{6,8},{7,5},{8,10},{9,7},{10,... | collective-permute-start | bytes 1179656 | tf_op jit(solution)/shard_map/ppermute | solution.py:522
  25.4 10.5 %collective-permute-start.2 = (bf16[128,1536]{1,0:T(8,128)(2,1)}, bf16[128,1536]{1,0:T(8,128)(2,1)}, u32[]{:S(2)}, u32[]{:S(2)}) collective-permute-start(bf16[128,1536]{1,0:T(8,128)(2,1)} %collective-permute-done.refs_0_), channel_id=1, source_target_pairs={{0,1},{1,0},{2,3},{3,2},{4,5},{5,4},{6,7},{7,6},{8,9},{9,8},{10,11... | collective-permute-start | bytes 1179656 | tf_op jit(solution)/shard_map/ppermute | solution.py:515
  25.4 10.5 %collective-permute-start.3 = (bf16[128,1536]{1,0:T(8,128)(2,1)}, bf16[128,1536]{1,0:T(8,128)(2,1)}, u32[]{:S(2)}, u32[]{:S(2)}) collective-permute-start(bf16[128,1536]{1,0:T(8,128)(2,1)} %collective-permute-done.1.refs_1_), channel_id=1, source_target_pairs={{0,1},{1,0},{2,3},{3,2},{4,5},{5,4},{6,7},{7,6},{8,9},{9,8},{10,11... | collective-permute-start | bytes 1179656 | tf_op jit(solution)/shard_map/ppermute | solution.py:515
  27.0 5.6 %copy-start.10 = (bf16[1,1440]{1,0:T(2,128)(2,1)S(1)}, bf16[1,1440]{1,0:T(2,128)(2,1)}, u32[]{:S(2)}) copy-start(bf16[1,1440]{1,0:T(2,128)(2,1)} %param.22) | copy-start | bytes 8644
  27.0 9.0 %copy-start.5 = (bf16[3,1440,1024]{2,1,0:T(8,128)(2,1)S(1)}, bf16[3,1440,1024]{2,1,0:T(8,128)(2,1)}, u32[]{:S(2)}) copy-start(bf16[3,1440,1024]{2,1,0:T(8,128)(2,1)} %get-tuple-element.38.refs_6_.refs_4_) | copy-start | bytes 26542084
  27.0 9.0 %copy-start.8 = (f32[3,1,1024]{2,1,0:T(1,128)S(1)}, f32[3,1,1024]{2,1,0:T(1,128)}, u32[]{:S(2)}) copy-start(f32[3,1,1024]{2,1,0:T(1,128)} %get-tuple-element.40.refs_8_.refs_6_) | copy-start | bytes 36868
  32.6 14.3 %collective-permute-start.9 = (bf16[128,1536]{1,0:T(8,128)(2,1)S(1)}, bf16[128,1536]{1,0:T(8,128)(2,1)S(1)}, u32[]{:S(2)}, u32[]{:S(2)}) collective-permute-start(bf16[128,1536]{1,0:T(8,128)(2,1)S(1)} %collective-permute-done.5.refs_0_), channel_id=1, source_target_pairs={{0,2},{1,15},{2,4},{3,1},{4,6},{5,3},{6,8},{7,5},{8,10},{9,7},{10,... | collective-permute-start | bytes 1179656 | tf_op jit(solution)/shard_map/ppermute | solution.py:522
  33.3 14.9 %collective-permute-start.7 = (bf16[128,1536]{1,0:T(8,128)(2,1)S(1)}, bf16[128,1536]{1,0:T(8,128)(2,1)S(1)}, u32[]{:S(2)}, u32[]{:S(2)}) collective-permute-start(bf16[128,1536]{1,0:T(8,128)(2,1)S(1)} %collective-permute-done.5.refs_0_), channel_id=1, source_target_pairs={{0,1},{1,0},{2,3},{3,2},{4,5},{5,4},{6,7},{7,6},{8,9},{9,8},{10,11... | collective-permute-start | bytes 1179656 | tf_op jit(solution)/shard_map/ppermute | solution.py:515
  33.3 14.9 %collective-permute-start.8 = (bf16[128,1536]{1,0:T(8,128)(2,1)S(1)}, bf16[128,1536]{1,0:T(8,128)(2,1)S(1)}, u32[]{:S(2)}, u32[]{:S(2)}) collective-permute-start(bf16[128,1536]{1,0:T(8,128)(2,1)S(1)} %collective-permute-done.6.refs_1_), channel_id=1, source_target_pairs={{0,1},{1,0},{2,3},{3,2},{4,5},{5,4},{6,7},{7,6},{8,9},{9,8},{10,11... | collective-permute-start | bytes 1179656 | tf_op jit(solution)/shard_map/ppermute | solution.py:515
  35.8 12.3 %collective-permute-start.11 = (bf16[128,1536]{1,0:T(8,128)(2,1)S(1)}, bf16[128,1536]{1,0:T(8,128)(2,1)S(1)}, u32[]{:S(2)}, u32[]{:S(2)}) collective-permute-start(bf16[128,1536]{1,0:T(8,128)(2,1)S(1)} %collective-permute-done.6.refs_1_), channel_id=1, source_target_pairs={{0,2},{1,15},{2,4},{3,1},{4,6},{5,3},{6,8},{7,5},{8,10},{9,7},{10,... | collective-permute-start | bytes 1179656 | tf_op jit(solution)/shard_map/ppermute | solution.py:522
  46.1 0.8 copy-start.6
  46.9 8.3 %collective-permute-start.10 = (bf16[128,1536]{1,0:T(8,128)(2,1)S(1)}, bf16[128,1536]{1,0:T(8,128)(2,1)S(1)}, u32[]{:S(2)}, u32[]{:S(2)}) collective-permute-start(bf16[128,1536]{1,0:T(8,128)(2,1)S(1)} %collective-permute-done.9.refs_1_), channel_id=1, source_target_pairs={{0,2},{1,15},{2,4},{3,1},{4,6},{5,3},{6,8},{7,5},{8,10},{9,7},{10,... | collective-permute-start | bytes 1179656 | tf_op jit(solution)/shard_map/ppermute | solution.py:522
  47.1 8.8 %collective-permute-start.13 = (bf16[128,1536]{1,0:T(8,128)(2,1)S(1)}, bf16[128,1536]{1,0:T(8,128)(2,1)S(1)}, u32[]{:S(2)}, u32[]{:S(2)}) collective-permute-start(bf16[128,1536]{1,0:T(8,128)(2,1)S(1)} %collective-permute-done.9.refs_1_), channel_id=1, source_target_pairs={{0,1},{1,0},{2,3},{3,2},{4,5},{5,4},{6,7},{7,6},{8,9},{9,8},{10,11... | collective-permute-start | bytes 1179656 | tf_op jit(solution)/shard_map/ppermute | solution.py:515
  48.2 7.7 %collective-permute-start.14 = (bf16[128,1536]{1,0:T(8,128)(2,1)S(1)}, bf16[128,1536]{1,0:T(8,128)(2,1)S(1)}, u32[]{:S(2)}, u32[]{:S(2)}) collective-permute-start(bf16[128,1536]{1,0:T(8,128)(2,1)S(1)} %collective-permute-done.11.refs_2_), channel_id=1, source_target_pairs={{0,1},{1,0},{2,3},{3,2},{4,5},{5,4},{6,7},{7,6},{8,9},{9,8},{10,11... | collective-permute-start | bytes 1179656 | tf_op jit(solution)/shard_map/ppermute | solution.py:515
  54.4 0.7 copy-start.7
  55.2 2.0 %collective-permute-start.12 = (bf16[128,1536]{1,0:T(8,128)(2,1)S(1)}, bf16[128,1536]{1,0:T(8,128)(2,1)S(1)}, u32[]{:S(2)}, u32[]{:S(2)}) collective-permute-start(bf16[128,1536]{1,0:T(8,128)(2,1)S(1)} %collective-permute-done.10.refs_0_), channel_id=1, source_target_pairs={{0,1},{1,0},{2,3},{3,2},{4,5},{5,4},{6,7},{7,6},{8,9},{9,8},{10,11... | collective-permute-start | bytes 1179656 | tf_op jit(solution)/shard_map/ppermute | solution.py:515
  65.8 2.1 %collective-permute-start.15 = (bf16[192,1536]{1,0:T(8,128)(2,1)S(1)}, bf16[192,1536]{1,0:T(8,128)(2,1)S(1)}, u32[]{:S(2)}, u32[]{:S(2)}) collective-permute-start(bf16[192,1536]{1,0:T(8,128)(2,1)S(1)} %get-tuple-element.54), channel_id=1, source_target_pairs={{0,1},{1,0},{2,3},{3,2},{4,5},{5,4},{6,7},{7,6},{8,9},{9,8},{10,11... | collective-permute-start | bytes 1769480 | tf_op jit(solution)/shard_map/ppermute | solution.py:515
  69.2 8.2 %collective-permute-start.18 = (f16[128,1536]{1,0:T(8,128)(2,1)}, f16[128,1536]{1,0:T(8,128)(2,1)}, u32[]{:S(2)}, u32[]{:S(2)}) collective-permute-start(f16[128,1536]{1,0:T(8,128)(2,1)} %convert_element_type.52), channel_id=1, source_target_pairs={{0,14},{1,3},{2,0},{3,5},{4,2},{5,7},{6,4},{7,9},{8,6},{9,11},{10,... | collective-permute-start | bytes 1179656 | tf_op jit(solution)/shard_map/ppermute | solution.py:580
  70.3 8.4 %collective-permute-start.17 = (bf16[128,1536]{1,0:T(8,128)(2,1)}, bf16[128,1536]{1,0:T(8,128)(2,1)S(1)}, u32[]{:S(2)}, u32[]{:S(2)}) collective-permute-start(bf16[128,1536]{1,0:T(8,128)(2,1)} %copy-done.7), channel_id=1, source_target_pairs={{0,1},{1,0},{2,3},{3,2},{4,5},{5,4},{6,7},{7,6},{8,9},{9,8},{10,11... | collective-permute-start | bytes 1179656 | tf_op jit(solution)/shard_map/ppermute | solution.py:515
  71.6 10.2 %collective-permute-start.16 = (bf16[192,1536]{1,0:T(8,128)(2,1)}, bf16[192,1536]{1,0:T(8,128)(2,1)S(1)}, u32[]{:S(2)}, u32[]{:S(2)}) collective-permute-start(bf16[192,1536]{1,0:T(8,128)(2,1)} %copy-done.6), channel_id=1, source_target_pairs={{0,1},{1,0},{2,3},{3,2},{4,5},{5,4},{6,7},{7,6},{8,9},{9,8},{10,11... | collective-permute-start | bytes 1769480 | tf_op jit(solution)/shard_map/ppermute | solution.py:515
  71.7 9.7 %collective-permute-start.22 = (f16[128,1536]{1,0:T(8,128)(2,1)S(1)}, f16[128,1536]{1,0:T(8,128)(2,1)S(1)}, u32[]{:S(2)}, u32[]{:S(2)}) collective-permute-start(f16[128,1536]{1,0:T(8,128)(2,1)S(1)} %convert_element_type.60), channel_id=1, source_target_pairs={{0,14},{1,3},{2,0},{3,5},{4,2},{5,7},{6,4},{7,9},{8,6},{9,11},{10,... | collective-permute-start | bytes 1179656 | tf_op jit(solution)/shard_map/ppermute | solution.py:580
  78.4 17.7 %copy-start.11 = (bf16[1440]{0:T(1024)(128)(2,1)S(1)}, bf16[1440]{0:T(1024)(128)(2,1)}, u32[]{:S(2)}) copy-start(bf16[1440]{0:T(1024)(128)(2,1)} %param.23) | copy-start | bytes 8644
  78.5 7.9 %collective-permute-start.19 = (f16[128,1536]{1,0:T(8,128)(2,1)S(1)}, f16[128,1536]{1,0:T(8,128)(2,1)S(1)}, u32[]{:S(2)}, u32[]{:S(2)}) collective-permute-start(f16[128,1536]{1,0:T(8,128)(2,1)S(1)} %add_convert_fusion.4), channel_id=1, source_target_pairs={{0,14},{1,3},{2,0},{3,5},{4,2},{5,7},{6,4},{7,9},{8,6},{9,11},{10,... | collective-permute-start | bytes 1179656 | tf_op jit(solution)/shard_map/ppermute | solution.py:580
  81.6 24.2 %copy-start.3 = (bf16[1440,256]{1,0:T(8,128)(2,1)S(1)}, bf16[1440,256]{1,0:T(8,128)(2,1)}, u32[]{:S(2)}) copy-start(bf16[1440,256]{1,0:T(8,128)(2,1)} %key_ref.1) | copy-start | bytes 2211844
  81.6 24.2 %copy-start.4 = (bf16[1440,256]{1,0:T(8,128)(2,1)S(1)}, bf16[1440,256]{1,0:T(8,128)(2,1)}, u32[]{:S(2)}) copy-start(bf16[1440,256]{1,0:T(8,128)(2,1)} %value_ref.1) | copy-start | bytes 2211844
  81.6 9.0 %collective-permute-start.23 = (f16[128,1536]{1,0:T(8,128)(2,1)S(1)}, f16[128,1536]{1,0:T(8,128)(2,1)S(1)}, u32[]{:S(2)}, u32[]{:S(2)}) collective-permute-start(f16[128,1536]{1,0:T(8,128)(2,1)S(1)} %add_convert_fusion.1), channel_id=1, source_target_pairs={{0,14},{1,3},{2,0},{3,5},{4,2},{5,7},{6,4},{7,9},{8,6},{9,11},{10,... | collective-permute-start | bytes 1179656 | tf_op jit(solution)/shard_map/ppermute | solution.py:580
  86.5 8.3 %collective-permute-start.20 = (f16[128,1536]{1,0:T(8,128)(2,1)S(1)}, f16[128,1536]{1,0:T(8,128)(2,1)S(1)}, u32[]{:S(2)}, u32[]{:S(2)}) collective-permute-start(f16[128,1536]{1,0:T(8,128)(2,1)S(1)} %add_convert_fusion.3), channel_id=1, source_target_pairs={{0,14},{1,3},{2,0},{3,5},{4,2},{5,7},{6,4},{7,9},{8,6},{9,11},{10,... | collective-permute-start | bytes 1179656 | tf_op jit(solution)/shard_map/ppermute | solution.py:580
  91.4 7.7 %collective-permute-start.24 = (f16[128,1536]{1,0:T(8,128)(2,1)}, f16[128,1536]{1,0:T(8,128)(2,1)S(1)}, u32[]{:S(2)}, u32[]{:S(2)}) collective-permute-start(f16[128,1536]{1,0:T(8,128)(2,1)} %add_convert_fusion), channel_id=1, source_target_pairs={{0,15},{1,2},{2,1},{3,4},{4,3},{5,6},{6,5},{7,8},{8,7},{9,10},{10,... | collective-permute-start | bytes 1179656 | tf_op jit(solution)/shard_map/ppermute | solution.py:580
  95.6 9.0 %collective-permute-start.21 = (f16[128,1536]{1,0:T(8,128)(2,1)}, f16[128,1536]{1,0:T(8,128)(2,1)}, u32[]{:S(2)}, u32[]{:S(2)}) collective-permute-start(f16[128,1536]{1,0:T(8,128)(2,1)} %add_convert_fusion.2), channel_id=1, source_target_pairs={{0,14},{1,3},{2,0},{3,5},{4,2},{5,7},{6,4},{7,9},{8,6},{9,11},{10,... | collective-permute-start | bytes 1179656 | tf_op jit(solution)/shard_map/ppermute | solution.py:580
  105.8 9.0 %copy-start.9 = (f32[32]{0:T(128)S(1)}, f32[32]{0:T(128)}, u32[]{:S(2)}) copy-start(f32[32]{0:T(128)} %sinks_ref.1) | copy-start | bytes 388
  107.2 7.6 %collective-permute-start.25 = (bf16[128,512]{1,0:T(8,128)(2,1)S(1)}, bf16[128,512]{1,0:T(8,128)(2,1)S(1)}, u32[]{:S(2)}, u32[]{:S(2)}) collective-permute-start(bf16[128,512]{1,0:T(8,128)(2,1)S(1)} %get-tuple-element.71.own_ref), channel_id=1, source_target_pairs={{0,1},{1,2},{2,3},{3,4},{4,5},{5,6},{6,7},{7,8},{8,9},{9,10},{10,1... | collective-permute-start | bytes 393224 | tf_op jit(solution)/shard_map/ppermute | solution.py:595
  109.3 2.7 %copy-start.1 = (bf16[1440,2048]{1,0:T(8,128)(2,1)S(1)}, bf16[1440,2048]{1,0:T(8,128)(2,1)}, u32[]{:S(2)}) copy-start(bf16[1440,2048]{1,0:T(8,128)(2,1)} %weight_ref.1) | copy-start | bytes 17694724
